TPU v7x, 512 devices: a whole 4x4x16 slice. The times are simulated.
512 devices in a mesh: front: 4 (over x), row: 16 (over z), col: 8 (over y, core).
Axes of the slice: x: 4, y: 4, z: 16, core: 2. Of those that a mesh axis runs over, the one named last changes fastest.
Arguments:
- front_entries: float32 [4, 2, 2, 16, 8, 16, 8, 4, 256], P('front', None, None, 'row', 'col'), may hold values from -5 to 5
- child_updates: float32 [8, 12, 2, 16, 8, 12, 256], P('front', None, None, 'row', 'col'), may hold values from -1.5 to 1.5
- diag_boost: float32 [4, 32, 256], P('front'), may hold values from 96 to 192
- tile_mask: int32 [4, 32, 32], P('front'), may hold values 0 or 1
- child_parent: int32 [8], replicated, may hold values from 0 to 3, as said below
- child_index: int32 [8, 12], replicated, may hold values from 0 to 31, as said below
Outputs:
- factored_front: float32 [4, 2, 16, 256, 4, 8, 256], P('front', None, 'row', None, None, 'col')
Inputs may be any that keep to these rules, and one draw needn't show every extreme that they name: `child_parent`: the 2 children stored in group g of the front axis, numbers g * 2 to g * 2 + 1, go to distinct parent fronts. `child_index`: each row lists 12 distinct parent tiles in increasing order.
All inputs are finite; a program needn't handle non-finite values. No bound on the sum of `tile_mask` on one device may be relied on, other than what follows from the above.
Results may differ from a plain program's by a relative error of at most 0.0001.
Values sent between devices are 32-bit elements; how exact they have to be, the bound alone decides.
No kernel may reach another device: no remote copies, remote signals or barrier semaphores. Data moves between devices by JAX's collectives and lax.ppermute only.
A program may use at most 64 MiB of HBM per device.

v0:
```python
import jax
import jax.numpy as jnp
from jax import lax
from jax.sharding import PartitionSpec as P

PANELS = 4


def from_root(value, axis, source):
    kept = jnp.where(lax.axis_index(axis) == source, value, 0).astype(value.dtype)
    return lax.psum(kept, axis)


def mirror_lower(block):
    return jnp.tril(block) + jnp.transpose(jnp.tril(block, -1))


def body(front_entries, child_updates, diag_boost, tile_mask, child_parent, child_index):
    grid_rows = lax.axis_size("row")
    grid_cols = lax.axis_size("col")
    my_group = lax.axis_index("front")
    my_row = lax.axis_index("row")
    my_col = lax.axis_index("col")
    local_rows = front_entries.shape[1]
    slices = front_entries.shape[2]
    local_cols = front_entries.shape[7]
    tile_size = front_entries.shape[8]
    held_count = child_updates.shape[0]
    child_tiles = child_updates.shape[1]
    highest = lax.Precision.HIGHEST
    entries = front_entries.reshape(local_rows, slices, grid_rows, grid_cols, local_cols, tile_size)
    mask_tiles = jnp.transpose(
        tile_mask[0].reshape(local_rows, grid_rows, local_cols, grid_cols), (0, 1, 3, 2)
    )
    masked = jnp.where(mask_tiles[:, None, :, :, :, None] == 1, entries, 0.0)
    pieces = child_updates.reshape(held_count, child_tiles, slices, child_tiles, tile_size)
    arrived = lax.all_gather(pieces, "front", axis=0, tiled=True)
    weight = (child_parent == my_group).astype(jnp.float32)
    row_tile_ids = jnp.arange(local_rows)[:, None] * grid_rows + jnp.arange(grid_rows)[None, :]
    col_tile_ids = jnp.arange(local_cols)[:, None] * grid_cols + jnp.arange(grid_cols)[None, :]
    row_hits = (child_index[:, None, None, :] == row_tile_ids[None, :, :, None]).astype(jnp.float32)
    row_hits = row_hits * weight[:, None, None, None]
    col_hits = (child_index[:, None, None, :] == col_tile_ids[None, :, :, None]).astype(jnp.float32)
    spread = jnp.einsum("naube,ntpb->nautpe", arrived, col_hits, precision=highest)
    contribution = jnp.einsum("niqa,nautpe->iuqpte", row_hits, spread, precision=highest)
    assembled = masked + contribution
    joined = assembled.reshape(local_rows, slices, grid_rows * grid_cols, local_cols, tile_size)
    relaid = lax.all_to_all(joined, ("row", "col"), split_axis=2, concat_axis=2, tiled=True)
    front_tiles = relaid.reshape(local_rows, tile_size, local_cols, tile_size)
    global_rows = jnp.arange(local_rows) * grid_rows + my_row
    global_cols = jnp.arange(local_cols) * grid_cols + my_col
    boosts = jnp.take(diag_boost[0], global_rows, axis=0)
    on_diagonal = global_rows[:, None] == global_cols[None, :]
    eye_mask = jnp.eye(tile_size, dtype=bool)
    placed = on_diagonal[:, None, :, None] & eye_mask[None, :, None, :]
    front_tiles = front_tiles + jnp.where(placed, boosts[:, :, None, None], 0.0)
    identity = jnp.eye(tile_size, dtype=jnp.float32)
    tile_ids = global_rows[:, None, None]
    for panel_step in range(PANELS):
        row_root = panel_step % grid_rows
        col_root = panel_step % grid_cols
        home_row = panel_step // grid_rows
        home_col = panel_step // grid_cols
        candidate = jnp.where(my_col == col_root, front_tiles[home_row, :, home_col, :], identity)
        pivot_block = from_root(candidate, "row", row_root)
        pivot_factor = jnp.linalg.cholesky(mirror_lower(pivot_block))
        current = front_tiles[:, :, home_col, :]
        solved = lax.linalg.triangular_solve(
            pivot_factor,
            current.reshape(local_rows * tile_size, tile_size),
            left_side=False,
            lower=True,
            transpose_a=True,
        )
        solved = solved.reshape(local_rows, tile_size, tile_size)
        column = jnp.where(
            tile_ids > panel_step,
            solved,
            jnp.where(tile_ids == panel_step, pivot_factor[None], 0.0),
        )
        front_tiles = front_tiles.at[:, :, home_col, :].set(
            jnp.where(my_col == col_root, column, current)
        )
        received = from_root(column, "col", col_root)
        update = jnp.where(tile_ids > panel_step, received, 0.0)
        pieces_list = []
        for offset in range(grid_rows // grid_cols):
            pieces_list.append(from_root(update, "row", my_col + grid_cols * offset))
        across = jnp.stack(pieces_list, axis=1).reshape(local_cols, tile_size, tile_size)
        front_tiles = front_tiles - jnp.einsum("isk,tek->iste", update, across, precision=highest)
    return front_tiles.reshape(1, local_rows, 1, tile_size, local_cols, 1, tile_size)


def solution(mesh):
    placed = (
        P("front", None, None, "row", "col", None, None, None, None),
        P("front", None, None, "row", "col", None, None),
        P("front", None, None),
        P("front", None, None),
        P(),
        P(),
    )
    return jax.shard_map(
        body,
        mesh=mesh,
        in_specs=placed,
        out_specs=P("front", None, "row", None, None, "col", None),
        check_vma=False,
    )
```

profile of v0, /device:TPU:1, one launch (start us, length us, event | category | flops | bytes accessed | tf_op | source)
XLA Modules:
  0.0 1862.9 jit_solution(13154090566239110110)
XLA Ops:
  6.5 2.2 copy.66
  10.5 44.9 %all-gather.3.cloned.1.call-done = f32[8,12,2,1,1,12,256]{6,2,5,4,3,1,0:T(2,128)} async-done(((f32[2,12,2,1,1,12,256]{6,2,5,4,3,1,0:T(2,128)}), f32[8,12,2,1,1,12,256]{6,2,5,4,3,1,0:T(2,128)}) %all-gather.3.cloned.1.call-update) | async-done | bytes 2359312 | tf_op jit(solution)/shard_map/all_gather | solution.py:37
  55.5 4.5 fusion.4
  60.0 12.8 bitcast_add_fusion
  72.8 1.6 copy.139
  74.5 2.7 copy.71
  77.1 16.6 all-to-all-start
  94.7 96.0 %all-to-all-done = f32[2,2,128,4,256]{4,3,1,0,2:T(4,128)S(1)} async-done(((f32[2,2,128,4,256]{4,3,1,0,2:T(4,128)}), f32[2,2,128,4,256]{4,3,1,0,2:T(4,128)S(1)}, u32[]{:S(2)}, u32[]{:S(2)}) %all-to-all-start) | async-done | bytes 2097184 | tf_op jit(solution)/shard_map/all_to_all | solution.py:48
  193.5 119.5 %all-reduce.18.cloned.1.call-done = f32[256,256]{1,0:T(8,128)} async-done(((f32[256,256]{1,0:T(8,128)}), f32[256,256]{1,0:T(8,128)}) %all-reduce.18.cloned.1.call-update) | async-done | bytes 262160 | tf_op jit(solution)/shard_map/psum | solution.py:11
  315.3 11.7 cholesky.214
  327.1 9.8 custom-call.17
  337.4 11.7 cholesky.231
  351.1 4.0 while.12
  351.9 1.3 bitcast_dynamic-update-slice_fusion.8
  353.8 1.3 bitcast_dynamic-update-slice_fusion.8
  355.2 19.7 %custom-call.18 = f32[2,128,128]{1,2,0:T(8,128)S(1)} custom-call(f32[2,128,128]{2,1,0:T(8,128)S(1)} %get-tuple-element.81), custom_call_target="InvertDiagBlocksLowerTriangular" | custom-call | tf_op jit(solution)/shard_map/triangular_solve/custom-call.0 | solution.py:68
  376.5 1.3 fusion.63
  379.0 80.9 %all-reduce.20.cloned.1.call-done = f32[2,256,256]{2,1,0:T(8,128)} async-done(((f32[2,256,256]{2,1,0:T(8,128)}), f32[2,256,256]{2,1,0:T(8,128)}) %all-reduce.20.cloned.1.call-update) | async-done | bytes 524304 | tf_op jit(solution)/shard_map/psum | solution.py:11
  459.9 2.2 select_bitcast_fusion.7
  462.4 130.4 %all-reduce.40.cloned.1.call-done = (f32[2,1,256,256]{3,2,0,1:T(8,128)}, f32[2,1,256,256]{3,2,0,1:T(8,128)}) async-done(((f32[2,1,256,256]{3,2,0,1:T(8,128)}, f32[2,1,256,256]{3,2,0,1:T(8,128)}), (f32[2,1,256,256]{3,2,0,1:T(8,128)}, f32[2,1,256,256]{3,2,0,1:T(8,128)})) %all-reduce.40.cloned.1.call-update) | async-done | bytes 1048592 | tf_op jit(solution)/shard_map/psum | solution.py:11
  592.8 1.3 pad_maximum_fusion
  594.2 3.5 convolution_subtract_fusion.2
  598.8 132.2 %all-reduce.22.cloned.1.call-done = f32[256,256]{1,0:T(8,128)} async-done(((f32[256,256]{1,0:T(8,128)}), f32[256,256]{1,0:T(8,128)}) %all-reduce.22.cloned.1.call-update) | async-done | bytes 262160 | tf_op jit(solution)/shard_map/psum | solution.py:11
  733.3 11.7 cholesky.248
  745.1 9.8 custom-call.19
  755.4 11.7 cholesky.265
  769.7 4.1 while.13
  770.6 1.3 bitcast_dynamic-update-slice_fusion.9
  772.5 1.3 bitcast_dynamic-update-slice_fusion.9
  773.8 19.7 %custom-call.20 = f32[2,128,128]{1,2,0:T(8,128)S(1)} custom-call(f32[2,128,128]{2,1,0:T(8,128)S(1)} %get-tuple-element.82), custom_call_target="InvertDiagBlocksLowerTriangular" | custom-call | tf_op jit(solution)/shard_map/triangular_solve/custom-call.0 | solution.py:68
  795.2 1.3 fusion.59
  797.7 81.0 %all-reduce.24.cloned.1.call-done = f32[2,256,256]{2,1,0:T(8,128)} async-done(((f32[2,256,256]{2,1,0:T(8,128)}), f32[2,256,256]{2,1,0:T(8,128)}) %all-reduce.24.cloned.1.call-update) | async-done | bytes 524304 | tf_op jit(solution)/shard_map/psum | solution.py:11
  878.6 2.2 select_bitcast_fusion.5
  881.1 130.6 %all-reduce.38.cloned.1.call-done = (f32[2,1,256,256]{3,2,0,1:T(8,128)}, f32[2,1,256,256]{3,2,0,1:T(8,128)}) async-done(((f32[2,1,256,256]{3,2,0,1:T(8,128)}, f32[2,1,256,256]{3,2,0,1:T(8,128)}), (f32[2,1,256,256]{3,2,0,1:T(8,128)}, f32[2,1,256,256]{3,2,0,1:T(8,128)})) %all-reduce.38.cloned.1.call-update) | async-done | bytes 1048592 | tf_op jit(solution)/shard_map/psum | solution.py:11
  1011.7 1.3 pad_maximum_fusion.1
  1013.1 3.5 convolution_subtract_fusion.1
  1017.9 131.9 %all-reduce.26.cloned.1.call-done = f32[256,256]{1,0:T(8,128)} async-done(((f32[256,256]{1,0:T(8,128)}), f32[256,256]{1,0:T(8,128)}) %all-reduce.26.cloned.1.call-update) | async-done | bytes 262160 | tf_op jit(solution)/shard_map/psum | solution.py:11
  1152.2 11.7 cholesky.282
  1164.0 9.8 custom-call.21
  1174.3 11.7 cholesky.299
  1188.6 4.0 while.14
  1189.4 1.3 bitcast_dynamic-update-slice_fusion.10
  1191.3 1.3 bitcast_dynamic-update-slice_fusion.10
  1192.6 19.7 %custom-call.22 = f32[2,128,128]{1,2,0:T(8,128)S(1)} custom-call(f32[2,128,128]{2,1,0:T(8,128)S(1)} %get-tuple-element.83), custom_call_target="InvertDiagBlocksLowerTriangular" | custom-call | tf_op jit(solution)/shard_map/triangular_solve/custom-call.0 | solution.py:68
  1214.0 1.3 fusion.55
  1216.5 80.9 %all-reduce.28.cloned.1.call-done = f32[2,256,256]{2,1,0:T(8,128)} async-done(((f32[2,256,256]{2,1,0:T(8,128)}), f32[2,256,256]{2,1,0:T(8,128)}) %all-reduce.28.cloned.1.call-update) | async-done | bytes 524304 | tf_op jit(solution)/shard_map/psum | solution.py:11
  1297.4 2.2 select_bitcast_fusion.3
  1299.9 130.4 %all-reduce.36.cloned.1.call-done = (f32[2,1,256,256]{3,2,0,1:T(8,128)}, f32[2,1,256,256]{3,2,0,1:T(8,128)}) async-done(((f32[2,1,256,256]{3,2,0,1:T(8,128)}, f32[2,1,256,256]{3,2,0,1:T(8,128)}), (f32[2,1,256,256]{3,2,0,1:T(8,128)}, f32[2,1,256,256]{3,2,0,1:T(8,128)})) %all-reduce.36.cloned.1.call-update) | async-done | bytes 1048592 | tf_op jit(solution)/shard_map/psum | solution.py:11
  1430.3 1.3 pad_maximum_fusion.2
  1431.7 3.5 convolution_subtract_fusion
  1436.3 132.2 %all-reduce.30.cloned.1.call-done = f32[256,256]{1,0:T(8,128)} async-done(((f32[256,256]{1,0:T(8,128)}), f32[256,256]{1,0:T(8,128)}) %all-reduce.30.cloned.1.call-update) | async-done | bytes 262160 | tf_op jit(solution)/shard_map/psum | solution.py:11
  1570.9 11.7 cholesky.316
  1582.6 9.8 custom-call.23
  1592.9 11.7 cholesky.333
  1607.2 4.0 while.15
  1608.1 1.3 bitcast_dynamic-update-slice_fusion.11
  1610.0 1.3 bitcast_dynamic-update-slice_fusion.11
  1611.3 19.7 %custom-call.24 = f32[2,128,128]{1,2,0:T(8,128)S(1)} custom-call(f32[2,128,128]{2,1,0:T(8,128)S(1)} %get-tuple-element.84), custom_call_target="InvertDiagBlocksLowerTriangular" | custom-call | tf_op jit(solution)/shard_map/triangular_solve/custom-call.0 | solution.py:68
  1635.2 81.0 %all-reduce.32.cloned.1.call-done = f32[2,256,256]{2,1,0:T(8,128)} async-done(((f32[2,256,256]{2,1,0:T(8,128)}), f32[2,256,256]{2,1,0:T(8,128)}) %all-reduce.32.cloned.1.call-update) | async-done | bytes 524304 | tf_op jit(solution)/shard_map/psum | solution.py:11
  1716.1 2.2 select_bitcast_fusion.1
  1718.5 130.6 %all-reduce.34.cloned.1.call-done = (f32[2,1,256,256]{3,2,0,1:T(8,128)}, f32[2,1,256,256]{3,2,0,1:T(8,128)}) async-done(((f32[2,1,256,256]{3,2,0,1:T(8,128)}, f32[2,1,256,256]{3,2,0,1:T(8,128)}), (f32[2,1,256,256]{3,2,0,1:T(8,128)}, f32[2,1,256,256]{3,2,0,1:T(8,128)})) %all-reduce.34.cloned.1.call-update) | async-done | bytes 1048592 | tf_op jit(solution)/shard_map/psum | solution.py:11
  1849.2 1.3 pad_maximum_fusion.3
  1850.6 1.9 subtract_bitcast_fusion
  1852.5 3.5 copy.97
  (193 shorter events, 43.8 us)
Async XLA Ops:
  6.5 87.4 %copy-start = (f32[1,32,256]{2,1,0:T(8,128)S(1)}, f32[1,32,256]{2,1,0:T(8,128)}, u32[]{:S(2)}) copy-start(f32[1,32,256]{2,1,0:T(8,128)} %param.19) | copy-start | bytes 98308
  6.5 48.9 %all-gather.3.cloned.1.call-start = ((), (), s32[]{:S(2)}) async-start(), calls=%async_computation.9 | async-start | bytes 2949120 | tf_op jit(solution)/shard_map/all_gather | solution.py:37
  55.5 4.5 copy-start.5
  55.5 4.5 copy-start.14
  77.1 113.5 %all-to-all-start = ((f32[2,2,128,4,256]{4,3,1,0,2:T(4,128)}), f32[2,2,128,4,256]{4,3,1,0,2:T(4,128)S(1)}, u32[]{:S(2)}, u32[]{:S(2)}) async-start(f32[2,2,128,4,256]{4,3,1,0,2:T(4,128)} %copy.71), calls=%async_computation | async-start | bytes 4194304 | tf_op jit(solution)/shard_map/all_to_all | solution.py:48
  93.8 219.2 %all-reduce.18.cloned.1.call-start = ((), (), s32[]{:S(2)}) async-start(), calls=%async_computation.1 | async-start | bytes 524288 | tf_op jit(solution)/shard_map/psum | solution.py:11
  193.0 266.9 %all-reduce.20.cloned.1.call-start = ((), (), s32[]{:S(2)}) async-start(), calls=%async_computation.2 | async-start | bytes 1048576 | tf_op jit(solution)/shard_map/psum | solution.py:11
  374.8 0.7 copy-start.10
  379.0 213.8 %all-reduce.40.cloned.1.call-start = ((), (), s32[]{:S(2)}) async-start(), calls=%async_computation.13 | async-start | bytes 2097152 | tf_op jit(solution)/shard_map/psum | solution.py:11
  462.1 268.9 %all-reduce.22.cloned.1.call-start = ((), (), s32[]{:S(2)}) async-start(), calls=%async_computation.3 | async-start | bytes 524288 | tf_op jit(solution)/shard_map/psum | solution.py:11
  462.4 131.8 %copy-start.4 = (f32[2,256,4,256]{3,1,2,0:T(8,128)}, f32[2,256,4,256]{3,1,2,0:T(8,128)S(1)}, u32[]{:S(2)}) copy-start(f32[2,256,4,256]{3,1,2,0:T(8,128)S(1)} %select_dynamic-update-slice_fusion.3) | copy-start | bytes 6291460
  592.8 1.4 copy-start.6
  598.5 280.2 %all-reduce.24.cloned.1.call-start = ((), (), s32[]{:S(2)}) async-start(), calls=%async_computation.4 | async-start | bytes 1048576 | tf_op jit(solution)/shard_map/psum | solution.py:11
  793.5 0.7 copy-start.11
  797.6 214.0 %all-reduce.38.cloned.1.call-start = ((), (), s32[]{:S(2)}) async-start(), calls=%async_computation.12 | async-start | bytes 2097152 | tf_op jit(solution)/shard_map/psum | solution.py:11
  880.9 269.0 %all-reduce.26.cloned.1.call-start = ((), (), s32[]{:S(2)}) async-start(), calls=%async_computation.5 | async-start | bytes 524288 | tf_op jit(solution)/shard_map/psum | solution.py:11
  881.1 132.0 %copy-start.3 = (f32[2,256,4,256]{3,1,2,0:T(8,128)}, f32[2,256,4,256]{3,1,2,0:T(8,128)S(1)}, u32[]{:S(2)}) copy-start(f32[2,256,4,256]{3,1,2,0:T(8,128)S(1)} %select_dynamic-update-slice_fusion.2) | copy-start | bytes 6291460
  1011.7 1.4 copy-start.8
  1017.4 280.1 %all-reduce.28.cloned.1.call-start = ((), (), s32[]{:S(2)}) async-start(), calls=%async_computation.6 | async-start | bytes 1048576 | tf_op jit(solution)/shard_map/psum | solution.py:11
  1212.3 0.7 copy-start.12
  1216.4 213.8 %all-reduce.36.cloned.1.call-start = ((), (), s32[]{:S(2)}) async-start(), calls=%async_computation.11 | async-start | bytes 2097152 | tf_op jit(solution)/shard_map/psum | solution.py:11
  1299.6 268.9 %all-reduce.30.cloned.1.call-start = ((), (), s32[]{:S(2)}) async-start(), calls=%async_computation.7 | async-start | bytes 524288 | tf_op jit(solution)/shard_map/psum | solution.py:11
  1299.9 131.8 %copy-start.2 = (f32[2,256,4,256]{3,1,2,0:T(8,128)}, f32[2,256,4,256]{3,1,2,0:T(8,128)S(1)}, u32[]{:S(2)}) copy-start(f32[2,256,4,256]{3,1,2,0:T(8,128)S(1)} %select_dynamic-update-slice_fusion.1) | copy-start | bytes 6291460
  1430.3 1.4 copy-start.7
  1436.0 280.1 %all-reduce.32.cloned.1.call-start = ((), (), s32[]{:S(2)}) async-start(), calls=%async_computation.8 | async-start | bytes 1048576 | tf_op jit(solution)/shard_map/psum | solution.py:11
  1631.0 0.7 copy-start.13
  1635.1 214.0 %all-reduce.34.cloned.1.call-start = ((), (), s32[]{:S(2)}) async-start(), calls=%async_computation.10 | async-start | bytes 2097152 | tf_op jit(solution)/shard_map/psum | solution.py:11
  1849.2 1.4 copy-start.9
  1850.6 5.4 copy-start.1
Sparse Core Ops, SparseCore 0:
  9.5 45.9 all-gather.2
  193.1 119.8 all-reduce.17
  379.1 80.7 all-reduce.19
  462.3 130.4 all-reduce.39
  598.6 132.3 all-reduce.21
  797.8 80.8 all-reduce.23
  881.1 130.4 all-reduce.37
  1017.5 132.3 all-reduce.25
  1216.6 80.8 all-reduce.27
  1299.8 130.4 all-reduce.35
  1436.1 132.3 all-reduce.29
  1635.2 80.8 all-reduce.31
  1718.6 130.4 all-reduce.33
where the time goes:
time: 1880 us; the launch traced here: 1860 us
  waiting for transfers between devices  1500 us (80%)
  other arithmetic  246 us (13%)
  matrix products  40.6 us (2%)
  local copies, waits for them, and re-layouts  35.2 us (2%)
  between operations  19.6 us (1%)
    psum x12, waiting for transfers between devices, from_root(): return lax.psum(kept, axis)  1360 us
    another operation x27, other arithmetic, body(): pivot_factor = jnp.linalg.cholesky(mirror_lower(pivot_block))  138 us
    all_to_all x1, waiting for transfers between devices, body(): lax.all_to_all(joined, ('row', 'col'), split_axis=2, concat_axis=2, tiled...  96 us
    another operation x13, other arithmetic, body(): lax.linalg.triangular_solve(pivot_factor, current.reshape(local_rows * ti...  79 us
    all_gather x1, waiting for transfers between devices, body(): arrived = lax.all_gather(pieces, 'front', axis=0, tiled=True)  44.9 us
  transfers between devices with their start and end apart: 14, of which 14 were waited for; matrix products, arithmetic and copies ran while one was open for 0% of the time, Pallas kernels for 0%

commit v1 on v0

v1 whole, which is shorter than its diff:
```python
import jax
import jax.numpy as jnp
from jax import lax
from jax.experimental import pallas as pl
from jax.experimental.pallas import tpu as pltpu
from jax.sharding import PartitionSpec as P

PANELS = 4
BLOCK = 128
HIGHEST = lax.Precision.HIGHEST
ROWS_BY_ROWS = (((1,), (1,)), ((), ()))
ROWS_BY_COLUMNS = (((1,), (0,)), ((), ()))


def times(left, right, numbers):
    return lax.dot_general(left, right, numbers, precision=HIGHEST, preferred_element_type=jnp.float32)


def over_lanes(value, lane):
    return jnp.broadcast_to(value[:, lane : lane + 1], value.shape)


def over_sublanes(value, sublane):
    return jnp.broadcast_to(value[sublane : sublane + 1, :], value.shape)


def factor_block(block):
    groups = BLOCK // 8
    row = lax.broadcasted_iota(jnp.int32, (8, BLOCK), 0)
    lane = lax.broadcasted_iota(jnp.int32, (8, BLOCK), 1)
    rest = [block[8 * g : 8 * g + 8, :] for g in range(groups)]
    extra = [jnp.where(lane == row + 8 * g, 1.0, 0.0).astype(jnp.float32) for g in range(groups)]
    upper, inverse = [], []
    for g in range(groups):
        base = 8 * g
        raw = [[over_lanes(rest[h], base + k) for k in range(8)] for h in range(g, groups)]
        small = [[over_sublanes(raw[0][k], i) if i >= k else None for k in range(8)] for i in range(8)]
        scale = []
        for k in range(8):
            inv = lax.rsqrt(small[k][k])
            inv = inv * (1.5 - 0.5 * small[k][k] * inv * inv)
            scale.append(inv)
            for i in range(k + 1, 8):
                small[i][k] = small[i][k] * inv
            for j in range(k + 1, 8):
                for i in range(j, 8):
                    small[i][j] = small[i][j] - small[i][k] * small[j][k]

        def forward(parts, small=small, scale=scale):
            done = []
            for k in range(8):
                part = parts[k]
                for m in range(k):
                    part = part - small[k][m] * done[m]
                done.append(part * scale[k])
            return done

        wide = forward([over_sublanes(rest[g], k) for k in range(8)])
        solved = forward([over_sublanes(extra[g], k) for k in range(8)])
        upper_rows, inverse_rows = wide[0], solved[0]
        for k in range(1, 8):
            upper_rows = jnp.where(row == k, wide[k], upper_rows)
            inverse_rows = jnp.where(row == k, solved[k], inverse_rows)
        upper.append(jnp.where(lane >= row + base, upper_rows, 0.0))
        inverse.append(inverse_rows)
        for h in range(g + 1, groups):
            tall = forward(raw[h - g])
            for k in range(8):
                rest[h] = rest[h] - tall[k] * wide[k]
                extra[h] = extra[h] - tall[k] * solved[k]
    return jnp.concatenate(upper, 0), jnp.concatenate(inverse, 0)


def factor_kernel(top_ref, held_ref, diagonal_ref):
    blocks = held_ref.shape[0] // BLOCK
    held_ref[...] = top_ref[...]
    row = lax.broadcasted_iota(jnp.int32, (BLOCK, BLOCK), 0)
    col = lax.broadcasted_iota(jnp.int32, (BLOCK, BLOCK), 1)

    @pl.loop(0, blocks)
    def _(k):
        here = pl.ds(pl.multiple_of(k * BLOCK, BLOCK), BLOCK)
        block = held_ref[here, here]
        block = jnp.where(row >= col, block, 0.0) + jnp.where(col > row, jnp.where(row > col, block, 0.0).T, 0.0)
        upper, inverse = factor_block(block)
        diagonal_ref[here, :] = upper.T

        @pl.loop(k + 1, blocks)
        def _(j):
            held_ref[here, pl.ds(pl.multiple_of(j * BLOCK, BLOCK), BLOCK)] = jnp.zeros((BLOCK, BLOCK), jnp.float32)

        held_ref[here, here] = jnp.where(row == col, 1.0, 0.0).astype(jnp.float32)
        held_ref[:, here] = times(held_ref[:, here], inverse, ROWS_BY_ROWS)

        @pl.loop(k + 1, blocks)
        def _(j):
            there = pl.ds(pl.multiple_of(j * BLOCK, BLOCK), BLOCK)
            held_ref[:, there] = held_ref[:, there] - times(held_ref[:, here], held_ref[there, here], ROWS_BY_ROWS)


def factor(top):
    order = top.shape[0]
    whole = pl.BlockSpec(memory_space=pltpu.VMEM)
    return pl.pallas_call(
        factor_kernel,
        out_shape=(
            jax.ShapeDtypeStruct((order, order), jnp.float32),
            jax.ShapeDtypeStruct((order, BLOCK), jnp.float32),
        ),
        in_specs=[whole],
        out_specs=(whole, whole),
        compiler_params=pltpu.CompilerParams(vmem_limit_bytes=40 * 2**20),
        cost_estimate=pl.CostEstimate(flops=50 * 10**9, bytes_accessed=16 * 2**20, transcendentals=1024),
        name="factor",
    )(top)


def body(front_entries, child_updates, diag_boost, tile_mask, child_parent, child_index):
    grid_rows = lax.axis_size("row")
    grid_cols = lax.axis_size("col")
    groups = lax.axis_size("front")
    my_group = lax.axis_index("front")
    my_row = lax.axis_index("row")
    my_col = lax.axis_index("col")
    local_rows = front_entries.shape[1]
    slices = front_entries.shape[2]
    local_cols = front_entries.shape[7]
    size = front_entries.shape[8]
    held = child_updates.shape[0]
    child_tiles = child_updates.shape[1]
    halves = grid_rows // grid_cols
    order = PANELS * size

    pieces = child_updates.reshape(held, child_tiles, slices, child_tiles, size)
    parents = child_parent.reshape(groups, held)
    mine = lax.dynamic_index_in_dim(parents, my_group, 0, keepdims=False)
    goes = (mine[None, :] == jnp.arange(groups)[:, None])[:, :, None, None, None, None]
    slots = jnp.sum(jnp.where(goes, pieces[None], 0.0), axis=1)
    arrived = lax.all_to_all(slots, "front", split_axis=0, concat_axis=0, tiled=True)
    comes = parents == my_group
    index = jnp.sum(jnp.where(comes[:, :, None], child_index.reshape(groups, held, child_tiles), 0), axis=1)
    weight = jnp.any(comes, axis=1).astype(jnp.float32)

    entries = front_entries.reshape(local_rows, slices, grid_rows, grid_cols, local_cols, size)
    mask_tiles = jnp.transpose(tile_mask[0].reshape(local_rows, grid_rows, local_cols, grid_cols), (0, 1, 3, 2))
    masked = jnp.where(mask_tiles[:, None, :, :, :, None] == 1, entries, 0.0)
    row_ids = jnp.arange(local_rows)[:, None] * grid_rows + jnp.arange(grid_rows)[None, :]
    col_ids = jnp.arange(local_cols)[:, None] * grid_cols + jnp.arange(grid_cols)[None, :]
    row_hits = (index[:, None, None, :] == row_ids[None, :, :, None]).astype(jnp.float32) * weight[:, None, None, None]
    col_hits = (index[:, None, None, :] == col_ids[None, :, :, None]).astype(jnp.float32)
    spread = jnp.einsum("naube,ntpb->nautpe", arrived, col_hits, precision=HIGHEST)
    assembled = masked + jnp.einsum("niqa,nautpe->iuqpte", row_hits, spread, precision=HIGHEST)

    panel = assembled[:, :, :, :PANELS, 0, :]
    within = jnp.arange(slices) * grid_rows * grid_cols + my_row * grid_cols + my_col
    boost = jnp.where(
        within[:, None, None, None] == jnp.arange(size),
        jnp.where(jnp.eye(PANELS, dtype=bool)[:, :, None], diag_boost[0, :PANELS, None, :], 0.0),
        0.0,
    )
    panel = panel.at[0, :, :PANELS].add(boost)

    top = jnp.transpose(panel[0, :, :PANELS], (1, 0, 2, 3)).reshape(PANELS * slices, order)
    gathered = lax.all_gather(top, ("row", "col"), axis=0)
    top_block = jnp.transpose(gathered, (1, 0, 2)).reshape(order, order)

    assembled, panel, top_block = lax.optimization_barrier((assembled, panel, top_block))
    joined = assembled.reshape(local_rows, slices, grid_rows * grid_cols, local_cols, size)
    relaid = lax.all_to_all(joined, ("row", "col"), split_axis=2, concat_axis=2, tiled=True)
    tiles = relaid.reshape(local_rows, size, local_cols, size)

    for_rows = lax.all_to_all(panel, "row", split_axis=2, concat_axis=2, tiled=True)
    for_rows = lax.all_gather(for_rows, "col", axis=3)
    row_panel = for_rows.reshape(local_rows * size, order)
    split = panel.reshape(local_rows, slices, halves, grid_cols, PANELS, size)
    for_cols = lax.all_to_all(split, "col", split_axis=3, concat_axis=3, tiled=True)
    for_cols = jnp.transpose(for_cols, (0, 2, 1, 3, 4, 5))
    for_cols = lax.all_gather(for_cols, "row", axis=3)
    col_panel = for_cols.reshape(local_cols, size, order)

    both, diagonal = factor(top_block)
    block_row = jnp.arange(order)[:, None] // BLOCK
    block_col = jnp.arange(order)[None, :] // BLOCK
    lower = jnp.where(block_row > block_col, both, 0.0)
    lower = jnp.where(block_row == block_col, jnp.tile(diagonal, (1, order // BLOCK)), lower)
    inverse = jnp.where(block_row > block_col, 0.0, both)

    solved = times(row_panel, inverse, ROWS_BY_COLUMNS).reshape(local_rows, size, order)
    own = lax.dynamic_slice_in_dim(lower, jnp.minimum(my_row, PANELS - 1) * size, size, 0)
    solved = solved.at[0].set(jnp.where(my_row < PANELS, own, solved[0]))
    tile_ids = jnp.arange(local_rows) * grid_rows + my_row
    panel_ids = jnp.arange(order) // size
    update = jnp.where(tile_ids[:, None, None] > panel_ids[None, None, :], solved, 0.0)
    both_sides = times(update.reshape(local_rows * size, order), inverse, ROWS_BY_ROWS)

    change = lax.dot_general(
        both_sides, col_panel, (((1,), (2,)), ((), ())), precision=HIGHEST, preferred_element_type=jnp.float32
    )
    tiles = tiles - change.reshape(local_rows, size, local_cols, size)
    global_rows = jnp.arange(local_rows) * grid_rows + my_row
    global_cols = jnp.arange(local_cols) * grid_cols + my_col
    boosts = jnp.take(diag_boost[0], global_rows, axis=0)
    on_diagonal = global_rows[:, None] == global_cols[None, :]
    placed = on_diagonal[:, None, :, None] & jnp.eye(size, dtype=bool)[None, :, None, :]
    tiles = tiles + jnp.where(placed, boosts[:, :, None, None], 0.0)
    column = lax.dynamic_slice_in_dim(solved, jnp.minimum(my_col, PANELS - 1) * size, size, 2)
    tiles = tiles.at[:, :, 0, :].set(jnp.where(my_col < PANELS, column, tiles[:, :, 0, :]))
    return tiles.reshape(1, local_rows, 1, size, local_cols, 1, size)


def solution(mesh):
    placed = (
        P("front", None, None, "row", "col", None, None, None, None),
        P("front", None, None, "row", "col", None, None),
        P("front", None, None),
        P("front", None, None),
        P(),
        P(),
    )
    return jax.shard_map(
        body,
        mesh=mesh,
        in_specs=placed,
        out_specs=P("front", None, "row", None, None, "col", None),
        check_vma=False,
    )
```

time: 1880 us -> 429 us (0.23)
  the two profiles are of different devices: /device:TPU:1 before, /device:TPU:2 now
where the time goes in v1:
time: 429 us; the launch traced here: 421 us
  waiting for transfers between devices  207 us (48%)
  Pallas kernels  61.3 us (14%)
  local copies, waits for them, and re-layouts  50.4 us (12%)
  matrix products  35.7 us (8%)
  blocking collectives  25.7 us (6%)
  starting transfers between devices  23.1 us (5%)
  between operations  13.7 us (3%)
    all_gather x1, waiting for transfers between devices, body(): gathered = lax.all_gather(top, ('row', 'col'), axis=0)  145 us
    pallas_call x1, Pallas kernels, factor(): pl.pallas_call(factor_kernel, out_shape=(jax.ShapeDtypeStruct((order, ord...  61.3 us
    all_gather x1, waiting for transfers between devices, body(): for_cols = lax.all_gather(for_cols, 'row', axis=3)  48.4 us
    all_to_all x1, blocking collectives, body(): lax.all_to_all(panel, 'row', split_axis=2, concat_axis=2, tiled=True)  25.7 us
    dot_general x2, matrix products, times(): lax.dot_general(left, right, numbers, precision=HIGHEST, preferred_elemen...  18.3 us
    unnamed x20, local copies, waits for them, and re-layouts  10.7 us
    all_to_all x1, waiting for transfers between devices, body(): lax.all_to_all(slots, 'front', split_axis=0, concat_axis=0, tiled=True)  9.64 us
    all_to_all x1, starting transfers between devices, body(): lax.all_to_all(slots, 'front', split_axis=0, concat_axis=0, tiled=True)  9.4 us
  transfers between devices with their start and end apart: 6, of which 4 were waited for; matrix products, arithmetic and copies ran while one was open for 11% of the time, Pallas kernels for 15%

profile of v1, /device:TPU:2, one launch (start us, length us, event | category | flops | bytes accessed | tf_op | source)
XLA Modules:
  0.0 420.7 jit_solution(12503628522719618389)
XLA Ops:
  6.5 0.7 reshape.502
  7.3 0.1 iota_compare_fusion.3
  7.4 1.4 copy.106
  8.7 0.1 copy.66
  8.8 1.0 select_reduce_fusion
  9.9 0.0 copy-start.5
  9.9 0.0 copy-start.7
  9.9 1.9 copy.67
  11.8 9.4 %all-to-all-start = ((f32[4,12,2,12,256]{4,2,3,1,0:T(2,128)}), f32[4,12,2,12,256]{4,2,3,1,0:T(2,128)S(1)}, u32[]{:S(2)}, u32[]{:S(2)}) async-start(f32[4,12,2,12,256]{4,2,3,1,0:T(2,128)} %copy.67), calls=%async_computation | async-start | bytes 2359296 | tf_op jit(solution)/shard_map/all_to_all | solution.py:139
  21.2 0.1 fusion.53
  21.4 0.1 eq.128
  21.5 0.1 copy.63
  21.6 0.1 iota_add_fusion.1
  21.7 0.1 select_reduce_fusion.1
  21.8 0.1 iota_compare_fusion.2
  21.9 0.1 iota_add_fusion
  22.0 0.1 broadcast_select_fusion
  22.1 9.6 %all-to-all-done = f32[4,12,2,12,256]{4,2,3,1,0:T(2,128)S(1)} async-done(((f32[4,12,2,12,256]{4,2,3,1,0:T(2,128)}), f32[4,12,2,12,256]{4,2,3,1,0:T(2,128)S(1)}, u32[]{:S(2)}, u32[]{:S(2)}) %all-to-all-start) | async-done | bytes 1179680 | tf_op jit(solution)/shard_map/all_to_all | solution.py:139
  31.7 1.5 convolution_bitcast_fusion
  33.2 0.1 copy-done.4
  33.3 7.1 %bitcast_add_fusion = f32[2,2,16,8,4,256]{5,2,0,3,4,1:T(8,128)S(1)} fusion(f32[1,2,2,1,1,16,8,4,256]{8,7,6,5,4,3,2,1,0:T(4,128)S(1)} %copy-done.4, f32[4,12,2,4,8,256,1]{5,4,2,1,3,0,6:T(8,128)S(1)} %convolution_bitcast_fusion, pred[2,16,8,4]{1,0,2,3:T(4,128)(4,1)S(1)} %copy.63, f32[4]{0:T(128)S(1)} %convert_element_type.9, s32[2,16]{1,0:T(2,128)S(1)} %iota_add_fusion.1, ...), kind=kOutput, calls=%fused_computation.14 | convolution fusion | flops 303041536 | bytes 7341392 | tf_op jit(solution)/shard_map/niqa,nautpe->iuqpte/dot_general | solution.py:152
  40.4 0.6 all_gather_reshape.3
  41.1 0.0 all-gather.6.cloned.1.call-update
  41.1 0.2 all-gather.8.cloned.1.call-start
  41.4 145.4 %all-gather.6.cloned.1.call-done = f32[128,8,1024]{2,1,0:T(8,128)} async-done(((f32[1,8,1024]{2,1,0:T(8,128)}), f32[128,8,1024]{2,1,0:T(8,128)}) %all-gather.6.cloned.1.call-update) | async-done | bytes 4194320 | tf_op jit(solution)/shard_map/all_gather | solution.py:164
  186.8 6.6 %copy.72 = f32[8,128,1024]{2,1,0:T(8,128)} copy(f32[8,128,1024]{2,0,1:T(8,128)} %bitcast.106) | data formatting | bytes 8388608 | tf_op jit(solution)/shard_map/transpose | solution.py:165
  193.4 0.2 copy.76
  193.6 25.7 %all_to_all.20 = f32[2,2,16,4,256]{4,0,3,1,2:T(2,128)} all-to-all(f32[2,2,16,4,256]{4,0,3,1,2:T(2,128)S(1)} %copy.76), channel_id=1, replica_groups=mesh['front'=4,'row'=16,'col'=8] {'row'}, dimensions={2} | all-to-all | bytes 524288 | tf_op jit(solution)/shard_map/all_to_all | solution.py:172
  219.3 0.0 all-gather.8.cloned.1.call-update
  219.3 0.8 copy.78
  220.1 4.0 all-to-all-start.3
  224.1 1.6 copy.105
  225.8 2.7 copy.74
  228.4 3.2 all-to-all-done.3
  231.7 9.2 %all-to-all-start.1 = ((f32[2,2,128,4,256]{4,3,1,0,2:T(4,128)}), f32[2,2,128,4,256]{4,3,1,0,2:T(4,128)}, u32[]{:S(2)}, u32[]{:S(2)}) async-start(f32[2,2,128,4,256]{4,3,1,0,2:T(4,128)} %copy.74), calls=%async_computation.1 | async-start | bytes 4194304 | tf_op jit(solution)/shard_map/all_to_all | solution.py:169
  240.9 0.3 all-gather.10.cloned.1.call-start
  241.1 0.8 copy.79
  241.9 0.0 all-gather.10.cloned.1.call-update
  242.0 0.1 dynamic-slice.25
  242.1 0.6 gather_fusion
  242.7 0.1 broadcast_compare_fusion.4
  242.8 0.1 broadcast_select_fusion.1
  242.9 0.1 broadcast_compare_fusion.2
  242.9 0.7 broadcast_compare_fusion
  243.6 2.2 copy-done.2
  245.8 61.3 %factor.1 = (f32[1024,1024]{1,0:T(8,128)S(1)}, f32[1024,128]{1,0:T(8,128)S(1)}) custom-call(f32[1024,1024]{1,0:T(8,128)S(1)} %bitcast.99), custom_call_target="tpu_custom_call" | custom-call | flops 49999998976 | bytes 16777216 | tf_op jit(solution)/shard_map/factor/pallas_call | solution.py:104
  307.1 0.3 tile.4
  307.4 1.7 copy-done
  309.1 3.0 copy.104
  312.1 3.3 copy.77
  315.3 1.8 reshape.509
  317.2 9.8 %fusion.5 = f32[512,1024]{1,0:T(8,128)S(1)} fusion(f32[512,1024]{1,0:T(8,128)S(1)} %reshape.509, f32[1024,1024]{1,0:T(8,128)} %copy-done, s32[1024]{0:T(1024)S(1)} %add_select_fusion), kind=kOutput, calls=%fused_computation.7 | convolution fusion | flops 6444548096 | bytes 8392704 | tf_op jit(solution)/shard_map/dot_general | solution.py:16
  327.0 0.2 copy.108
  327.2 1.9 copy-done.1
  329.2 1.5 fusion.25
  330.7 8.5 %fusion = f32[2,256,1024]{2,1,0:T(8,128)} fusion(f32[1024,1024]{1,0:T(8,128)S(1)} %copy-done.1, f32[2,256,1024]{2,1,0:T(8,128)S(1)} %fusion.25, s32[1024]{0:T(1024)S(1)} %add_select_fusion, pred[2,1024]{1,0:T(4,128)(4,1)S(1)} %broadcast_compare_fusion.2), kind=kOutput, calls=%fused_computation.2 | convolution fusion | flops 6445072384 | bytes 8394752 | tf_op jit(solution)/shard_map/dot_general | solution.py:16
  339.2 48.4 %all-gather.10.cloned.1.call-done = f32[2,2,2,128,4,256]{5,4,2,1,0,3:T(4,128)} async-done(((f32[2,2,2,8,4,256]{5,4,2,1,0,3:T(4,128)}), f32[2,2,2,128,4,256]{5,4,2,1,0,3:T(4,128)}) %all-gather.10.cloned.1.call-update) | async-done | bytes 4194320 | tf_op jit(solution)/shard_map/all_gather | solution.py:178
  387.6 4.9 %copy.80 = f32[2,2,2,128,4,256]{5,4,3,2,1,0:T(4,128)} copy(f32[2,2,2,128,4,256]{5,4,2,1,0,3:T(4,128)} %all-gather.10.cloned.1.call-done) | data formatting | bytes 8388608 | tf_op jit(solution)/shard_map/all_gather | solution.py:178
  392.5 6.0 %reshape.535 = f32[4,256,1024,1]{2,1,0,3:T(8,128)} reshape(f32[2,2,2,128,4,256]{5,4,3,2,1,0:T(4,128)} %copy.80) | data formatting | bytes 8388608 | tf_op jit(solution)/shard_map/reshape | solution.py:179
  398.5 3.0 copy.75
  401.5 8.8 %fusion.11 = f32[2,256,4,256]{3,1,2,0:T(8,128)S(1)} fusion(f32[2,2,128,4,256]{4,2,1,3,0:T(8,128)S(1)} %copy.75, f32[4,256,1024,1]{2,1,0,3:T(8,128)S(1)} %copy-done.3, f32[2,256,1024]{2,1,0:T(8,128)} %fusion, f32[2,256]{1,0:T(2,128)S(1)} %broadcast_select_fusion.1, pred[256,256]{1,0:T(8,128)(4,1)S(1)} %iota_compare_fusion, ...), kind=kOutput, calls=%fused_computation.16 | convolution fusion | flops 6444548096 | bytes 10553352 | tf_op jit(solution)/shard_map/dot_general | solution.py:196
  410.3 0.1 copy.109
  410.4 0.1 fusion.30
  410.5 3.5 copy.82
  (33 shorter events, 0.2 us)
Async XLA Ops:
  9.9 11.5 %copy-start.5 = (s32[1,32,32]{2,1,0:T(8,128)S(1)}, s32[1,32,32]{2,1,0:T(8,128)}, u32[]{:S(2)}) copy-start(s32[1,32,32]{2,1,0:T(8,128)} %param.15) | copy-start | bytes 12292
  9.9 11.8 %copy-start.7 = (s32[8,12]{1,0:T(8,128)S(1)}, s32[8,12]{1,0:T(8,128)}, u32[]{:S(2)}) copy-start(s32[8,12]{1,0:T(8,128)} %param.17) | copy-start | bytes 1156
  9.9 12.1 %copy-start.6 = (f32[1,32,256]{2,1,0:T(8,128)S(1)}, f32[1,32,256]{2,1,0:T(8,128)}, u32[]{:S(2)}) copy-start(f32[1,32,256]{2,1,0:T(8,128)} %param.14) | copy-start | bytes 98308
  11.8 19.9 %all-to-all-start = ((f32[4,12,2,12,256]{4,2,3,1,0:T(2,128)}), f32[4,12,2,12,256]{4,2,3,1,0:T(2,128)S(1)}, u32[]{:S(2)}, u32[]{:S(2)}) async-start(f32[4,12,2,12,256]{4,2,3,1,0:T(2,128)} %copy.67), calls=%async_computation | async-start | bytes 2359296 | tf_op jit(solution)/shard_map/all_to_all | solution.py:139
  21.2 165.5 %all-gather.6.cloned.1.call-start = ((), (), s32[]{:S(2)}) async-start(), calls=%async_computation.4 | async-start | bytes 4227072 | tf_op jit(solution)/shard_map/all_gather | solution.py:164
  31.7 1.6 copy-start.4
  41.1 271.0 %all-gather.8.cloned.1.call-start = ((), (), s32[]{:S(2)}) async-start(), calls=%async_computation.5 | async-start | bytes 2359296 | tf_op jit(solution)/shard_map/all_gather | solution.py:173
  220.1 11.5 %all-to-all-start.3 = ((f32[2,2,2,8,4,256]{5,2,0,4,1,3:T(2,128)}), f32[2,2,2,8,4,256]{5,2,0,4,1,3:T(2,128)S(1)}, u32[]{:S(2)}, u32[]{:S(2)}) async-start(f32[2,2,2,8,4,256]{5,2,0,4,1,3:T(2,128)} %copy.78), calls=%async_computation.3 | async-start | bytes 524288 | tf_op jit(solution)/shard_map/all_to_all | solution.py:176
  231.7 166.8 %all-to-all-start.1 = ((f32[2,2,128,4,256]{4,3,1,0,2:T(4,128)}), f32[2,2,128,4,256]{4,3,1,0,2:T(4,128)}, u32[]{:S(2)}, u32[]{:S(2)}) async-start(f32[2,2,128,4,256]{4,3,1,0,2:T(4,128)} %copy.74), calls=%async_computation.1 | async-start | bytes 4194304 | tf_op jit(solution)/shard_map/all_to_all | solution.py:169
  240.9 146.7 %all-gather.10.cloned.1.call-start = ((), (), s32[]{:S(2)}) async-start(), calls=%async_computation.6 | async-start | bytes 4456448 | tf_op jit(solution)/shard_map/all_gather | solution.py:178
  243.6 2.2 copy-start.2
  307.1 2.0 copy-start
  327.0 2.2 copy-start.1
  398.5 3.0 copy-start.3
Sparse Core Ops, SparseCore 0:
  41.2 145.5 all-gather.5
  219.4 28.5 all-gather.7
  250.1 137.4 all-gather.9

commit v2 on v1

--- a/solution.py
+++ b/solution.py
@@ -1,3 +1,5 @@
+import functools
+
 import jax
 import jax.numpy as jnp
 from jax import lax
@@ -10,10 +12,23 @@
 HIGHEST = lax.Precision.HIGHEST
 ROWS_BY_ROWS = (((1,), (1,)), ((), ()))
 ROWS_BY_COLUMNS = (((1,), (0,)), ((), ()))
+WHOLE = pl.BlockSpec(memory_space=pltpu.VMEM)
+SCALARS = pl.BlockSpec(memory_space=pltpu.SMEM)
 
 
 def times(left, right, numbers):
     return lax.dot_general(left, right, numbers, precision=HIGHEST, preferred_element_type=jnp.float32)
+
+
+def parts_of(value):
+    high = value.astype(jnp.bfloat16)
+    return high, (value - high.astype(jnp.float32)).astype(jnp.bfloat16)
+
+
+def times_parts(left, right, numbers):
+    pairs = ((left[0], right[0]), (left[0], right[1]), (left[1], right[0]))
+    products = [lax.dot_general(x, y, numbers, preferred_element_type=jnp.float32) for x, y in pairs]
+    return products[0] + (products[1] + products[2])
 
 
 def over_lanes(value, lane):
@@ -71,11 +86,23 @@
     return jnp.concatenate(upper, 0), jnp.concatenate(inverse, 0)
 
 
-def factor_kernel(top_ref, held_ref, diagonal_ref):
+def lower_pairs(blocks):
+    return [(m, n) for m in range(blocks) for n in range(m + 1)]
+
+
+def factor_kernel(packed_ref, lower_ref, inverse_ref, held_ref, diagonal_ref):
     blocks = held_ref.shape[0] // BLOCK
-    held_ref[...] = top_ref[...]
     row = lax.broadcasted_iota(jnp.int32, (BLOCK, BLOCK), 0)
     col = lax.broadcasted_iota(jnp.int32, (BLOCK, BLOCK), 1)
+    zeros = jnp.zeros((BLOCK, BLOCK), jnp.float32)
+
+    def at(ref, m, n):
+        return ref.at[m * BLOCK : (m + 1) * BLOCK, n * BLOCK : (n + 1) * BLOCK]
+
+    for place, (m, n) in enumerate(lower_pairs(blocks)):
+        at(held_ref, m, n)[...] = packed_ref[:, place * BLOCK : (place + 1) * BLOCK]
+        if m > n:
+            at(held_ref, n, m)[...] = zeros
 
     @pl.loop(0, blocks)
     def _(k):
@@ -87,7 +114,7 @@
 
         @pl.loop(k + 1, blocks)
         def _(j):
-            held_ref[here, pl.ds(pl.multiple_of(j * BLOCK, BLOCK), BLOCK)] = jnp.zeros((BLOCK, BLOCK), jnp.float32)
+            held_ref[here, pl.ds(pl.multiple_of(j * BLOCK, BLOCK), BLOCK)] = zeros
 
         held_ref[here, here] = jnp.where(row == col, 1.0, 0.0).astype(jnp.float32)
         held_ref[:, here] = times(held_ref[:, here], inverse, ROWS_BY_ROWS)
@@ -97,22 +124,127 @@
             there = pl.ds(pl.multiple_of(j * BLOCK, BLOCK), BLOCK)
             held_ref[:, there] = held_ref[:, there] - times(held_ref[:, here], held_ref[there, here], ROWS_BY_ROWS)
 
-
-def factor(top):
-    order = top.shape[0]
-    whole = pl.BlockSpec(memory_space=pltpu.VMEM)
+    for m, n in lower_pairs(blocks):
+        if m > n:
+            at(lower_ref, m, n)[...] = at(held_ref, m, n)[...]
+            at(lower_ref, n, m)[...] = zeros
+            at(inverse_ref, n, m)[...] = at(held_ref, n, m)[...]
+            at(inverse_ref, m, n)[...] = zeros
+        else:
+            at(lower_ref, m, m)[...] = diagonal_ref[m * BLOCK : (m + 1) * BLOCK, :]
+            at(inverse_ref, m, m)[...] = at(held_ref, m, m)[...]
+
+
+def factor(packed, order):
+    square = jax.ShapeDtypeStruct((order, order), jnp.float32)
     return pl.pallas_call(
         factor_kernel,
-        out_shape=(
-            jax.ShapeDtypeStruct((order, order), jnp.float32),
-            jax.ShapeDtypeStruct((order, BLOCK), jnp.float32),
-        ),
-        in_specs=[whole],
-        out_specs=(whole, whole),
+        out_shape=(square, square),
+        in_specs=[WHOLE],
+        out_specs=(WHOLE, WHOLE),
+        scratch_shapes=[pltpu.VMEM((order, order), jnp.float32), pltpu.VMEM((order, BLOCK), jnp.float32)],
         compiler_params=pltpu.CompilerParams(vmem_limit_bytes=40 * 2**20),
         cost_estimate=pl.CostEstimate(flops=50 * 10**9, bytes_accessed=16 * 2**20, transcendentals=1024),
         name="factor",
-    )(top)
+    )(packed)
+
+
+def solve_kernel(grid_rows, place_ref, rows_ref, lower_ref, inverse_ref, solved_ref, sides_ref):
+    total, order = solved_ref.shape
+    size = order // PANELS
+    per = size // BLOCK
+    my_row = place_ref[0]
+    inverse = [
+        [parts_of(inverse_ref[j * size : (j + 1) * size, k * size : (k + 1) * size]) if k >= j else None for k in range(PANELS)]
+        for j in range(PANELS)
+    ]
+    rows = [parts_of(jnp.concatenate([rows_ref[per * k + h] for h in range(per)], axis=1)) for k in range(PANELS)]
+    for k in range(PANELS):
+        total_k = times_parts(rows[0], inverse[0][k], ROWS_BY_COLUMNS)
+        for j in range(1, k + 1):
+            total_k = total_k + times_parts(rows[j], inverse[j][k], ROWS_BY_COLUMNS)
+        solved_ref[:, k * size : (k + 1) * size] = total_k
+
+    @pl.when(my_row < PANELS)
+    def _():
+        solved_ref[0:size, :] = lower_ref[pl.ds(pl.multiple_of(my_row * size, size), size), :]
+
+    tile = lax.broadcasted_iota(jnp.int32, (total, size), 0) // size * grid_rows + my_row
+    used = [parts_of(jnp.where(tile > k, solved_ref[:, k * size : (k + 1) * size], 0.0)) for k in range(PANELS)]
+    for j in range(PANELS):
+        total_j = times_parts(used[j], inverse[j][j], ROWS_BY_ROWS)
+        for k in range(j + 1, PANELS):
+            total_j = total_j + times_parts(used[k], inverse[j][k], ROWS_BY_ROWS)
+        sides_ref[:, j * size : (j + 1) * size] = total_j
+
+
+def solve(place, rows, lower, inverse, grid_rows):
+    out = jax.ShapeDtypeStruct((rows.shape[1], lower.shape[0]), jnp.float32)
+    return pl.pallas_call(
+        functools.partial(solve_kernel, grid_rows),
+        out_shape=(out, out),
+        in_specs=[SCALARS, WHOLE, WHOLE, WHOLE],
+        out_specs=(WHOLE, WHOLE),
+        compiler_params=pltpu.CompilerParams(vmem_limit_bytes=48 * 2**20),
+        cost_estimate=pl.CostEstimate(flops=8 * 10**9, bytes_accessed=14 * 2**20, transcendentals=0),
+        name="solve",
+    )(place, rows, lower, inverse)
+
+
+def finish_kernel(grid_rows, grid_cols, place_ref, tiles_ref, sides_ref, across_ref, solved_ref, boost_ref, out_ref):
+    t = pl.program_id(0)
+    my_row, my_col = place_ref[0], place_ref[1]
+    size = boost_ref.shape[2]
+    halves = size // BLOCK
+    local_rows = sides_ref.shape[0] // size
+    lines = tiles_ref.shape[0] // BLOCK
+    per = lines // (local_rows * halves)
+    order = sides_ref.shape[1]
+    across = jnp.concatenate([across_ref[:, u].reshape(BLOCK, order) for u in range(halves)], axis=0)
+    change = times_parts(parts_of(sides_ref[...]), parts_of(across), ROWS_BY_ROWS)
+    row = lax.broadcasted_iota(jnp.int32, (BLOCK, BLOCK), 0)
+    col = lax.broadcasted_iota(jnp.int32, (BLOCK, BLOCK), 1)
+    in_panel = jnp.logical_and(t == 0, my_col < PANELS)
+    for i in range(local_rows):
+        on_diagonal = i * grid_rows + my_row == t * grid_cols + my_col
+        for u in range(halves):
+            for h in range(halves):
+                start = i * size + u * BLOCK
+                value = tiles_ref[pl.ds((i * halves + u) * per + t * halves + h, BLOCK, stride=lines), :]
+                value = value - change[start : start + BLOCK, h * BLOCK : (h + 1) * BLOCK]
+                if u == h:
+                    line = boost_ref[i * grid_rows + my_row][:, h * BLOCK : (h + 1) * BLOCK]
+                    value = value + jnp.where(jnp.logical_and(on_diagonal, row == col), line, 0.0)
+                lane = pl.multiple_of(jnp.minimum(my_col, PANELS - 1) * size + h * BLOCK, BLOCK)
+                value = jnp.where(in_panel, solved_ref[start : start + BLOCK, pl.ds(lane, BLOCK)], value)
+                out_ref[pl.ds(start * per + t * halves + h, BLOCK, stride=per), :] = value
+
+
+def finish(place, tiles, sides, across, solved, boost, grid_rows, grid_cols):
+    ranks, lines, cols, order = across.shape
+    halves = boost.shape[2] // BLOCK
+    steps = lines // halves
+
+    def still(*shape):
+        return pl.BlockSpec(shape, lambda t: (0,) * len(shape))
+
+    return pl.pallas_call(
+        functools.partial(finish_kernel, grid_rows, grid_cols),
+        grid=(steps,),
+        out_shape=jax.ShapeDtypeStruct(tiles.shape, jnp.float32),
+        in_specs=[
+            SCALARS,
+            still(*tiles.shape),
+            still(*sides.shape),
+            pl.BlockSpec((ranks, halves, cols, order), lambda t: (0, t, 0, 0)),
+            still(*solved.shape),
+            still(*boost.shape),
+        ],
+        out_specs=still(*tiles.shape),
+        compiler_params=pltpu.CompilerParams(vmem_limit_bytes=48 * 2**20),
+        cost_estimate=pl.CostEstimate(flops=4 * 10**9, bytes_accessed=12 * 2**20, transcendentals=0),
+        name="finish",
+    )(place, tiles, sides, across, solved, boost)
 
 
 def body(front_entries, child_updates, diag_boost, tile_mask, child_parent, child_index):
@@ -143,15 +275,17 @@
 
     entries = front_entries.reshape(local_rows, slices, grid_rows, grid_cols, local_cols, size)
     mask_tiles = jnp.transpose(tile_mask[0].reshape(local_rows, grid_rows, local_cols, grid_cols), (0, 1, 3, 2))
-    masked = jnp.where(mask_tiles[:, None, :, :, :, None] == 1, entries, 0.0)
+    kept = (mask_tiles == 1)[:, None, :, :, :, None]
     row_ids = jnp.arange(local_rows)[:, None] * grid_rows + jnp.arange(grid_rows)[None, :]
     col_ids = jnp.arange(local_cols)[:, None] * grid_cols + jnp.arange(grid_cols)[None, :]
     row_hits = (index[:, None, None, :] == row_ids[None, :, :, None]).astype(jnp.float32) * weight[:, None, None, None]
     col_hits = (index[:, None, None, :] == col_ids[None, :, :, None]).astype(jnp.float32)
-    spread = jnp.einsum("naube,ntpb->nautpe", arrived, col_hits, precision=HIGHEST)
-    assembled = masked + jnp.einsum("niqa,nautpe->iuqpte", row_hits, spread, precision=HIGHEST)
-
-    panel = assembled[:, :, :, :PANELS, 0, :]
+    first = index[:, :PANELS, None] == jnp.arange(PANELS)
+    narrow = jnp.sum(
+        jnp.where(first[:, None, None, :, :, None], arrived[:, :, :, :PANELS, None, :], 0.0), axis=3
+    )
+    panel = jnp.where(kept[:, :, :, :PANELS, 0], entries[:, :, :, :PANELS, 0, :], 0.0)
+    panel = panel + jnp.einsum("niqa,nauke->iuqke", row_hits, narrow, precision=HIGHEST)
     within = jnp.arange(slices) * grid_rows * grid_cols + my_row * grid_cols + my_col
     boost = jnp.where(
         within[:, None, None, None] == jnp.arange(size),
@@ -160,52 +294,40 @@
     )
     panel = panel.at[0, :, :PANELS].add(boost)
 
-    top = jnp.transpose(panel[0, :, :PANELS], (1, 0, 2, 3)).reshape(PANELS * slices, order)
-    gathered = lax.all_gather(top, ("row", "col"), axis=0)
-    top_block = jnp.transpose(gathered, (1, 0, 2)).reshape(order, order)
-
-    assembled, panel, top_block = lax.optimization_barrier((assembled, panel, top_block))
-    joined = assembled.reshape(local_rows, slices, grid_rows * grid_cols, local_cols, size)
-    relaid = lax.all_to_all(joined, ("row", "col"), split_axis=2, concat_axis=2, tiled=True)
-    tiles = relaid.reshape(local_rows, size, local_cols, size)
-
-    for_rows = lax.all_to_all(panel, "row", split_axis=2, concat_axis=2, tiled=True)
-    for_rows = lax.all_gather(for_rows, "col", axis=3)
-    row_panel = for_rows.reshape(local_rows * size, order)
-    split = panel.reshape(local_rows, slices, halves, grid_cols, PANELS, size)
-    for_cols = lax.all_to_all(split, "col", split_axis=3, concat_axis=3, tiled=True)
-    for_cols = jnp.transpose(for_cols, (0, 2, 1, 3, 4, 5))
-    for_cols = lax.all_gather(for_cols, "row", axis=3)
-    col_panel = for_cols.reshape(local_cols, size, order)
-
-    both, diagonal = factor(top_block)
-    block_row = jnp.arange(order)[:, None] // BLOCK
-    block_col = jnp.arange(order)[None, :] // BLOCK
-    lower = jnp.where(block_row > block_col, both, 0.0)
-    lower = jnp.where(block_row == block_col, jnp.tile(diagonal, (1, order // BLOCK)), lower)
-    inverse = jnp.where(block_row > block_col, 0.0, both)
-
-    solved = times(row_panel, inverse, ROWS_BY_COLUMNS).reshape(local_rows, size, order)
-    own = lax.dynamic_slice_in_dim(lower, jnp.minimum(my_row, PANELS - 1) * size, size, 0)
-    solved = solved.at[0].set(jnp.where(my_row < PANELS, own, solved[0]))
-    tile_ids = jnp.arange(local_rows) * grid_rows + my_row
-    panel_ids = jnp.arange(order) // size
-    update = jnp.where(tile_ids[:, None, None] > panel_ids[None, None, :], solved, 0.0)
-    both_sides = times(update.reshape(local_rows * size, order), inverse, ROWS_BY_ROWS)
-
-    change = lax.dot_general(
-        both_sides, col_panel, (((1,), (2,)), ((), ())), precision=HIGHEST, preferred_element_type=jnp.float32
-    )
-    tiles = tiles - change.reshape(local_rows, size, local_cols, size)
-    global_rows = jnp.arange(local_rows) * grid_rows + my_row
-    global_cols = jnp.arange(local_cols) * grid_cols + my_col
-    boosts = jnp.take(diag_boost[0], global_rows, axis=0)
-    on_diagonal = global_rows[:, None] == global_cols[None, :]
-    placed = on_diagonal[:, None, :, None] & jnp.eye(size, dtype=bool)[None, :, None, :]
-    tiles = tiles + jnp.where(placed, boosts[:, :, None, None], 0.0)
-    column = lax.dynamic_slice_in_dim(solved, jnp.minimum(my_col, PANELS - 1) * size, size, 2)
-    tiles = tiles.at[:, :, 0, :].set(jnp.where(my_col < PANELS, column, tiles[:, :, 0, :]))
-    return tiles.reshape(1, local_rows, 1, size, local_cols, 1, size)
+    blocks = order // BLOCK
+    top = jnp.transpose(panel[0, :, :PANELS], (1, 0, 2, 3)).reshape(blocks, order)
+    packed = jnp.concatenate([top[m, : (m + 1) * BLOCK] for m in range(blocks)])
+    over_row = lax.all_gather(packed, "row", axis=0)
+
+    split = panel.reshape(local_rows, slices, halves, grid_cols, order)
+    split = jnp.transpose(split, (3, 0, 2, 1, 4)).reshape(grid_cols, local_cols * slices, 1, order)
+    for_cols = lax.all_to_all(split, "col", split_axis=0, concat_axis=2, tiled=True)
+    for_cols = for_cols.reshape(local_cols * slices, grid_cols, order)
+    lines = jnp.transpose(panel.reshape(local_rows, slices, grid_rows, grid_cols, BLOCK), (2, 3, 0, 1, 4))
+    lines = lines.reshape(grid_rows * grid_cols, local_rows * slices, BLOCK)
+    for_rows = lax.all_to_all(lines, ("row", "col"), split_axis=0, concat_axis=0, tiled=True)
+    for_rows = jnp.transpose(for_rows, (1, 0, 2)).reshape(local_rows * size, BLOCK)
+
+    spread = jnp.einsum("naube,ntpb->nautpe", arrived, col_hits, precision=HIGHEST)
+    assembled = jnp.where(kept, entries, 0.0) + jnp.einsum("niqa,nautpe->iuqpte", row_hits, spread, precision=HIGHEST)
+    joined = jnp.transpose(assembled, (2, 3, 0, 1, 4, 5))
+    joined = joined.reshape(grid_rows * grid_cols, local_rows * slices, local_cols * size // BLOCK, BLOCK)
+
+    over_row, joined, for_cols = lax.optimization_barrier((over_row, joined, for_cols))
+    across = lax.all_gather(for_cols, "row", axis=0)
+    copies = jnp.broadcast_to(over_row[None], (grid_cols,) + over_row.shape)
+    over_both = lax.all_to_all(copies, "col", split_axis=0, concat_axis=0, tiled=True)
+    over_both = jnp.transpose(over_both, (1, 0, 2)).reshape(grid_rows * grid_cols, packed.shape[0])
+    copies = jnp.broadcast_to(for_rows[None], (grid_cols,) + for_rows.shape)
+    row_panel = lax.all_to_all(copies, "col", split_axis=0, concat_axis=0, tiled=True)
+    tiles = lax.all_to_all(joined, ("row", "col"), split_axis=0, concat_axis=0, tiled=True)
+    tiles = tiles.reshape(-1, BLOCK)
+
+    place = jnp.stack([my_row, my_col]).astype(jnp.int32)
+    lower, inverse = factor(over_both, order)
+    solved, sides = solve(place, row_panel, lower, inverse, grid_rows)
+    out = finish(place, tiles, sides, across, solved, diag_boost[0][:, None, :], grid_rows, grid_cols)
+    return out.reshape(1, local_rows, 1, size, local_cols, 1, size)
 
 
 def solution(mesh):

time: 429 us -> 374 us (0.87)
  the two profiles are of different devices: /device:TPU:2 before, /device:TPU:1 now
where the time goes in v2:
time: 374 us; the launch traced here: 368 us
  waiting for transfers between devices  92.3 us (25%)
  Pallas kernels  80.5 us (22%)
  blocking collectives  59.2 us (16%)
  starting transfers between devices  58.9 us (16%)
  local copies, waits for them, and re-layouts  49.7 us (13%)
  between operations  13.7 us (4%)
  matrix products  10.8 us (3%)
    pallas_call x1, Pallas kernels, factor(): pl.pallas_call(factor_kernel, out_shape=(square, square), in_specs=[WHOLE...  62.5 us
    all_gather x1, waiting for transfers between devices, body(): across = lax.all_gather(for_cols, 'row', axis=0)  57.4 us
    all_to_all x1, blocking collectives, body(): lax.all_to_all(copies, 'col', split_axis=0, concat_axis=0, tiled=True)  30.5 us
    all_to_all x1, waiting for transfers between devices, body(): lax.all_to_all(copies, 'col', split_axis=0, concat_axis=0, tiled=True)  29.1 us
    all_gather x1, blocking collectives, body(): over_row = lax.all_gather(packed, 'row', axis=0)  28.6 us
    unnamed x48, local copies, waits for them, and re-layouts  22.7 us
    all_to_all x1, starting transfers between devices, body(): lax.all_to_all(lines, ('row', 'col'), split_axis=0, concat_axis=0, tiled=...  19.4 us
    all_to_all x1, starting transfers between devices, body(): lax.all_to_all(joined, ('row', 'col'), split_axis=0, concat_axis=0, tiled...  13.4 us
  transfers between devices with their start and end apart: 6, of which 3 were waited for; matrix products, arithmetic and copies ran while one was open for 11% of the time, Pallas kernels for 20%

profile of v2, /device:TPU:1, one launch (start us, length us, event | category | flops | bytes accessed | tf_op | source)
XLA Modules:
  0.0 368.1 jit_solution(18309712848284143765)
XLA Ops:
  6.5 0.7 reshape.219
  7.4 1.4 copy.132
  8.8 1.0 select_reduce_fusion
  9.8 1.9 copy.82
  11.8 4.8 %all-to-all-start = ((f32[4,12,2,12,256]{4,2,3,1,0:T(2,128)}), f32[4,12,2,12,256]{4,2,3,1,0:T(2,128)S(1)}, u32[]{:S(2)}, u32[]{:S(2)}) async-start(f32[4,12,2,12,256]{4,2,3,1,0:T(2,128)} %copy.82), calls=%async_computation | async-start | bytes 2359296 | tf_op jit(solution)/shard_map/all_to_all | solution.py:271
  16.6 0.1 fusion.25
  16.9 0.1 copy.107
  17.1 2.5 copy.131
  19.6 0.7 iota_add_fusion
  20.3 0.1 copy.86
  20.4 0.1 select_reduce_fusion.2
  20.7 0.7 slice_bitcast_fusion.1
  21.5 5.8 %all-to-all-done = f32[4,12,2,12,256]{4,2,3,1,0:T(2,128)S(1)} async-done(((f32[4,12,2,12,256]{4,2,3,1,0:T(2,128)}), f32[4,12,2,12,256]{4,2,3,1,0:T(2,128)S(1)}, u32[]{:S(2)}, u32[]{:S(2)}) %all-to-all-start) | async-done | bytes 1179680 | tf_op jit(solution)/shard_map/all_to_all | solution.py:271
  27.3 0.1 slice.92
  27.4 0.1 copy.83
  27.6 0.6 select_reduce_fusion.1
  28.2 1.6 fusion.6
  29.9 0.6 slice.95
  30.4 0.6 slice_reduce_fusion.3
  31.0 0.6 slice.97
  31.6 0.6 slice_reduce_fusion.2
  32.2 1.3 constant_dynamic-update-slice_fusion.7
  33.5 0.2 copy.90
  33.7 0.8 reshape.223
  34.5 1.0 copy.91
  35.5 0.9 copy.92
  36.3 11.2 %all-to-all-start.1 = ((f32[8,8,1,1024]{3,1,2,0:T(8,128)}), f32[8,8,1,1024]{3,1,2,0:T(8,128)}, u32[]{:S(2)}, u32[]{:S(2)}) async-start(f32[8,8,1,1024]{3,1,2,0:T(8,128)} %copy.92), calls=%async_computation.1 | async-start | bytes 524288 | tf_op jit(solution)/shard_map/all_to_all | solution.py:304
  47.6 1.3 constant_dynamic-update-slice_fusion.6
  48.9 1.3 constant_dynamic-update-slice_fusion.5
  50.2 1.3 constant_dynamic-update-slice_fusion.4
  51.4 1.3 constant_dynamic-update-slice_fusion.3
  52.7 1.3 slice.101
  54.1 0.8 reshape.227
  54.9 1.8 copy.94
  56.7 1.3 slice_reduce_fusion.1
  58.0 1.3 slice_reduce_fusion
  59.4 19.4 %all-to-all-start.3 = ((f32[128,4,128]{2,1,0:T(4,128)}), f32[128,4,128]{2,1,0:T(4,128)S(1)}, u32[]{:S(2)}, u32[]{:S(2)}) async-start(f32[128,4,128]{2,1,0:T(4,128)} %copy.94), calls=%async_computation.3 | async-start | bytes 524288 | tf_op jit(solution)/shard_map/all_to_all | solution.py:308
  78.8 1.3 constant_dynamic-update-slice_fusion.2
  80.1 1.3 constant_dynamic-update-slice_fusion.1
  81.4 1.3 constant_dynamic-update-slice_fusion
  82.7 0.7 reshape.233
  83.4 28.6 %all-gather.2 = f32[16,1,4608]{2,1,0:T(1,128)S(1)} all-gather(f32[1,1,4608]{2,1,0:T(1,128)S(1)} %reshape.233), channel_id=2, replica_groups=mesh['front'=4,'row'=16,'col'=8] {'row'}, dimensions={0}, use_global_device_ids=true | all-gather | bytes 313344 | tf_op jit(solution)/shard_map/all_gather | solution.py:300
  112.1 0.7 copy.133
  112.8 2.2 convolution_bitcast_fusion
  115.1 7.0 %fusion.2 = f32[16,8,2,2,4,256]{5,0,2,1,3,4:T(8,128)S(1)} fusion(f32[4,12,2,4,8,256,1]{5,4,2,1,3,0,6:T(8,128)S(1)} %convolution_bitcast_fusion, pred[2,16,8,4]{1,0,2,3:T(4,128)(4,1)S(1)} %copy.86, f32[4]{0:T(128)S(1)} %copy-done.17, s32[2,16]{1,0:T(2,128)S(1)} %copy-done.14, s32[4,12]{1,0:T(4,128)S(1)} %copy-done.10, ...), kind=kOutput, calls=%fused_computation.5 | convolution fusion | flops 303041536 | bytes 7341392 | tf_op jit(solution)/shard_map/niqa,nautpe->iuqpte/dot_general | solution.py:312
  122.0 1.4 copy.89
  123.4 1.8 reshape.222
  125.3 1.6 broadcast_in_dim.178
  126.9 10.0 %all-to-all-start.5 = ((f32[8,16,4608]{2,1,0:T(8,128)}), f32[8,16,4608]{2,1,0:T(8,128)S(1)}, u32[]{:S(2)}, u32[]{:S(2)}) async-start(f32[8,16,4608]{2,1,0:T(8,128)} %broadcast_in_dim.178), calls=%async_computation.5 | async-start | bytes 4718592 | tf_op jit(solution)/shard_map/all_to_all | solution.py:319
  136.9 29.1 %all-to-all-done.5 = f32[8,16,4608]{2,1,0:T(8,128)S(1)} async-done(((f32[8,16,4608]{2,1,0:T(8,128)}), f32[8,16,4608]{2,1,0:T(8,128)S(1)}, u32[]{:S(2)}, u32[]{:S(2)}) %all-to-all-start.5) | async-done | bytes 2359328 | tf_op jit(solution)/shard_map/all_to_all | solution.py:319
  166.0 0.1 broadcast_in_dim.177
  166.2 30.5 %all_to_all.40.rows_ref = f32[8,512,128]{2,1,0:T(8,128)} all-to-all(f32[8,512,128]{2,1,0:T(8,128)S(1)} %broadcast_in_dim.177), channel_id=1, replica_groups=mesh['front'=4,'row'=16,'col'=8] {'col'}, dimensions={0} | all-to-all | bytes 4194304 | tf_op jit(solution)/shard_map/all_to_all | solution.py:322
  196.7 13.4 %all-to-all-start.2 = ((f32[128,4,8,128]{3,2,1,0:T(8,128)}), f32[128,4,8,128]{3,2,1,0:T(8,128)S(1)}, u32[]{:S(2)}, u32[]{:S(2)}) async-start(f32[128,4,8,128]{3,2,1,0:T(8,128)} %reshape.222), calls=%async_computation.2 | async-start | bytes 4194304 | tf_op jit(solution)/shard_map/all_to_all | solution.py:323
  210.2 1.8 copy.97
  212.2 3.0 copy.130
  215.2 62.5 %factor.1 = (f32[1024,1024]{1,0:T(8,128)S(1)}, f32[1024,1024]{1,0:T(8,128)S(1)}) custom-call(f32[128,4608]{1,0:T(8,128)S(1)} %bitcast.102), custom_call_target="tpu_custom_call" | custom-call | flops 49999998976 | bytes 16777216 | tf_op jit(solution)/shard_map/factor/pallas_call | solution.py:140
  277.7 2.0 copy-done.3
  279.7 2.0 copy-done.4
  281.6 9.6 %solve.1 = (f32[512,1024]{1,0:T(8,128)S(1)}, f32[512,1024]{1,0:T(8,128)S(1)}) custom-call(s32[2]{0:T(128)S(1)} %pad_add_fusion.place_ref, f32[8,512,128]{2,1,0:T(8,128)} %all_to_all.40.rows_ref, f32[1024,1024]{1,0:T(8,128)} %copy-done.3, f32[1024,1024]{1,0:T(8,128)} %copy-done.4), custom_call_target="tpu_custom_call" | custom-call | flops 8000000000 | bytes 14680064 | tf_op jit(solution)/shard_map/solve/pallas_call | solution.py:183
  291.3 1.3 copy-done
  292.6 1.3 copy-done.1
  293.9 57.4 %all-gather.5.cloned.1.call-done = f32[128,8,1024]{2,1,0:T(8,128)} async-done(((f32[8,8,1024]{2,1,0:T(8,128)}), f32[128,8,1024]{2,1,0:T(8,128)}) %all-gather.5.cloned.1.call-update) | async-done | bytes 4194320 | tf_op jit(solution)/shard_map/all_gather | solution.py:317
  351.3 1.6 copy-done.2
  352.9 8.4 %finish.1 = f32[4096,128]{1,0:T(8,128)} custom-call(s32[2]{0:T(128)S(1)} %pad_add_fusion.place_ref, f32[4096,128]{1,0:T(8,128)S(1)} %bitcast.103, f32[512,1024]{1,0:T(8,128)S(1)} %copy-done.2, f32[16,8,8,1024]{3,2,1,0:T(8,128)} %bitcast.131, f32[512,1024]{1,0:T(8,128)} %copy-done, f32[32,1,256]{2,1,0:T(1,128)S(1)} %broadcast_in_dim_squeeze.4.boost_ref), custom_call_target="tpu_custom_call" | custom-call | flops 4000000000 | bytes 12582912 | tf_op jit(solution)/shard_map/finish/pallas_call | solution.py:231
  (57 shorter events, 0.9 us)
Async XLA Ops:
  9.8 7.0 %copy-start.12 = (s32[1,32,32]{2,1,0:T(8,128)S(1)}, s32[1,32,32]{2,1,0:T(8,128)}, u32[]{:S(2)}) copy-start(s32[1,32,32]{2,1,0:T(8,128)} %param.11) | copy-start | bytes 12292
  9.8 7.3 %copy-start.6 = (f32[1,2,2,1,1,16,8,4,256]{8,7,6,5,4,3,2,1,0:T(4,128)S(1)}, f32[1,2,2,1,1,16,8,4,256]{8,7,6,5,4,3,2,1,0:T(4,128)}, u32[]{:S(2)}) copy-start(f32[1,2,2,1,1,16,8,4,256]{8,7,6,5,4,3,2,1,0:T(4,128)} %param.8) | copy-start | bytes 6291460
  11.8 15.5 %all-to-all-start = ((f32[4,12,2,12,256]{4,2,3,1,0:T(2,128)}), f32[4,12,2,12,256]{4,2,3,1,0:T(2,128)S(1)}, u32[]{:S(2)}, u32[]{:S(2)}) async-start(f32[4,12,2,12,256]{4,2,3,1,0:T(2,128)} %copy.82), calls=%async_computation | async-start | bytes 2359296 | tf_op jit(solution)/shard_map/all_to_all | solution.py:271
  16.8 11.4 %copy-start.16 = (f32[4]{0:T(128)}, f32[4]{0:T(128)S(1)}, u32[]{:S(2)}) copy-start(f32[4]{0:T(128)S(1)} %convert_element_type.9) | copy-start | bytes 52
  17.1 11.1 %copy-start.13 = (s32[2,16]{1,0:T(2,128)}, s32[2,16]{1,0:T(2,128)S(1)}, u32[]{:S(2)}) copy-start(s32[2,16]{1,0:T(2,128)S(1)} %iota_add_fusion.1) | copy-start | bytes 388
  17.1 3.3 copy-start.15
  20.5 13.0 %copy-start.9 = (s32[4,12]{1,0:T(4,128)}, s32[4,12]{1,0:T(4,128)S(1)}, u32[]{:S(2)}) copy-start(s32[4,12]{1,0:T(4,128)S(1)} %select_reduce_fusion.2) | copy-start | bytes 580
  29.8 3.7 copy-start.8
  36.3 23.1 %all-to-all-start.1 = ((f32[8,8,1,1024]{3,1,2,0:T(8,128)}), f32[8,8,1,1024]{3,1,2,0:T(8,128)}, u32[]{:S(2)}, u32[]{:S(2)}) async-start(f32[8,8,1,1024]{3,1,2,0:T(8,128)} %copy.92), calls=%async_computation.1 | async-start | bytes 524288 | tf_op jit(solution)/shard_map/all_to_all | solution.py:304
  59.4 65.9 %all-to-all-start.3 = ((f32[128,4,128]{2,1,0:T(4,128)}), f32[128,4,128]{2,1,0:T(4,128)S(1)}, u32[]{:S(2)}, u32[]{:S(2)}) async-start(f32[128,4,128]{2,1,0:T(4,128)} %copy.94), calls=%async_computation.3 | async-start | bytes 524288 | tf_op jit(solution)/shard_map/all_to_all | solution.py:308
  112.8 2.2 copy-start.10
  112.8 2.2 copy-start.14
  112.8 2.3 copy-start.17
  123.4 1.9 copy-start.7
  126.9 39.1 %all-to-all-start.5 = ((f32[8,16,4608]{2,1,0:T(8,128)}), f32[8,16,4608]{2,1,0:T(8,128)S(1)}, u32[]{:S(2)}, u32[]{:S(2)}) async-start(f32[8,16,4608]{2,1,0:T(8,128)} %broadcast_in_dim.178), calls=%async_computation.5 | async-start | bytes 4718592 | tf_op jit(solution)/shard_map/all_to_all | solution.py:319
  166.0 30.7 %copy-start.5 = (f32[8,16,4608]{2,1,0:T(8,128)}, f32[8,16,4608]{2,1,0:T(8,128)S(1)}, u32[]{:S(2)}) copy-start(f32[8,16,4608]{2,1,0:T(8,128)S(1)} %all-to-all-done.5) | copy-start | bytes 7077892
  196.7 15.3 %copy-start.11 = (f32[1,32,256]{2,1,0:T(8,128)S(1)}, f32[1,32,256]{2,1,0:T(8,128)}, u32[]{:S(2)}) copy-start(f32[1,32,256]{2,1,0:T(8,128)} %param.10) | copy-start | bytes 98308
  196.7 154.6 %all-to-all-start.2 = ((f32[128,4,8,128]{3,2,1,0:T(8,128)}), f32[128,4,8,128]{3,2,1,0:T(8,128)S(1)}, u32[]{:S(2)}, u32[]{:S(2)}) async-start(f32[128,4,8,128]{3,2,1,0:T(8,128)} %reshape.222), calls=%async_computation.2 | async-start | bytes 4194304 | tf_op jit(solution)/shard_map/all_to_all | solution.py:323
  210.1 141.1 %all-gather.5.cloned.1.call-start = ((), (), s32[]{:S(2)}) async-start(), calls=%async_computation.6 | async-start | bytes 4456448 | tf_op jit(solution)/shard_map/all_gather | solution.py:317
  277.7 2.0 copy-start.3
  279.7 2.0 copy-start.4
  291.2 1.3 copy-start
  292.6 1.3 copy-start.1
  351.3 1.6 copy-start.2
Sparse Core Ops, SparseCore 0:
  213.1 138.1 all-gather.4

commit v3 on v2

--- a/solution.py
+++ b/solution.py
@@ -86,12 +86,75 @@
     return jnp.concatenate(upper, 0), jnp.concatenate(inverse, 0)
 
 
-def lower_pairs(blocks):
-    return [(m, n) for m in range(blocks) for n in range(m + 1)]
-
-
-def factor_kernel(packed_ref, lower_ref, inverse_ref, held_ref, diagonal_ref):
+def dealt_pairs(blocks):
+    share = (blocks + 2) // 2
+    dealt = [None] * blocks
+    for a in range(blocks // 2):
+        both = [(m, a) for m in range(a, blocks)] + [(m, blocks - 1 - a) for m in range(blocks - 1 - a, blocks)]
+        dealt[a], dealt[blocks - 1 - a] = both[:share], both[share:]
+    return [pairs + [(0, blocks - 1)] * (share - len(pairs)) for pairs in dealt]
+
+
+def panel_kernel(grid_rows, index_ref, base_ref, narrow_ref, lines_ref, split_ref, rows_ref):
+    groups, child_tiles = index_ref.shape
+    total, blocks, _ = base_ref.shape
+    slices = narrow_ref.shape[0] // (groups * child_tiles)
+    local_rows = total // (slices * grid_rows)
+    dealt = dealt_pairs(blocks)
+    share = len(dealt[0])
+    per = local_rows * slices + share
+    rows_ref[...] = base_ref[...]
+    for g in range(groups):
+        for a in range(child_tiles):
+            tile = index_ref[g, a]
+            for u in range(slices):
+                at = (tile // grid_rows * slices + u) * grid_rows + lax.rem(tile, grid_rows)
+                rows_ref[at] = rows_ref[at] + narrow_ref[(g * child_tiles + a) * slices + u]
+    for q in range(grid_rows):
+        for line in range(local_rows * slices):
+            lines_ref[pl.ds(q * blocks * per + line, blocks, stride=per), :] = rows_ref[line * grid_rows + q]
+    for p in range(blocks):
+        for j, (m, n) in enumerate(dealt[p]):
+            value = rows_ref[m % slices * grid_rows + m // slices][n : n + 1, :]
+            start = p * per + local_rows * slices + j
+            lines_ref[pl.ds(start, grid_rows, stride=blocks * per), :] = jnp.broadcast_to(value, (grid_rows, BLOCK))
+    halves = grid_rows // blocks
+    for p in range(blocks):
+        for i in range(local_rows):
+            for h in range(halves):
+                for u in range(slices):
+                    split_ref[p, (i * halves + h) * slices + u] = rows_ref[(i * slices + u) * grid_rows + h * blocks + p]
+
+
+def make_panel(index, base, narrow, grid_rows):
+    total, blocks, _ = base.shape
+    per = total // grid_rows + len(dealt_pairs(blocks)[0])
+    return pl.pallas_call(
+        functools.partial(panel_kernel, grid_rows),
+        out_shape=(
+            jax.ShapeDtypeStruct((grid_rows * blocks * per, BLOCK), jnp.float32),
+            jax.ShapeDtypeStruct((blocks, total // blocks, blocks, BLOCK), jnp.float32),
+        ),
+        in_specs=[SCALARS, WHOLE, WHOLE],
+        out_specs=(WHOLE, WHOLE),
+        scratch_shapes=[pltpu.VMEM(base.shape, jnp.float32)],
+        cost_estimate=pl.CostEstimate(flops=10**6, bytes_accessed=2 * 2**20, transcendentals=0),
+        name="panel",
+    )(index, base, narrow)
+
+
+SOURCES = (0, 1, -1, 2)
+
+
+def source_col(place_ref, step, core):
+    chip = lax.rem(place_ref[1] // 2 - SOURCES[step] + 4, 4)
+    mine = lax.rem(place_ref[1], 2)
+    return chip * 2 + (mine if core == 0 else 1 - mine)
+
+
+def factor_kernel(place_ref, pairs_ref, own_ref, other_ref, lower_ref, inverse_ref, held_ref, diagonal_ref):
     blocks = held_ref.shape[0] // BLOCK
+    share = own_ref.shape[1]
     row = lax.broadcasted_iota(jnp.int32, (BLOCK, BLOCK), 0)
     col = lax.broadcasted_iota(jnp.int32, (BLOCK, BLOCK), 1)
     zeros = jnp.zeros((BLOCK, BLOCK), jnp.float32)
@@ -99,10 +162,14 @@
     def at(ref, m, n):
         return ref.at[m * BLOCK : (m + 1) * BLOCK, n * BLOCK : (n + 1) * BLOCK]
 
-    for place, (m, n) in enumerate(lower_pairs(blocks)):
-        at(held_ref, m, n)[...] = packed_ref[:, place * BLOCK : (place + 1) * BLOCK]
-        if m > n:
-            at(held_ref, n, m)[...] = zeros
+    for core, source in enumerate((own_ref, other_ref)):
+        for step in range(len(SOURCES)):
+            first = source_col(place_ref, step, core) * share
+            for j in range(share):
+                m, n = pairs_ref[0, first + j], pairs_ref[1, first + j]
+                down = pl.ds(pl.multiple_of(m * BLOCK, BLOCK), BLOCK)
+                along = pl.ds(pl.multiple_of(n * BLOCK, BLOCK), BLOCK)
+                held_ref[down, along] = source[step, j]
 
     @pl.loop(0, blocks)
     def _(k):
@@ -124,7 +191,7 @@
             there = pl.ds(pl.multiple_of(j * BLOCK, BLOCK), BLOCK)
             held_ref[:, there] = held_ref[:, there] - times(held_ref[:, here], held_ref[there, here], ROWS_BY_ROWS)
 
-    for m, n in lower_pairs(blocks):
+    for m, n in [(m, n) for m in range(blocks) for n in range(m + 1)]:
         if m > n:
             at(lower_ref, m, n)[...] = at(held_ref, m, n)[...]
             at(lower_ref, n, m)[...] = zeros
@@ -135,25 +202,30 @@
             at(inverse_ref, m, m)[...] = at(held_ref, m, m)[...]
 
 
-def factor(packed, order):
+def factor(place, own, other, order):
     square = jax.ShapeDtypeStruct((order, order), jnp.float32)
+    pairs = [pair for dealt in dealt_pairs(order // BLOCK) for pair in dealt]
+    pairs = jnp.asarray([[m for m, _ in pairs], [n for _, n in pairs]], jnp.int32)
     return pl.pallas_call(
         factor_kernel,
         out_shape=(square, square),
-        in_specs=[WHOLE],
+        in_specs=[SCALARS, SCALARS, WHOLE, WHOLE],
         out_specs=(WHOLE, WHOLE),
         scratch_shapes=[pltpu.VMEM((order, order), jnp.float32), pltpu.VMEM((order, BLOCK), jnp.float32)],
         compiler_params=pltpu.CompilerParams(vmem_limit_bytes=40 * 2**20),
-        cost_estimate=pl.CostEstimate(flops=50 * 10**9, bytes_accessed=16 * 2**20, transcendentals=1024),
+        cost_estimate=pl.CostEstimate(flops=10**9, bytes_accessed=2**20, transcendentals=1024),
         name="factor",
-    )(packed)
-
-
-def solve_kernel(grid_rows, place_ref, rows_ref, lower_ref, inverse_ref, solved_ref, sides_ref):
+    )(place, pairs, own, other)
+
+
+def solve_kernel(grid_rows, place_ref, *refs):
+    *sources, lower_ref, inverse_ref, solved_ref, sides_ref, rows_ref = refs
     total, order = solved_ref.shape
     size = order // PANELS
     per = size // BLOCK
     my_row = place_ref[0]
+    for shift, source in enumerate(sources):
+        rows_ref[lax.rem(place_ref[1] - shift + len(sources), len(sources))] = source[...]
     inverse = [
         [parts_of(inverse_ref[j * size : (j + 1) * size, k * size : (k + 1) * size]) if k >= j else None for k in range(PANELS)]
         for j in range(PANELS)
@@ -179,16 +251,17 @@
 
 
 def solve(place, rows, lower, inverse, grid_rows):
-    out = jax.ShapeDtypeStruct((rows.shape[1], lower.shape[0]), jnp.float32)
+    out = jax.ShapeDtypeStruct((rows[0].shape[0], lower.shape[0]), jnp.float32)
     return pl.pallas_call(
         functools.partial(solve_kernel, grid_rows),
         out_shape=(out, out),
-        in_specs=[SCALARS, WHOLE, WHOLE, WHOLE],
+        in_specs=[SCALARS] + [WHOLE] * (len(rows) + 2),
         out_specs=(WHOLE, WHOLE),
+        scratch_shapes=[pltpu.VMEM((len(rows),) + rows[0].shape, jnp.float32)],
         compiler_params=pltpu.CompilerParams(vmem_limit_bytes=48 * 2**20),
         cost_estimate=pl.CostEstimate(flops=8 * 10**9, bytes_accessed=14 * 2**20, transcendentals=0),
         name="solve",
-    )(place, rows, lower, inverse)
+    )(place, *rows, lower, inverse)
 
 
 def finish_kernel(grid_rows, grid_cols, place_ref, tiles_ref, sides_ref, across_ref, solved_ref, boost_ref, out_ref):
@@ -284,48 +357,52 @@
     narrow = jnp.sum(
         jnp.where(first[:, None, None, :, :, None], arrived[:, :, :, :PANELS, None, :], 0.0), axis=3
     )
-    panel = jnp.where(kept[:, :, :, :PANELS, 0], entries[:, :, :, :PANELS, 0, :], 0.0)
-    panel = panel + jnp.einsum("niqa,nauke->iuqke", row_hits, narrow, precision=HIGHEST)
+    narrow = narrow.reshape(-1, order // BLOCK, BLOCK) * jnp.repeat(weight, child_tiles * slices)[:, None, None]
     within = jnp.arange(slices) * grid_rows * grid_cols + my_row * grid_cols + my_col
     boost = jnp.where(
         within[:, None, None, None] == jnp.arange(size),
-        jnp.where(jnp.eye(PANELS, dtype=bool)[:, :, None], diag_boost[0, :PANELS, None, :], 0.0),
+        jnp.where(jnp.eye(grid_rows, PANELS, dtype=bool)[:, :, None], diag_boost[0, :PANELS], 0.0),
         0.0,
     )
-    panel = panel.at[0, :, :PANELS].add(boost)
-
-    blocks = order // BLOCK
-    top = jnp.transpose(panel[0, :, :PANELS], (1, 0, 2, 3)).reshape(blocks, order)
-    packed = jnp.concatenate([top[m, : (m + 1) * BLOCK] for m in range(blocks)])
-    over_row = lax.all_gather(packed, "row", axis=0)
-
-    split = panel.reshape(local_rows, slices, halves, grid_cols, order)
-    split = jnp.transpose(split, (3, 0, 2, 1, 4)).reshape(grid_cols, local_cols * slices, 1, order)
-    for_cols = lax.all_to_all(split, "col", split_axis=0, concat_axis=2, tiled=True)
-    for_cols = for_cols.reshape(local_cols * slices, grid_cols, order)
-    lines = jnp.transpose(panel.reshape(local_rows, slices, grid_rows, grid_cols, BLOCK), (2, 3, 0, 1, 4))
-    lines = lines.reshape(grid_rows * grid_cols, local_rows * slices, BLOCK)
-    for_rows = lax.all_to_all(lines, ("row", "col"), split_axis=0, concat_axis=0, tiled=True)
-    for_rows = jnp.transpose(for_rows, (1, 0, 2)).reshape(local_rows * size, BLOCK)
+    boost = jnp.where((jnp.arange(local_rows) == 0)[:, None, None, None, None], boost, 0.0)
+    base = jnp.where(kept[:, :, :, :PANELS, 0], entries[:, :, :, :PANELS, 0, :], 0.0) + boost
+    lines, split = make_panel(index, base.reshape(-1, order // BLOCK, BLOCK), narrow, grid_rows)
+
+    split = lax.all_to_all(split, "col", split_axis=0, concat_axis=0, tiled=True)
+    for_cols = jnp.transpose(split, (1, 0, 2, 3)).reshape(local_cols * slices, grid_cols, order)
+
+    lines = lines.reshape(grid_rows * grid_cols, -1, 1, BLOCK)
+    lines, for_cols = lax.optimization_barrier((lines, for_cols))
+    across = lax.all_gather(for_cols, "row", axis=0)
+    lines = lax.all_to_all(lines, ("row", "col"), split_axis=0, concat_axis=0, tiled=True)
+    lines = jnp.transpose(lines.reshape(grid_rows * grid_cols, -1, BLOCK), (1, 0, 2))
+    for_rows, for_top = lines[: local_rows * slices].reshape(local_rows * size, BLOCK), lines[local_rows * slices :]
 
     spread = jnp.einsum("naube,ntpb->nautpe", arrived, col_hits, precision=HIGHEST)
     assembled = jnp.where(kept, entries, 0.0) + jnp.einsum("niqa,nautpe->iuqpte", row_hits, spread, precision=HIGHEST)
     joined = jnp.transpose(assembled, (2, 3, 0, 1, 4, 5))
     joined = joined.reshape(grid_rows * grid_cols, local_rows * slices, local_cols * size // BLOCK, BLOCK)
 
-    over_row, joined, for_cols = lax.optimization_barrier((over_row, joined, for_cols))
-    across = lax.all_gather(for_cols, "row", axis=0)
-    copies = jnp.broadcast_to(over_row[None], (grid_cols,) + over_row.shape)
-    over_both = lax.all_to_all(copies, "col", split_axis=0, concat_axis=0, tiled=True)
-    over_both = jnp.transpose(over_both, (1, 0, 2)).reshape(grid_rows * grid_cols, packed.shape[0])
-    copies = jnp.broadcast_to(for_rows[None], (grid_cols,) + for_rows.shape)
-    row_panel = lax.all_to_all(copies, "col", split_axis=0, concat_axis=0, tiled=True)
-    tiles = lax.all_to_all(joined, ("row", "col"), split_axis=0, concat_axis=0, tiled=True)
-    tiles = tiles.reshape(-1, BLOCK)
+    for_top, joined = lax.optimization_barrier((for_top, joined))
+    tiles = lax.all_to_all(joined, ("row", "col"), split_axis=0, concat_axis=0, tiled=True).reshape(-1, BLOCK)
+
+    def over_chips(value):
+        cols = range(grid_cols)
+        moved = [lax.ppermute(value, "col", [(c, (c + 2 * d) % grid_cols) for c in cols]) for d in SOURCES[1:]]
+        return jnp.stack([value] + moved)
+
+    def over_cores(value):
+        return lax.ppermute(value, "col", [(c, c ^ 1) for c in range(grid_cols)])
 
     place = jnp.stack([my_row, my_col]).astype(jnp.int32)
-    lower, inverse = factor(over_both, order)
-    solved, sides = solve(place, row_panel, lower, inverse, grid_rows)
+    own_top = over_chips(for_top)
+    own_top, for_rows = lax.optimization_barrier((own_top, for_rows))
+    rows = [for_rows]
+    for shift in range(1, grid_cols):
+        rows.append(lax.ppermute(for_rows, "col", [(c, (c + shift) % grid_cols) for c in range(grid_cols)]))
+    other_top = over_cores(own_top)
+    lower, inverse = factor(place, own_top, other_top, order)
+    solved, sides = solve(place, rows, lower, inverse, grid_rows)
     out = finish(place, tiles, sides, across, solved, diag_boost[0][:, None, :], grid_rows, grid_cols)
     return out.reshape(1, local_rows, 1, size, local_cols, 1, size)
 

time: 374 us -> 283 us (0.76)
  blocking collectives: 59.2 us -> 0 us
  waiting for transfers between devices: 92.3 us -> 56.5 us
  local copies, waits for them, and re-layouts: 49.7 us -> 30.3 us
  starting transfers between devices: 58.9 us -> 75 us
  other arithmetic: 2.94 us -> 8.44 us
    all_gather x1, waiting for transfers between devices: 57.4 us -> 15.4 us  [body(): across = lax.all_gather(for_cols, 'row', axis=0)]
    ppermute x0 -> x11, starting transfers between devices: none -> 31.3 us  [the longest x7 18 us: body(): lax.ppermute(for_rows, 'col', [(c, (c + shift) % grid_cols) for c in rang...]
    all_to_all x1 -> x0, blocking collectives: 30.5 us -> none  [body(): lax.all_to_all(copies, 'col', split_axis=0, concat_axis=0, tiled=True)]
    all_gather x1 -> x0, blocking collectives: 28.6 us -> none  [body(): over_row = lax.all_gather(packed, 'row', axis=0)]
    all_to_all x2 -> x1, waiting for transfers between devices: 29.1 us -> 4.4 us  [body(): lax.all_to_all(split, 'col', split_axis=0, concat_axis=0, tiled=True)]
    all_to_all x1, waiting for transfers between devices: 0.01 us -> 19.9 us  [body(): lax.all_to_all(lines, ('row', 'col'), split_axis=0, concat_axis=0, tiled=...]
    ppermute x0 -> x11, waiting for transfers between devices: none -> 14.4 us  [the longest x3 14.4 us: over_chips(): lax.ppermute(value, 'col', [(c, (c + 2 * d) % grid_cols) for c in cols])]
    unnamed x48 -> x32, local copies, waits for them, and re-layouts: 22.7 us -> 10.3 us
  transfers between devices with their start and end apart: 6 -> 16, of which waited for: 3 -> 7; matrix products, arithmetic and copies ran while one was open for 11% -> 9% of each run, Pallas kernels for 20% -> 26%
where the time goes in v3:
time: 283 us; the launch traced here: 277 us
  Pallas kernels  84 us (30%)
  starting transfers between devices  75 us (27%)
  waiting for transfers between devices  56.5 us (20%)
  local copies, waits for them, and re-layouts  30.3 us (11%)
  between operations  13.8 us (5%)
  matrix products  9.23 us (3%)
  other arithmetic  8.44 us (3%)
    pallas_call x1, Pallas kernels, factor(): pl.pallas_call(factor_kernel, out_shape=(square, square), in_specs=[SCALA...  62.9 us
    all_to_all x1, waiting for transfers between devices, body(): lax.all_to_all(lines, ('row', 'col'), split_axis=0, concat_axis=0, tiled=...  19.9 us
    all_to_all x1, starting transfers between devices, body(): lax.all_to_all(lines, ('row', 'col'), split_axis=0, concat_axis=0, tiled=...  18.5 us
    ppermute x7, starting transfers between devices, body(): lax.ppermute(for_rows, 'col', [(c, (c + shift) % grid_cols) for c in rang...  18 us
    all_gather x1, waiting for transfers between devices, body(): across = lax.all_gather(for_cols, 'row', axis=0)  15.4 us
    ppermute x3, waiting for transfers between devices, over_chips(): lax.ppermute(value, 'col', [(c, (c + 2 * d) % grid_cols) for c in cols])  14.4 us
    all_to_all x1, starting transfers between devices, body(): lax.all_to_all(split, 'col', split_axis=0, concat_axis=0, tiled=True)  11.2 us
    ppermute x3, starting transfers between devices, over_chips(): lax.ppermute(value, 'col', [(c, (c + 2 * d) % grid_cols) for c in cols])  10.3 us
  transfers between devices with their start and end apart: 16, of which 7 were waited for; matrix products, arithmetic and copies ran while one was open for 9% of the time, Pallas kernels for 26%

profile of v3, /device:TPU:1, one launch (start us, length us, event | category | flops | bytes accessed | tf_op | source)
XLA Modules:
  0.0 277.3 jit_solution(2972482750900324675)
XLA Ops:
  6.5 0.7 reshape.171
  7.3 1.4 copy.99
  8.6 0.1 copy.65
  8.8 1.0 select_reduce_fusion
  9.8 1.9 copy.66
  11.8 5.0 %all-to-all-start = ((f32[4,12,2,12,256]{4,2,3,1,0:T(2,128)}), f32[4,12,2,12,256]{4,2,3,1,0:T(2,128)S(1)}, u32[]{:S(2)}, u32[]{:S(2)}) async-start(f32[4,12,2,12,256]{4,2,3,1,0:T(2,128)} %copy.66), calls=%async_computation | async-start | bytes 2359296 | tf_op jit(solution)/shard_map/all_to_all | solution.py:344
  16.7 0.7 slice_bitcast_fusion
  17.7 0.8 broadcast_in_dim.181
  18.5 1.2 copy.97
  19.8 0.2 copy.63
  19.9 0.8 squeeze.9
  20.9 0.1 broadcast_in_dim.172
  20.9 0.1 eq.120
  21.0 0.1 copy.81
  21.2 0.1 broadcast_in_dim.168
  21.3 0.1 copy.61
  21.4 0.8 fusion.18
  22.3 0.8 select_reduce_fusion.2.index_ref
  23.2 2.0 select_add_fusion.base_ref
  25.2 2.3 all-to-all-done
  27.4 0.1 slice.30
  27.6 0.1 copy.67
  27.7 1.3 select_reduce_fusion.1
  29.0 1.9 reshape.174
  30.9 1.9 broadcast_multiply_fusion.narrow_ref
  32.8 2.4 panel.1
  35.2 11.2 %all-to-all-start.1 = ((f32[8,8,8,128]{3,2,1,0:T(8,128)}), f32[8,8,8,128]{3,2,1,0:T(8,128)S(1)}, u32[]{:S(2)}, u32[]{:S(2)}) async-start(f32[8,8,8,128]{3,2,1,0:T(8,128)} %get-tuple-element.18), calls=%async_computation.1 | async-start | bytes 524288 | tf_op jit(solution)/shard_map/all_to_all | solution.py:371
  46.5 2.1 reshape.175
  48.6 4.4 %all-to-all-done.1 = f32[8,8,8,128]{3,2,1,0:T(8,128)S(1)} async-done(((f32[8,8,8,128]{3,2,1,0:T(8,128)}), f32[8,8,8,128]{3,2,1,0:T(8,128)S(1)}, u32[]{:S(2)}, u32[]{:S(2)}) %all-to-all-start.1) | async-done | bytes 262176 | tf_op jit(solution)/shard_map/all_to_all | solution.py:371
  53.0 0.7 copy-done.6
  53.7 1.0 reshape.176
  54.7 2.7 copy.68
  57.3 18.5 %all-to-all-start.2 = ((f32[128,9,1,128]{3,2,1,0:T(1,128)}), f32[128,9,1,128]{3,2,1,0:T(1,128)}, u32[]{:S(2)}, u32[]{:S(2)}) async-start(f32[128,9,1,128]{3,2,1,0:T(1,128)} %copy.68), calls=%async_computation.2 | async-start | bytes 1179648 | tf_op jit(solution)/shard_map/all_to_all | solution.py:377
  75.8 0.8 copy.70
  76.8 2.3 convolution_bitcast_fusion
  79.1 7.0 %fusion.2 = f32[16,8,2,2,4,256]{5,0,2,1,4,3:T(8,128)S(1)} fusion(f32[4,12,2,4,8,256,1]{5,4,2,1,3,0,6:T(8,128)S(1)} %convolution_bitcast_fusion, pred[2,16,8,4]{1,0,2,3:T(4,128)(4,1)S(1)} %copy.70, f32[4]{0:T(128)S(1)} %copy-done.14, s32[2,16]{1,0:T(2,128)S(1)} %iota_add_fusion.1, s32[4,12]{1,0:T(4,128)S(1)} %copy-done.9, ...), kind=kOutput, calls=%fused_computation.4 | convolution fusion | flops 303041536 | bytes 7341392 | tf_op jit(solution)/shard_map/niqa,nautpe->iuqpte/dot_general | solution.py:382
  86.1 1.4 copy.73
  87.4 1.8 reshape.178
  89.3 19.9 %all-to-all-done.2 = f32[128,9,1,128]{3,2,1,0:T(1,128)} async-done(((f32[128,9,1,128]{3,2,1,0:T(1,128)}), f32[128,9,1,128]{3,2,1,0:T(1,128)}, u32[]{:S(2)}, u32[]{:S(2)}) %all-to-all-start.2) | async-done | bytes 589856 | tf_op jit(solution)/shard_map/all_to_all | solution.py:377
  109.2 1.1 copy.98
  110.3 9.0 %all-to-all-start.3 = ((f32[128,4,8,128]{3,2,1,0:T(8,128)}), f32[128,4,8,128]{3,2,1,0:T(8,128)S(1)}, u32[]{:S(2)}, u32[]{:S(2)}) async-start(f32[128,4,8,128]{3,2,1,0:T(8,128)} %reshape.178), calls=%async_computation.3 | async-start | bytes 4194304 | tf_op jit(solution)/shard_map/all_to_all | solution.py:387
  119.4 0.9 copy.74
  120.3 4.8 %collective-permute-start.2 = (f32[5,128,128]{2,1,0:T(8,128)S(1)}, f32[5,128,128]{2,1,0:T(8,128)S(1)}, u32[]{:S(2)}, u32[]{:S(2)}) collective-permute-start(f32[5,128,128]{2,1,0:T(8,128)S(1)} %slice.31), channel_id=1, source_target_pairs={{0,4},{1,5},{2,6},{3,7},{4,0},{5,1},{6,2},{7,3},{8,12},{9,13},{10,... | collective-permute-start | bytes 983048 | tf_op jit(solution)/shard_map/ppermute | solution.py:391
  125.1 2.8 %collective-permute-start.1 = (f32[5,128,128]{2,1,0:T(8,128)S(1)}, f32[5,128,128]{2,1,0:T(8,128)S(1)}, u32[]{:S(2)}, u32[]{:S(2)}) collective-permute-start(f32[5,128,128]{2,1,0:T(8,128)S(1)} %slice.31), channel_id=1, source_target_pairs={{0,6},{1,7},{2,0},{3,1},{4,2},{5,3},{6,4},{7,5},{8,14},{9,15},{10,... | collective-permute-start | bytes 983048 | tf_op jit(solution)/shard_map/ppermute | solution.py:391
  127.9 2.7 collective-permute-start
  130.7 3.9 %collective-permute-done.2 = f32[5,128,128]{2,1,0:T(8,128)S(1)} collective-permute-done((f32[5,128,128]{2,1,0:T(8,128)S(1)}, f32[5,128,128]{2,1,0:T(8,128)S(1)}, u32[]{:S(2)}, u32[]{:S(2)}) %collective-permute-start.2) | collective-permute-done | bytes 327712 | tf_op jit(solution)/shard_map/ppermute | solution.py:391
  134.5 10.5 %collective-permute-done.1 = f32[5,128,128]{2,1,0:T(8,128)S(1)} collective-permute-done((f32[5,128,128]{2,1,0:T(8,128)S(1)}, f32[5,128,128]{2,1,0:T(8,128)S(1)}, u32[]{:S(2)}, u32[]{:S(2)}) %collective-permute-start.1) | collective-permute-done | bytes 327712 | tf_op jit(solution)/shard_map/ppermute | solution.py:391
  145.0 0.1 pad_maximum_fusion.own_ref
  145.2 3.0 %collective-permute-start.10 = (f32[4,5,128,128]{3,2,1,0:T(8,128)S(1)}, f32[4,5,128,128]{3,2,1,0:T(8,128)S(1)}, u32[]{:S(2)}, u32[]{:S(2)}) collective-permute-start(f32[4,5,128,128]{3,2,1,0:T(8,128)S(1)} %pad_maximum_fusion.own_ref), channel_id=1, source_target_pairs={{0,1},{1,0},{2,3},{3,2},{4,5},{5,4},{6,7},{7,6},{8,9},{9,8},{10,11... | collective-permute-start | bytes 3932168 | tf_op jit(solution)/shard_map/ppermute | solution.py:395
  148.2 1.5 collective-permute-start.3
  149.6 2.1 collective-permute-start.4
  151.8 3.8 %collective-permute-start.5 = (f32[512,128]{1,0:T(8,128)S(1)}, f32[512,128]{1,0:T(8,128)S(1)}, u32[]{:S(2)}, u32[]{:S(2)}) collective-permute-start(f32[512,128]{1,0:T(8,128)S(1)} %bitcast.71), channel_id=1, source_target_pairs={{0,3},{1,4},{2,5},{3,6},{4,7},{5,0},{6,1},{7,2},{8,11},{9,12},{10,... | collective-permute-start | bytes 786440 | tf_op jit(solution)/shard_map/ppermute | solution.py:402
  155.6 3.4 %collective-permute-start.6 = (f32[512,128]{1,0:T(8,128)S(1)}, f32[512,128]{1,0:T(8,128)S(1)}, u32[]{:S(2)}, u32[]{:S(2)}) collective-permute-start(f32[512,128]{1,0:T(8,128)S(1)} %bitcast.72), channel_id=1, source_target_pairs={{0,4},{1,5},{2,6},{3,7},{4,0},{5,1},{6,2},{7,3},{8,12},{9,13},{10,... | collective-permute-start | bytes 786440 | tf_op jit(solution)/shard_map/ppermute | solution.py:402
  159.0 3.2 %collective-permute-start.7 = (f32[512,128]{1,0:T(8,128)S(1)}, f32[512,128]{1,0:T(8,128)S(1)}, u32[]{:S(2)}, u32[]{:S(2)}) collective-permute-start(f32[512,128]{1,0:T(8,128)S(1)} %bitcast.73), channel_id=1, source_target_pairs={{0,5},{1,6},{2,7},{3,0},{4,1},{5,2},{6,3},{7,4},{8,13},{9,14},{10,... | collective-permute-start | bytes 786440 | tf_op jit(solution)/shard_map/ppermute | solution.py:402
  162.3 3.0 %collective-permute-start.8 = (f32[512,128]{1,0:T(8,128)S(1)}, f32[512,128]{1,0:T(8,128)S(1)}, u32[]{:S(2)}, u32[]{:S(2)}) collective-permute-start(f32[512,128]{1,0:T(8,128)S(1)} %bitcast.74), channel_id=1, source_target_pairs={{0,6},{1,7},{2,0},{3,1},{4,2},{5,3},{6,4},{7,5},{8,14},{9,15},{10,... | collective-permute-start | bytes 786440 | tf_op jit(solution)/shard_map/ppermute | solution.py:402
  165.3 1.0 collective-permute-start.9
  166.4 62.9 %factor.1 = (f32[1024,1024]{1,0:T(8,128)S(1)}, f32[1024,1024]{1,0:T(8,128)S(1)}) custom-call(s32[2]{0:T(128)S(1)} %pad_add_fusion.place_ref, s32[2,40]{1,0:T(2,128)S(1)} %copy-done, f32[4,5,128,128]{3,2,1,0:T(8,128)S(1)} %pad_maximum_fusion.own_ref, f32[4,5,128,128]{3,2,1,0:T(8,128)S(1)} %collective-permute-done.10.other_ref), custom_call_target="tpu_custom_call" | custom-call | flops 1000000000 | bytes 1048576 | tf_op jit(solution)/shard_map/factor/pallas_call | solution.py:209
  229.4 2.0 copy-done.1
  231.4 2.0 copy-done.2
  233.4 10.3 %solve.1 = (f32[512,1024]{1,0:T(8,128)S(1)}, f32[512,1024]{1,0:T(8,128)}) custom-call(s32[2]{0:T(128)S(1)} %pad_add_fusion.place_ref, f32[512,128]{1,0:T(8,128)S(1)} %bitcast.76, f32[512,128]{1,0:T(8,128)S(1)} %collective-permute-done.3.refs_1_, f32[512,128]{1,0:T(8,128)S(1)} %collective-permute-done.4.refs_2_, ...), custom_call_target="tpu_custom_call" | custom-call | flops 8000000000 | bytes 14680064 | tf_op jit(solution)/shard_map/solve/pallas_call | solution.py:255
  243.7 1.4 copy-done.3
  245.0 15.4 %all-gather.3.cloned.1.call-done = f32[128,8,1024]{2,1,0:T(8,128)} async-done(((f32[8,8,1024]{2,1,0:T(8,128)}), f32[128,8,1024]{2,1,0:T(8,128)}) %all-gather.3.cloned.1.call-update) | async-done | bytes 4194320 | tf_op jit(solution)/shard_map/all_gather | solution.py:376
  260.5 1.6 copy-done.4
  262.1 8.4 %finish.1 = f32[4096,128]{1,0:T(8,128)} custom-call(s32[2]{0:T(128)S(1)} %pad_add_fusion.place_ref, f32[4096,128]{1,0:T(8,128)S(1)} %bitcast.68, f32[512,1024]{1,0:T(8,128)S(1)} %copy-done.4, f32[16,8,8,1024]{3,2,1,0:T(8,128)} %bitcast.92, f32[512,1024]{1,0:T(8,128)} %copy-done.3, f32[32,1,256]{2,1,0:T(1,128)S(1)} %broadcast_in_dim_squeeze.3.boost_ref), custom_call_target="tpu_custom_call" | custom-call | flops 4000000000 | bytes 12582912 | tf_op jit(solution)/shard_map/finish/pallas_call | solution.py:304
  (62 shorter events, 1.1 us)
Async XLA Ops:
  7.3 2.5 copy-start.12
  11.8 6.8 %copy-start.5 = (f32[1,2,2,1,1,16,8,4,256]{8,7,6,5,4,3,2,1,0:T(4,128)S(1)}, f32[1,2,2,1,1,16,8,4,256]{8,7,6,5,4,3,2,1,0:T(4,128)}, u32[]{:S(2)}) copy-start(f32[1,2,2,1,1,16,8,4,256]{8,7,6,5,4,3,2,1,0:T(4,128)} %param.7) | copy-start | bytes 6291460
  11.8 15.7 %all-to-all-start = ((f32[4,12,2,12,256]{4,2,3,1,0:T(2,128)}), f32[4,12,2,12,256]{4,2,3,1,0:T(2,128)S(1)}, u32[]{:S(2)}, u32[]{:S(2)}) async-start(f32[4,12,2,12,256]{4,2,3,1,0:T(2,128)} %copy.66), calls=%async_computation | async-start | bytes 2359296 | tf_op jit(solution)/shard_map/all_to_all | solution.py:344
  18.5 2.2 copy-start.11
  21.0 11.8 %copy-start.7 = (pred[2,16,4,8]{3,2,1,0:T(4,128)(4,1)}, pred[2,16,4,8]{3,2,1,0:T(4,128)(4,1)S(1)}, u32[]{:S(2)}) copy-start(pred[2,16,4,8]{3,2,1,0:T(4,128)(4,1)S(1)} %eq.120) | copy-start | bytes 3076
  22.2 0.9 copy-start.13
  23.1 9.7 %copy-start.8 = (s32[4,12]{1,0:T(4,128)}, s32[4,12]{1,0:T(4,128)S(1)}, u32[]{:S(2)}) copy-start(s32[4,12]{1,0:T(4,128)S(1)} %select_reduce_fusion.2.index_ref) | copy-start | bytes 580
  35.2 17.7 %all-to-all-start.1 = ((f32[8,8,8,128]{3,2,1,0:T(8,128)}), f32[8,8,8,128]{3,2,1,0:T(8,128)S(1)}, u32[]{:S(2)}, u32[]{:S(2)}) async-start(f32[8,8,8,128]{3,2,1,0:T(8,128)} %get-tuple-element.18), calls=%async_computation.1 | async-start | bytes 524288 | tf_op jit(solution)/shard_map/all_to_all | solution.py:371
  53.0 0.7 copy-start.6
  57.3 51.9 %all-to-all-start.2 = ((f32[128,9,1,128]{3,2,1,0:T(1,128)}), f32[128,9,1,128]{3,2,1,0:T(1,128)}, u32[]{:S(2)}, u32[]{:S(2)}) async-start(f32[128,9,1,128]{3,2,1,0:T(1,128)} %copy.68), calls=%async_computation.2 | async-start | bytes 1179648 | tf_op jit(solution)/shard_map/all_to_all | solution.py:377
  76.8 2.3 copy-start.9
  76.8 2.3 copy-start.14
  110.3 150.1 %all-to-all-start.3 = ((f32[128,4,8,128]{3,2,1,0:T(8,128)}), f32[128,4,8,128]{3,2,1,0:T(8,128)S(1)}, u32[]{:S(2)}, u32[]{:S(2)}) async-start(f32[128,4,8,128]{3,2,1,0:T(8,128)} %reshape.178), calls=%async_computation.3 | async-start | bytes 4194304 | tf_op jit(solution)/shard_map/all_to_all | solution.py:387
  119.4 46.9 %copy-start.10 = (f32[1,32,256]{2,1,0:T(8,128)S(1)}, f32[1,32,256]{2,1,0:T(8,128)}, u32[]{:S(2)}) copy-start(f32[1,32,256]{2,1,0:T(8,128)} %param.9) | copy-start | bytes 98308
  119.4 47.0 %copy-start = (s32[2,40]{1,0:T(2,128)S(1)}, s32[2,40]{1,0:T(2,128)}, u32[]{:S(2)}) copy-start(s32[2,40]{1,0:T(2,128)} %constant.39.clone.pairs_ref) | copy-start | bytes 964
  119.4 141.1 %all-gather.3.cloned.1.call-start = ((), (), s32[]{:S(2)}) async-start(), calls=%async_computation.4 | async-start | bytes 4456448 | tf_op jit(solution)/shard_map/all_gather | solution.py:376
  120.3 14.2 %collective-permute-start.2 = (f32[5,128,128]{2,1,0:T(8,128)S(1)}, f32[5,128,128]{2,1,0:T(8,128)S(1)}, u32[]{:S(2)}, u32[]{:S(2)}) collective-permute-start(f32[5,128,128]{2,1,0:T(8,128)S(1)} %slice.31), channel_id=1, source_target_pairs={{0,4},{1,5},{2,6},{3,7},{4,0},{5,1},{6,2},{7,3},{8,12},{9,13},{10,... | collective-permute-start | bytes 983048 | tf_op jit(solution)/shard_map/ppermute | solution.py:391
  125.1 19.9 %collective-permute-start.1 = (f32[5,128,128]{2,1,0:T(8,128)S(1)}, f32[5,128,128]{2,1,0:T(8,128)S(1)}, u32[]{:S(2)}, u32[]{:S(2)}) collective-permute-start(f32[5,128,128]{2,1,0:T(8,128)S(1)} %slice.31), channel_id=1, source_target_pairs={{0,6},{1,7},{2,0},{3,1},{4,2},{5,3},{6,4},{7,5},{8,14},{9,15},{10,... | collective-permute-start | bytes 983048 | tf_op jit(solution)/shard_map/ppermute | solution.py:391
  127.9 17.1 %collective-permute-start = (f32[5,128,128]{2,1,0:T(8,128)S(1)}, f32[5,128,128]{2,1,0:T(8,128)S(1)}, u32[]{:S(2)}, u32[]{:S(2)}) collective-permute-start(f32[5,128,128]{2,1,0:T(8,128)S(1)} %slice.31), channel_id=1, source_target_pairs={{0,2},{1,3},{2,4},{3,5},{4,6},{5,7},{6,0},{7,1},{8,10},{9,11},{10,... | collective-permute-start | bytes 983048 | tf_op jit(solution)/shard_map/ppermute | solution.py:391
  145.2 20.1 %collective-permute-start.10 = (f32[4,5,128,128]{3,2,1,0:T(8,128)S(1)}, f32[4,5,128,128]{3,2,1,0:T(8,128)S(1)}, u32[]{:S(2)}, u32[]{:S(2)}) collective-permute-start(f32[4,5,128,128]{3,2,1,0:T(8,128)S(1)} %pad_maximum_fusion.own_ref), channel_id=1, source_target_pairs={{0,1},{1,0},{2,3},{3,2},{4,5},{5,4},{6,7},{7,6},{8,9},{9,8},{10,11... | collective-permute-start | bytes 3932168 | tf_op jit(solution)/shard_map/ppermute | solution.py:395
  148.2 10.9 %collective-permute-start.3 = (f32[512,128]{1,0:T(8,128)S(1)}, f32[512,128]{1,0:T(8,128)S(1)}, u32[]{:S(2)}, u32[]{:S(2)}) collective-permute-start(f32[512,128]{1,0:T(8,128)S(1)} %bitcast.69), channel_id=1, source_target_pairs={{0,1},{1,2},{2,3},{3,4},{4,5},{5,6},{6,7},{7,0},{8,9},{9,10},{10,1... | collective-permute-start | bytes 786440 | tf_op jit(solution)/shard_map/ppermute | solution.py:402
  149.6 12.7 %collective-permute-start.4 = (f32[512,128]{1,0:T(8,128)S(1)}, f32[512,128]{1,0:T(8,128)S(1)}, u32[]{:S(2)}, u32[]{:S(2)}) collective-permute-start(f32[512,128]{1,0:T(8,128)S(1)} %bitcast.70), channel_id=1, source_target_pairs={{0,2},{1,3},{2,4},{3,5},{4,6},{5,7},{6,0},{7,1},{8,10},{9,11},{10,... | collective-permute-start | bytes 786440 | tf_op jit(solution)/shard_map/ppermute | solution.py:402
  151.8 81.6 %collective-permute-start.5 = (f32[512,128]{1,0:T(8,128)S(1)}, f32[512,128]{1,0:T(8,128)S(1)}, u32[]{:S(2)}, u32[]{:S(2)}) collective-permute-start(f32[512,128]{1,0:T(8,128)S(1)} %bitcast.71), channel_id=1, source_target_pairs={{0,3},{1,4},{2,5},{3,6},{4,7},{5,0},{6,1},{7,2},{8,11},{9,12},{10,... | collective-permute-start | bytes 786440 | tf_op jit(solution)/shard_map/ppermute | solution.py:402
  155.6 77.8 %collective-permute-start.6 = (f32[512,128]{1,0:T(8,128)S(1)}, f32[512,128]{1,0:T(8,128)S(1)}, u32[]{:S(2)}, u32[]{:S(2)}) collective-permute-start(f32[512,128]{1,0:T(8,128)S(1)} %bitcast.72), channel_id=1, source_target_pairs={{0,4},{1,5},{2,6},{3,7},{4,0},{5,1},{6,2},{7,3},{8,12},{9,13},{10,... | collective-permute-start | bytes 786440 | tf_op jit(solution)/shard_map/ppermute | solution.py:402
  159.0 74.3 %collective-permute-start.7 = (f32[512,128]{1,0:T(8,128)S(1)}, f32[512,128]{1,0:T(8,128)S(1)}, u32[]{:S(2)}, u32[]{:S(2)}) collective-permute-start(f32[512,128]{1,0:T(8,128)S(1)} %bitcast.73), channel_id=1, source_target_pairs={{0,5},{1,6},{2,7},{3,0},{4,1},{5,2},{6,3},{7,4},{8,13},{9,14},{10,... | collective-permute-start | bytes 786440 | tf_op jit(solution)/shard_map/ppermute | solution.py:402
  162.3 71.1 %collective-permute-start.8 = (f32[512,128]{1,0:T(8,128)S(1)}, f32[512,128]{1,0:T(8,128)S(1)}, u32[]{:S(2)}, u32[]{:S(2)}) collective-permute-start(f32[512,128]{1,0:T(8,128)S(1)} %bitcast.74), channel_id=1, source_target_pairs={{0,6},{1,7},{2,0},{3,1},{4,2},{5,3},{6,4},{7,5},{8,14},{9,15},{10,... | collective-permute-start | bytes 786440 | tf_op jit(solution)/shard_map/ppermute | solution.py:402
  165.3 68.1 %collective-permute-start.9 = (f32[512,128]{1,0:T(8,128)S(1)}, f32[512,128]{1,0:T(8,128)S(1)}, u32[]{:S(2)}, u32[]{:S(2)}) collective-permute-start(f32[512,128]{1,0:T(8,128)S(1)} %bitcast.75), channel_id=1, source_target_pairs={{0,7},{1,0},{2,1},{3,2},{4,3},{5,4},{6,5},{7,6},{8,15},{9,8},{10,9... | collective-permute-start | bytes 786440 | tf_op jit(solution)/shard_map/ppermute | solution.py:402
  229.4 2.0 copy-start.1
  231.4 2.0 copy-start.2
  243.7 1.4 copy-start.3
  260.5 1.6 copy-start.4
Sparse Core Ops, SparseCore 0:
  122.3 138.1 all-gather.2

commit v4 on v3

--- a/solution.py
+++ b/solution.py
@@ -100,24 +100,38 @@
     total, blocks, _ = base_ref.shape
     slices = narrow_ref.shape[0] // (groups * child_tiles)
     local_rows = total // (slices * grid_rows)
+    halves = blocks // PANELS
     dealt = dealt_pairs(blocks)
     share = len(dealt[0])
     per = local_rows * slices + share
     rows_ref[...] = base_ref[...]
+    tile_of = lax.broadcasted_iota(jnp.int32, (blocks, BLOCK), 0) // halves
     for g in range(groups):
+        moved = []
+        for shift in range(PANELS):
+            here = jnp.zeros((blocks, BLOCK), jnp.int32)
+            for k in range(shift, PANELS):
+                here = jnp.where(tile_of == k, (index_ref[g, k - shift] == k).astype(jnp.int32), here)
+            moved.append(here == 1)
         for a in range(child_tiles):
-            tile = index_ref[g, a]
+            tile = jnp.maximum(index_ref[g, a], 0)
             for u in range(slices):
                 at = (tile // grid_rows * slices + u) * grid_rows + lax.rem(tile, grid_rows)
-                rows_ref[at] = rows_ref[at] + narrow_ref[(g * child_tiles + a) * slices + u]
+                part = narrow_ref[(g * child_tiles + a) * slices + u]
+                added = jnp.where(moved[0], part, 0.0)
+                for shift in range(1, PANELS):
+                    added = added + jnp.where(moved[shift], pltpu.roll(part, shift * halves, 0), 0.0)
+                rows_ref[at] = rows_ref[at] + added
     for q in range(grid_rows):
         for line in range(local_rows * slices):
-            lines_ref[pl.ds(q * blocks * per + line, blocks, stride=per), :] = rows_ref[line * grid_rows + q]
+            value = rows_ref[line * grid_rows + q]
+            for p in range(blocks):
+                lines_ref[(q * blocks + p) * per + line] = value[p : p + 1, :]
     for p in range(blocks):
         for j, (m, n) in enumerate(dealt[p]):
             value = rows_ref[m % slices * grid_rows + m // slices][n : n + 1, :]
-            start = p * per + local_rows * slices + j
-            lines_ref[pl.ds(start, grid_rows, stride=blocks * per), :] = jnp.broadcast_to(value, (grid_rows, BLOCK))
+            for q in range(grid_rows):
+                lines_ref[(q * blocks + p) * per + local_rows * slices + j] = value
     halves = grid_rows // blocks
     for p in range(blocks):
         for i in range(local_rows):
@@ -132,7 +146,7 @@
     return pl.pallas_call(
         functools.partial(panel_kernel, grid_rows),
         out_shape=(
-            jax.ShapeDtypeStruct((grid_rows * blocks * per, BLOCK), jnp.float32),
+            jax.ShapeDtypeStruct((grid_rows * blocks * per, 1, BLOCK), jnp.float32),
             jax.ShapeDtypeStruct((blocks, total // blocks, blocks, BLOCK), jnp.float32),
         ),
         in_specs=[SCALARS, WHOLE, WHOLE],
@@ -152,80 +166,88 @@
     return chip * 2 + (mine if core == 0 else 1 - mine)
 
 
-def factor_kernel(place_ref, pairs_ref, own_ref, other_ref, lower_ref, inverse_ref, held_ref, diagonal_ref):
-    blocks = held_ref.shape[0] // BLOCK
+def factor_kernel(place_ref, pairs_ref, own_ref, other_ref, inverse_ref, mine_ref, diagonal_ref, before_ref):
+    order = inverse_ref.shape[0]
+    blocks = order // BLOCK
     share = own_ref.shape[1]
+    held_ref = inverse_ref
     row = lax.broadcasted_iota(jnp.int32, (BLOCK, BLOCK), 0)
     col = lax.broadcasted_iota(jnp.int32, (BLOCK, BLOCK), 1)
+    any_row = lax.broadcasted_iota(jnp.int32, (order, BLOCK), 0)
     zeros = jnp.zeros((BLOCK, BLOCK), jnp.float32)
-
-    def at(ref, m, n):
-        return ref.at[m * BLOCK : (m + 1) * BLOCK, n * BLOCK : (n + 1) * BLOCK]
-
+    wide = 2 * BLOCK
+
+    def span(k):
+        return pl.ds(pl.multiple_of(k * BLOCK, BLOCK), BLOCK)
+
+    held_ref[...] = jnp.zeros_like(held_ref)
+    before_ref[...] = jnp.zeros_like(before_ref)
     for core, source in enumerate((own_ref, other_ref)):
         for step in range(len(SOURCES)):
             first = source_col(place_ref, step, core) * share
             for j in range(share):
-                m, n = pairs_ref[0, first + j], pairs_ref[1, first + j]
-                down = pl.ds(pl.multiple_of(m * BLOCK, BLOCK), BLOCK)
-                along = pl.ds(pl.multiple_of(n * BLOCK, BLOCK), BLOCK)
-                held_ref[down, along] = source[step, j]
+                held_ref[span(pairs_ref[0, first + j]), span(pairs_ref[1, first + j])] = source[step, j]
 
     @pl.loop(0, blocks)
     def _(k):
-        here = pl.ds(pl.multiple_of(k * BLOCK, BLOCK), BLOCK)
+        here = span(k)
         block = held_ref[here, here]
         block = jnp.where(row >= col, block, 0.0) + jnp.where(col > row, jnp.where(row > col, block, 0.0).T, 0.0)
+        before = before_ref[...]
+        later = jnp.where(any_row >= (k + 1) * BLOCK, before, 0.0)
         upper, inverse = factor_block(block)
+        for start in range(0, order, wide):
+            held_ref[:, start : start + wide] = held_ref[:, start : start + wide] - times(
+                before, later[start : start + wide], ROWS_BY_ROWS
+            )
         diagonal_ref[here, :] = upper.T
 
         @pl.loop(k + 1, blocks)
         def _(j):
-            held_ref[here, pl.ds(pl.multiple_of(j * BLOCK, BLOCK), BLOCK)] = zeros
+            held_ref[here, span(j)] = zeros
 
         held_ref[here, here] = jnp.where(row == col, 1.0, 0.0).astype(jnp.float32)
-        held_ref[:, here] = times(held_ref[:, here], inverse, ROWS_BY_ROWS)
-
-        @pl.loop(k + 1, blocks)
-        def _(j):
-            there = pl.ds(pl.multiple_of(j * BLOCK, BLOCK), BLOCK)
-            held_ref[:, there] = held_ref[:, there] - times(held_ref[:, here], held_ref[there, here], ROWS_BY_ROWS)
-
-    for m, n in [(m, n) for m in range(blocks) for n in range(m + 1)]:
-        if m > n:
-            at(lower_ref, m, n)[...] = at(held_ref, m, n)[...]
-            at(lower_ref, n, m)[...] = zeros
-            at(inverse_ref, n, m)[...] = at(held_ref, n, m)[...]
-            at(inverse_ref, m, n)[...] = zeros
-        else:
-            at(lower_ref, m, m)[...] = diagonal_ref[m * BLOCK : (m + 1) * BLOCK, :]
-            at(inverse_ref, m, m)[...] = at(held_ref, m, m)[...]
+        column = times(held_ref[:, here], inverse, ROWS_BY_ROWS)
+        held_ref[:, here] = column
+        before_ref[...] = column
+
+        @pl.when(k + 1 < blocks)
+        def _():
+            held_ref[:, span(k + 1)] = held_ref[:, span(k + 1)] - times(column, before_ref[span(k + 1), :], ROWS_BY_ROWS)
+
+    per = blocks // PANELS
+    for h in range(per):
+        m = jnp.minimum(place_ref[0], PANELS - 1) * per + h
+        for n in range(blocks):
+            value = jnp.where(m == n, diagonal_ref[span(m), :], held_ref[span(m), n * BLOCK : (n + 1) * BLOCK])
+            mine_ref[h * BLOCK : (h + 1) * BLOCK, n * BLOCK : (n + 1) * BLOCK] = jnp.where(n > m, 0.0, value)
+    for n in range(blocks - 1):
+        held_ref[(n + 1) * BLOCK :, n * BLOCK : (n + 1) * BLOCK] = jnp.zeros((order - (n + 1) * BLOCK, BLOCK), jnp.float32)
 
 
 def factor(place, own, other, order):
-    square = jax.ShapeDtypeStruct((order, order), jnp.float32)
     pairs = [pair for dealt in dealt_pairs(order // BLOCK) for pair in dealt]
     pairs = jnp.asarray([[m for m, _ in pairs], [n for _, n in pairs]], jnp.int32)
     return pl.pallas_call(
         factor_kernel,
-        out_shape=(square, square),
+        out_shape=(
+            jax.ShapeDtypeStruct((order, order), jnp.float32),
+            jax.ShapeDtypeStruct((order // PANELS, order), jnp.float32),
+        ),
         in_specs=[SCALARS, SCALARS, WHOLE, WHOLE],
         out_specs=(WHOLE, WHOLE),
-        scratch_shapes=[pltpu.VMEM((order, order), jnp.float32), pltpu.VMEM((order, BLOCK), jnp.float32)],
+        scratch_shapes=[pltpu.VMEM((order, BLOCK), jnp.float32), pltpu.VMEM((order, BLOCK), jnp.float32)],
         compiler_params=pltpu.CompilerParams(vmem_limit_bytes=40 * 2**20),
-        cost_estimate=pl.CostEstimate(flops=10**9, bytes_accessed=2**20, transcendentals=1024),
+        cost_estimate=pl.CostEstimate(flops=10**6, bytes_accessed=2**10, transcendentals=0),
         name="factor",
     )(place, pairs, own, other)
 
 
-def solve_kernel(grid_rows, place_ref, *refs):
-    *sources, lower_ref, inverse_ref, solved_ref, sides_ref, rows_ref = refs
+def solve_kernel(grid_rows, place_ref, rows_ref, mine_ref, inverse_ref, solved_ref, sides_ref):
     total, order = solved_ref.shape
     size = order // PANELS
     per = size // BLOCK
     my_row = place_ref[0]
-    for shift, source in enumerate(sources):
-        rows_ref[lax.rem(place_ref[1] - shift + len(sources), len(sources))] = source[...]
     inverse = [
         [parts_of(inverse_ref[j * size : (j + 1) * size, k * size : (k + 1) * size]) if k >= j else None for k in range(PANELS)]
         for j in range(PANELS)
@@ -239,7 +261,7 @@
 
     @pl.when(my_row < PANELS)
     def _():
-        solved_ref[0:size, :] = lower_ref[pl.ds(pl.multiple_of(my_row * size, size), size), :]
+        solved_ref[0:size, :] = mine_ref[...]
 
     tile = lax.broadcasted_iota(jnp.int32, (total, size), 0) // size * grid_rows + my_row
     used = [parts_of(jnp.where(tile > k, solved_ref[:, k * size : (k + 1) * size], 0.0)) for k in range(PANELS)]
@@ -250,21 +272,20 @@
         sides_ref[:, j * size : (j + 1) * size] = total_j
 
 
-def solve(place, rows, lower, inverse, grid_rows):
-    out = jax.ShapeDtypeStruct((rows[0].shape[0], lower.shape[0]), jnp.float32)
+def solve(place, rows, mine, inverse, grid_rows):
+    out = jax.ShapeDtypeStruct((rows.shape[1], mine.shape[1]), jnp.float32)
     return pl.pallas_call(
         functools.partial(solve_kernel, grid_rows),
         out_shape=(out, out),
-        in_specs=[SCALARS] + [WHOLE] * (len(rows) + 2),
+        in_specs=[SCALARS, WHOLE, WHOLE, WHOLE],
         out_specs=(WHOLE, WHOLE),
-        scratch_shapes=[pltpu.VMEM((len(rows),) + rows[0].shape, jnp.float32)],
         compiler_params=pltpu.CompilerParams(vmem_limit_bytes=48 * 2**20),
-        cost_estimate=pl.CostEstimate(flops=8 * 10**9, bytes_accessed=14 * 2**20, transcendentals=0),
+        cost_estimate=pl.CostEstimate(flops=10**6, bytes_accessed=2**10, transcendentals=0),
         name="solve",
-    )(place, *rows, lower, inverse)
-
-
-def finish_kernel(grid_rows, grid_cols, place_ref, tiles_ref, sides_ref, across_ref, solved_ref, boost_ref, out_ref):
+    )(place, rows, mine, inverse)
+
+
+def finish_kernel(grid_rows, grid_cols, place_ref, tiles_ref, sides_ref, across_ref, last_ref, solved_ref, boost_ref, out_ref, line_ref):
     t = pl.program_id(0)
     my_row, my_col = place_ref[0], place_ref[1]
     size = boost_ref.shape[2]
@@ -273,8 +294,15 @@
     lines = tiles_ref.shape[0] // BLOCK
     per = lines // (local_rows * halves)
     order = sides_ref.shape[1]
-    across = jnp.concatenate([across_ref[:, u].reshape(BLOCK, order) for u in range(halves)], axis=0)
-    change = times_parts(parts_of(sides_ref[...]), parts_of(across), ROWS_BY_ROWS)
+    early = pl.num_programs(0) // 2
+    for source, taken in ((across_ref, t < early), (last_ref, t >= early)):
+
+        @pl.when(taken)
+        def _(source=source):
+            for u in range(halves):
+                line_ref[u * BLOCK : (u + 1) * BLOCK, :] = source[:, u].reshape(BLOCK, order)
+
+    change = times_parts(parts_of(sides_ref[...]), parts_of(line_ref[...]), ROWS_BY_ROWS)
     row = lax.broadcasted_iota(jnp.int32, (BLOCK, BLOCK), 0)
     col = lax.broadcasted_iota(jnp.int32, (BLOCK, BLOCK), 1)
     in_panel = jnp.logical_and(t == 0, my_col < PANELS)
@@ -293,10 +321,11 @@
                 out_ref[pl.ds(start * per + t * halves + h, BLOCK, stride=per), :] = value
 
 
-def finish(place, tiles, sides, across, solved, boost, grid_rows, grid_cols):
+def finish(place, tiles, sides, across, last, solved, boost, grid_rows, grid_cols):
     ranks, lines, cols, order = across.shape
     halves = boost.shape[2] // BLOCK
-    steps = lines // halves
+    early = lines // halves
+    steps = 2 * early
 
     def still(*shape):
         return pl.BlockSpec(shape, lambda t: (0,) * len(shape))
@@ -309,15 +338,17 @@
             SCALARS,
             still(*tiles.shape),
             still(*sides.shape),
-            pl.BlockSpec((ranks, halves, cols, order), lambda t: (0, t, 0, 0)),
+            pl.BlockSpec((ranks, halves, cols, order), lambda t: (0, jnp.minimum(t, early - 1), 0, 0)),
+            pl.BlockSpec((ranks, halves, cols, order), lambda t: (0, jnp.maximum(t - early, 0), 0, 0)),
             still(*solved.shape),
             still(*boost.shape),
         ],
         out_specs=still(*tiles.shape),
+        scratch_shapes=[pltpu.VMEM((boost.shape[2], order), jnp.float32)],
         compiler_params=pltpu.CompilerParams(vmem_limit_bytes=48 * 2**20),
         cost_estimate=pl.CostEstimate(flops=4 * 10**9, bytes_accessed=12 * 2**20, transcendentals=0),
         name="finish",
-    )(place, tiles, sides, across, solved, boost)
+    )(place, tiles, sides, across, last, solved, boost)
 
 
 def body(front_entries, child_updates, diag_boost, tile_mask, child_parent, child_index):
@@ -338,26 +369,25 @@
 
     pieces = child_updates.reshape(held, child_tiles, slices, child_tiles, size)
     parents = child_parent.reshape(groups, held)
-    mine = lax.dynamic_index_in_dim(parents, my_group, 0, keepdims=False)
-    goes = (mine[None, :] == jnp.arange(groups)[:, None])[:, :, None, None, None, None]
-    slots = jnp.sum(jnp.where(goes, pieces[None], 0.0), axis=1)
-    arrived = lax.all_to_all(slots, "front", split_axis=0, concat_axis=0, tiled=True)
     comes = parents == my_group
     index = jnp.sum(jnp.where(comes[:, :, None], child_index.reshape(groups, held, child_tiles), 0), axis=1)
-    weight = jnp.any(comes, axis=1).astype(jnp.float32)
+    index = jnp.where(jnp.any(comes, axis=1)[:, None], index, -1)
+    mine = lax.dynamic_index_in_dim(parents, my_group, 0, keepdims=False)
+    goes = (mine[None, :] == jnp.arange(groups)[:, None])[:, :, None, None, None]
+    blocks = order // BLOCK
+    narrow = pieces[:, :, :, :PANELS].reshape(held, child_tiles * slices, blocks, BLOCK)
+    narrow = jnp.sum(jnp.where(goes, narrow[None], 0.0), axis=1)
+    narrow = lax.all_to_all(narrow, "front", split_axis=0, concat_axis=0, tiled=True)
+    arrived = lax.all_gather(pieces, "front", axis=0)
+    arrived = jnp.sum(jnp.where(comes[:, :, None, None, None, None], arrived, 0.0), axis=1)
 
     entries = front_entries.reshape(local_rows, slices, grid_rows, grid_cols, local_cols, size)
     mask_tiles = jnp.transpose(tile_mask[0].reshape(local_rows, grid_rows, local_cols, grid_cols), (0, 1, 3, 2))
     kept = (mask_tiles == 1)[:, None, :, :, :, None]
     row_ids = jnp.arange(local_rows)[:, None] * grid_rows + jnp.arange(grid_rows)[None, :]
     col_ids = jnp.arange(local_cols)[:, None] * grid_cols + jnp.arange(grid_cols)[None, :]
-    row_hits = (index[:, None, None, :] == row_ids[None, :, :, None]).astype(jnp.float32) * weight[:, None, None, None]
+    row_hits = (index[:, None, None, :] == row_ids[None, :, :, None]).astype(jnp.float32)
     col_hits = (index[:, None, None, :] == col_ids[None, :, :, None]).astype(jnp.float32)
-    first = index[:, :PANELS, None] == jnp.arange(PANELS)
-    narrow = jnp.sum(
-        jnp.where(first[:, None, None, :, :, None], arrived[:, :, :, :PANELS, None, :], 0.0), axis=3
-    )
-    narrow = narrow.reshape(-1, order // BLOCK, BLOCK) * jnp.repeat(weight, child_tiles * slices)[:, None, None]
     within = jnp.arange(slices) * grid_rows * grid_cols + my_row * grid_cols + my_col
     boost = jnp.where(
         within[:, None, None, None] == jnp.arange(size),
@@ -366,14 +396,15 @@
     )
     boost = jnp.where((jnp.arange(local_rows) == 0)[:, None, None, None, None], boost, 0.0)
     base = jnp.where(kept[:, :, :, :PANELS, 0], entries[:, :, :, :PANELS, 0, :], 0.0) + boost
-    lines, split = make_panel(index, base.reshape(-1, order // BLOCK, BLOCK), narrow, grid_rows)
+    lines, split = make_panel(index, base.reshape(-1, blocks, BLOCK), narrow.reshape(-1, blocks, BLOCK), grid_rows)
 
     split = lax.all_to_all(split, "col", split_axis=0, concat_axis=0, tiled=True)
     for_cols = jnp.transpose(split, (1, 0, 2, 3)).reshape(local_cols * slices, grid_cols, order)
 
     lines = lines.reshape(grid_rows * grid_cols, -1, 1, BLOCK)
     lines, for_cols = lax.optimization_barrier((lines, for_cols))
-    across = lax.all_gather(for_cols, "row", axis=0)
+    part = local_cols * slices // 2
+    across = lax.all_gather(for_cols[:part], "row", axis=0)
     lines = lax.all_to_all(lines, ("row", "col"), split_axis=0, concat_axis=0, tiled=True)
     lines = jnp.transpose(lines.reshape(grid_rows * grid_cols, -1, BLOCK), (1, 0, 2))
     for_rows, for_top = lines[: local_rows * slices].reshape(local_rows * size, BLOCK), lines[local_rows * slices :]
@@ -383,7 +414,7 @@
     joined = jnp.transpose(assembled, (2, 3, 0, 1, 4, 5))
     joined = joined.reshape(grid_rows * grid_cols, local_rows * slices, local_cols * size // BLOCK, BLOCK)
 
-    for_top, joined = lax.optimization_barrier((for_top, joined))
+    joined, across, last = lax.optimization_barrier((joined, across, for_cols[part:]))
     tiles = lax.all_to_all(joined, ("row", "col"), split_axis=0, concat_axis=0, tiled=True).reshape(-1, BLOCK)
 
     def over_chips(value):
@@ -396,14 +427,12 @@
 
     place = jnp.stack([my_row, my_col]).astype(jnp.int32)
     own_top = over_chips(for_top)
-    own_top, for_rows = lax.optimization_barrier((own_top, for_rows))
-    rows = [for_rows]
-    for shift in range(1, grid_cols):
-        rows.append(lax.ppermute(for_rows, "col", [(c, (c + shift) % grid_cols) for c in range(grid_cols)]))
     other_top = over_cores(own_top)
-    lower, inverse = factor(place, own_top, other_top, order)
-    solved, sides = solve(place, rows, lower, inverse, grid_rows)
-    out = finish(place, tiles, sides, across, solved, diag_boost[0][:, None, :], grid_rows, grid_cols)
+    rows = lax.all_gather(for_rows, "col", axis=0)
+    last = lax.all_gather(last, "row", axis=0)
+    inverse, mine = factor(place, own_top, other_top, order)
+    solved, sides = solve(place, rows, mine, inverse, grid_rows)
+    out = finish(place, tiles, sides, across, last, solved, diag_boost[0][:, None, :], grid_rows, grid_cols)
     return out.reshape(1, local_rows, 1, size, local_cols, 1, size)
 
 

time: 283 us -> 304 us (1.074)
  the two profiles are of different devices: /device:TPU:1 before, /device:TPU:16 now
where the time goes in v4:
time: 304 us
  waiting for transfers between devices  125 us (41%)
  Pallas kernels  75.7 us (25%)
  starting transfers between devices  44.9 us (15%)
  local copies, waits for them, and re-layouts  17.1 us (6%)
  between operations  15.2 us (5%)
  blocking collectives  11.8 us (4%)
  other arithmetic  7.21 us (2%)
  matrix products  7.2 us (2%)
    all_gather x1, waiting for transfers between devices, body(): across = lax.all_gather(for_cols[:part], 'row', axis=0)  64.9 us
    pallas_call x1, Pallas kernels, factor(): pl.pallas_call(factor_kernel, out_shape=(jax.ShapeDtypeStruct((order, ord...  55.7 us
    all_gather x1, waiting for transfers between devices, body(): last = lax.all_gather(last, 'row', axis=0)  36.4 us
    all_to_all x1, starting transfers between devices, body(): lax.all_to_all(lines, ('row', 'col'), split_axis=0, concat_axis=0, tiled=...  17.6 us
    ppermute x3, waiting for transfers between devices, over_chips(): lax.ppermute(value, 'col', [(c, (c + 2 * d) % grid_cols) for c in cols])  16 us
    all_to_all x1, blocking collectives, body(): lax.all_to_all(split, 'col', split_axis=0, concat_axis=0, tiled=True)  11.8 us
    all_to_all x1, starting transfers between devices, body(): lax.all_to_all(joined, ('row', 'col'), split_axis=0, concat_axis=0, tiled...  11.1 us
    unnamed x29, local copies, waits for them, and re-layouts  10.7 us
  transfers between devices with their start and end apart: 11, of which 7 were waited for; matrix products, arithmetic and copies ran while one was open for 7% of the time, Pallas kernels for 22%

profile of v4, /device:TPU:16, one launch (start us, length us, event | category | flops | bytes accessed | tf_op | source)
XLA Modules:
  0.0 303.6 jit_solution(2634262321551267699)
XLA Ops:
  7.4 2.2 copy.79
  9.6 0.0 all-gather.10.cloned.1.call-update
  9.7 0.3 copy.116
  10.0 0.1 reshape.181
  10.1 0.1 copy.88
  10.2 0.1 broadcast_in_dim.187
  10.3 0.9 select_reduce_fusion.1
  11.2 4.3 %all-to-all-start = ((f32[4,24,8,128]{3,2,1,0:T(8,128)}), f32[4,24,8,128]{3,2,1,0:T(8,128)S(1)}, u32[]{:S(2)}, u32[]{:S(2)}) async-start(f32[4,24,8,128]{3,2,1,0:T(8,128)} %select_reduce_fusion.1), calls=%async_computation | async-start | bytes 786432 | tf_op jit(solution)/shard_map/all_to_all | solution.py:380
  15.5 0.1 fusion.14
  15.6 0.1 select_reduce_fusion.2
  15.7 0.1 iota_compare_fusion.2
  15.8 0.7 broadcast_select_fusion.2.index_ref
  16.5 0.1 broadcast_select_fusion.1
  16.6 0.1 broadcast_in_dim.185
  16.8 0.1 eq.105
  16.8 0.1 copy.102
  17.0 0.1 broadcast_in_dim.172
  17.1 0.1 copy.85
  17.2 1.2 copy.114
  18.4 0.2 copy.86
  18.6 0.1 squeeze.9
  18.7 0.1 broadcast_in_dim.175
  18.8 0.1 broadcast_in_dim.176
  18.9 0.9 select_add_fusion.base_ref
  19.8 3.7 %all-to-all-done = f32[4,24,8,128]{3,2,1,0:T(8,128)S(1)} async-done(((f32[4,24,8,128]{3,2,1,0:T(8,128)}), f32[4,24,8,128]{3,2,1,0:T(8,128)S(1)}, u32[]{:S(2)}, u32[]{:S(2)}) %all-to-all-start) | async-done | bytes 393248 | tf_op jit(solution)/shard_map/all_to_all | solution.py:380
  23.5 0.8 copy-done.7
  24.3 2.6 panel.1
  26.9 11.8 %all_to_all.20 = f32[8,8,8,128]{3,2,1,0:T(8,128)S(1)} all-to-all(f32[8,8,8,128]{3,2,1,0:T(8,128)} %get-tuple-element.17), channel_id=1, replica_groups=mesh['front'=4,'row'=16,'col'=8] {'col'}, dimensions={0} | all-to-all | bytes 524288 | tf_op jit(solution)/shard_map/all_to_all | solution.py:401
  38.8 0.2 copy.89
  38.9 0.7 fusion.15
  39.7 17.6 %all-to-all-start.3 = ((f32[128,9,1,128]{3,2,1,0:T(1,128)}), f32[128,9,1,128]{3,2,1,0:T(1,128)S(1)}, u32[]{:S(2)}, u32[]{:S(2)}) async-start(f32[128,9,1,128]{3,2,1,0:T(1,128)} %bitcast.24), calls=%async_computation.3 | async-start | bytes 1179648 | tf_op jit(solution)/shard_map/all_to_all | solution.py:408
  57.3 0.1 copy.77
  57.4 0.1 iota_add_fusion.1
  57.5 0.1 iota_add_fusion
  57.6 4.0 %select_reduce_fusion = f32[4,12,2,12,256]{4,2,3,1,0:T(2,128)S(1)} fusion(f32[4,2,12,2,12,256]{5,3,4,2,1,0:T(2,128)} %bitcast.77, pred[4,2]{1,0:T(4,128)(4,1)S(1)} %get-tuple-element.28), kind=kLoop, calls=%fused_computation.2 | loop fusion | flops 884736 | bytes 3538952 | tf_op jit(solution)/shard_map/reduce_sum | solution.py:382
  61.6 1.5 convolution_bitcast_fusion
  63.1 5.7 %fusion.2 = f32[16,8,2,2,4,256]{5,0,2,1,4,3:T(8,128)S(1)} fusion(f32[4,12,2,4,8,256,1]{5,4,2,1,3,0,6:T(8,128)S(1)} %convolution_bitcast_fusion, pred[2,16,8,4]{1,0,2,3:T(4,128)(4,1)S(1)} %copy.77, s32[2,16]{1,0:T(2,128)S(1)} %iota_add_fusion.1, s32[4,12]{1,0:T(4,128)S(1)} %copy-done.9, f32[1,2,2,1,1,16,8,4,256]{8,7,6,5,4,3,2,1,0:T(4,128)S(1)} %copy-done.5), kind=kOutput, calls=%fused_computation.4 | convolution fusion | flops 303040000 | bytes 7341376 | tf_op jit(solution)/shard_map/niqa,nautpe->iuqpte/dot_general | solution.py:413
  68.8 1.4 copy.82
  70.1 1.8 reshape.183
  72.0 64.9 %all-gather.12.cloned.1.call-done = f32[64,8,1024]{2,1,0:T(8,128)} async-done(((f32[4,8,1024]{2,1,0:T(8,128)}), f32[64,8,1024]{2,1,0:T(8,128)}) %all-gather.12.cloned.1.call-update) | async-done | bytes 2097168 | tf_op jit(solution)/shard_map/all_gather | solution.py:407
  136.9 11.1 %all-to-all-start.2 = ((f32[128,4,8,128]{3,2,1,0:T(8,128)}), f32[128,4,8,128]{3,2,1,0:T(8,128)S(1)}, u32[]{:S(2)}, u32[]{:S(2)}) async-start(f32[128,4,8,128]{3,2,1,0:T(8,128)} %reshape.183), calls=%async_computation.2 | async-start | bytes 4194304 | tf_op jit(solution)/shard_map/all_to_all | solution.py:418
  148.0 0.0 all-gather.8.cloned.1.call-start
  148.1 0.7 slice.37
  148.9 0.0 all-gather.8.cloned.1.call-update
  148.9 0.0 all-gather.14.cloned.1.call-start
  148.9 0.5 all-gather.14.cloned.1.call-update
  149.5 3.1 %collective-permute-start = (f32[5,128,128]{2,1,0:T(8,128)S(1)}, f32[5,128,128]{2,1,0:T(8,128)S(1)}, u32[]{:S(2)}, u32[]{:S(2)}) collective-permute-start(f32[5,128,128]{2,1,0:T(8,128)S(1)} %get-tuple-element.30), channel_id=1, source_target_pairs={{0,2},{1,3},{2,4},{3,5},{4,6},{5,7},{6,0},{7,1},{8,10},{9,11},{10,... | collective-permute-start | bytes 983048 | tf_op jit(solution)/shard_map/ppermute | solution.py:422
  152.6 2.8 collective-permute-start.1
  155.4 4.0 %collective-permute-start.2 = (f32[5,128,128]{2,1,0:T(8,128)S(1)}, f32[5,128,128]{2,1,0:T(8,128)S(1)}, u32[]{:S(2)}, u32[]{:S(2)}) collective-permute-start(f32[5,128,128]{2,1,0:T(8,128)S(1)} %get-tuple-element.30), channel_id=1, source_target_pairs={{0,4},{1,5},{2,6},{3,7},{4,0},{5,1},{6,2},{7,3},{8,12},{9,13},{10,... | collective-permute-start | bytes 983048 | tf_op jit(solution)/shard_map/ppermute | solution.py:422
  159.4 4.5 %collective-permute-done = f32[5,128,128]{2,1,0:T(8,128)S(1)} collective-permute-done((f32[5,128,128]{2,1,0:T(8,128)S(1)}, f32[5,128,128]{2,1,0:T(8,128)S(1)}, u32[]{:S(2)}, u32[]{:S(2)}) %collective-permute-start) | collective-permute-done | bytes 327712 | tf_op jit(solution)/shard_map/ppermute | solution.py:422
  163.9 3.7 %collective-permute-done.1 = f32[5,128,128]{2,1,0:T(8,128)S(1)} collective-permute-done((f32[5,128,128]{2,1,0:T(8,128)S(1)}, f32[5,128,128]{2,1,0:T(8,128)S(1)}, u32[]{:S(2)}, u32[]{:S(2)}) %collective-permute-start.1) | collective-permute-done | bytes 327712 | tf_op jit(solution)/shard_map/ppermute | solution.py:422
  167.6 7.8 %collective-permute-done.2 = f32[5,128,128]{2,1,0:T(8,128)S(1)} collective-permute-done((f32[5,128,128]{2,1,0:T(8,128)S(1)}, f32[5,128,128]{2,1,0:T(8,128)S(1)}, u32[]{:S(2)}, u32[]{:S(2)}) %collective-permute-start.2) | collective-permute-done | bytes 327712 | tf_op jit(solution)/shard_map/ppermute | solution.py:422
  175.4 0.1 pad_maximum_fusion.own_ref
  175.6 1.9 collective-permute-start.3
  177.5 0.1 pad_add_fusion.place_ref
  177.6 2.9 collective-permute-done.3.other_ref
  180.5 55.7 %factor.1 = (f32[1024,1024]{1,0:T(8,128)S(1)}, f32[256,1024]{1,0:T(8,128)S(1)}) custom-call(s32[2]{0:T(128)S(1)} %pad_add_fusion.place_ref, s32[2,40]{1,0:T(2,128)S(1)} %copy-done.1, f32[4,5,128,128]{3,2,1,0:T(8,128)S(1)} %pad_maximum_fusion.own_ref, f32[4,5,128,128]{3,2,1,0:T(8,128)S(1)} %collective-permute-done.3.other_ref), custom_call_target="tpu_custom_call" | custom-call | flops 1000000 | bytes 1024 | tf_op jit(solution)/shard_map/factor/pallas_call | solution.py:231
  236.2 1.9 copy-done
  238.1 8.4 %solve.1 = (f32[512,1024]{1,0:T(8,128)S(1)}, f32[512,1024]{1,0:T(8,128)S(1)}) custom-call(s32[2]{0:T(128)S(1)} %pad_add_fusion.place_ref, f32[8,512,128]{2,1,0:T(8,128)} %all-gather.8.cloned.1.call-done.rows_ref, f32[256,1024]{1,0:T(8,128)S(1)} %get-tuple-element.21.mine_ref, f32[1024,1024]{1,0:T(8,128)} %copy-done), custom_call_target="tpu_custom_call" | custom-call | flops 1000000 | bytes 1024 | tf_op jit(solution)/shard_map/solve/pallas_call | solution.py:277
  246.5 1.3 copy-done.2
  247.8 1.3 copy-done.3
  249.1 36.4 %all-gather.14.cloned.1.call-done = f32[64,8,1024]{2,1,0:T(8,128)} async-done(((f32[4,8,1024]{2,1,0:T(8,128)}), f32[64,8,1024]{2,1,0:T(8,128)}) %all-gather.14.cloned.1.call-update) | async-done | bytes 2097168 | tf_op jit(solution)/shard_map/all_gather | solution.py:432
  285.5 1.6 copy-done.4
  287.1 9.0 %finish.1 = f32[4096,128]{1,0:T(8,128)} custom-call(s32[2]{0:T(128)S(1)} %pad_add_fusion.place_ref, f32[4096,128]{1,0:T(8,128)S(1)} %bitcast.72, f32[512,1024]{1,0:T(8,128)S(1)} %copy-done.4, f32[16,4,8,1024]{3,2,1,0:T(8,128)} %bitcast.89, f32[16,4,8,1024]{3,2,1,0:T(8,128)} %bitcast.90, f32[512,1024]{1,0:T(8,128)} %copy-done.2, ...), custom_call_target="tpu_custom_call" | custom-call | flops 4000000000 | bytes 12582912 | tf_op jit(solution)/shard_map/finish/pallas_call | solution.py:333
  (46 shorter events, 0.4 us)
Async XLA Ops:
  7.4 2.3 copy-start.6
  7.4 2.6 copy-start.12
  7.4 50.2 %all-gather.10.cloned.1.call-start = ((), (), s32[]{:S(2)}) async-start(), calls=%async_computation.5 | async-start | bytes 2949120 | tf_op jit(solution)/shard_map/all_gather | solution.py:381
  9.6 6.0 %copy-start.11 = (s32[8,12]{1,0:T(8,128)S(1)}, s32[8,12]{1,0:T(8,128)}, u32[]{:S(2)}) copy-start(s32[8,12]{1,0:T(8,128)} %param.12) | copy-start | bytes 1156
  9.6 6.8 %copy-start.8 = (f32[1,32,256]{2,1,0:T(8,128)S(1)}, f32[1,32,256]{2,1,0:T(8,128)}, u32[]{:S(2)}) copy-start(f32[1,32,256]{2,1,0:T(8,128)} %param.9) | copy-start | bytes 98308
  9.6 6.8 %copy-start.10 = (s32[1,32,32]{2,1,0:T(8,128)S(1)}, s32[1,32,32]{2,1,0:T(8,128)}, u32[]{:S(2)}) copy-start(s32[1,32,32]{2,1,0:T(8,128)} %param.10) | copy-start | bytes 12292
  10.0 7.2 %copy-start.5 = (f32[1,2,2,1,1,16,8,4,256]{8,7,6,5,4,3,2,1,0:T(4,128)S(1)}, f32[1,2,2,1,1,16,8,4,256]{8,7,6,5,4,3,2,1,0:T(4,128)}, u32[]{:S(2)}) copy-start(f32[1,2,2,1,1,16,8,4,256]{8,7,6,5,4,3,2,1,0:T(4,128)} %param.7) | copy-start | bytes 6291460
  11.2 12.4 %all-to-all-start = ((f32[4,24,8,128]{3,2,1,0:T(8,128)}), f32[4,24,8,128]{3,2,1,0:T(8,128)S(1)}, u32[]{:S(2)}, u32[]{:S(2)}) async-start(f32[4,24,8,128]{3,2,1,0:T(8,128)} %select_reduce_fusion.1), calls=%async_computation | async-start | bytes 786432 | tf_op jit(solution)/shard_map/all_to_all | solution.py:380
  15.5 121.4 %all-gather.12.cloned.1.call-start = ((), (), s32[]{:S(2)}) async-start(), calls=%async_computation.6 | async-start | bytes 2228224 | tf_op jit(solution)/shard_map/all_gather | solution.py:407
  23.5 0.8 copy-start.7
  39.7 21.9 %copy-start.9 = (s32[4,12]{1,0:T(4,128)S(1)}, s32[4,12]{1,0:T(4,128)}, u32[]{:S(2)}) copy-start(s32[4,12]{1,0:T(4,128)} %broadcast_select_fusion.2.index_ref) | copy-start | bytes 580
  39.7 97.2 %all-to-all-start.3 = ((f32[128,9,1,128]{3,2,1,0:T(1,128)}), f32[128,9,1,128]{3,2,1,0:T(1,128)S(1)}, u32[]{:S(2)}, u32[]{:S(2)}) async-start(f32[128,9,1,128]{3,2,1,0:T(1,128)} %bitcast.24), calls=%async_computation.3 | async-start | bytes 1179648 | tf_op jit(solution)/shard_map/all_to_all | solution.py:408
  136.9 148.6 %all-to-all-start.2 = ((f32[128,4,8,128]{3,2,1,0:T(8,128)}), f32[128,4,8,128]{3,2,1,0:T(8,128)S(1)}, u32[]{:S(2)}, u32[]{:S(2)}) async-start(f32[128,4,8,128]{3,2,1,0:T(8,128)} %reshape.183), calls=%async_computation.2 | async-start | bytes 4194304 | tf_op jit(solution)/shard_map/all_to_all | solution.py:418
  148.0 90.1 %all-gather.8.cloned.1.call-start = ((), (), s32[]{:S(2)}) async-start(), calls=%async_computation.4 | async-start | bytes 2359296 | tf_op jit(solution)/shard_map/all_gather | solution.py:431
  148.9 31.6 %copy-start.1 = (s32[2,40]{1,0:T(2,128)S(1)}, s32[2,40]{1,0:T(2,128)}, u32[]{:S(2)}) copy-start(s32[2,40]{1,0:T(2,128)} %constant.40.clone.pairs_ref) | copy-start | bytes 964
  148.9 136.6 %all-gather.14.cloned.1.call-start = ((), (), s32[]{:S(2)}) async-start(), calls=%async_computation.7 | async-start | bytes 2228224 | tf_op jit(solution)/shard_map/all_gather | solution.py:432
  149.5 14.4 %collective-permute-start = (f32[5,128,128]{2,1,0:T(8,128)S(1)}, f32[5,128,128]{2,1,0:T(8,128)S(1)}, u32[]{:S(2)}, u32[]{:S(2)}) collective-permute-start(f32[5,128,128]{2,1,0:T(8,128)S(1)} %get-tuple-element.30), channel_id=1, source_target_pairs={{0,2},{1,3},{2,4},{3,5},{4,6},{5,7},{6,0},{7,1},{8,10},{9,11},{10,... | collective-permute-start | bytes 983048 | tf_op jit(solution)/shard_map/ppermute | solution.py:422
  152.6 15.0 %collective-permute-start.1 = (f32[5,128,128]{2,1,0:T(8,128)S(1)}, f32[5,128,128]{2,1,0:T(8,128)S(1)}, u32[]{:S(2)}, u32[]{:S(2)}) collective-permute-start(f32[5,128,128]{2,1,0:T(8,128)S(1)} %get-tuple-element.30), channel_id=1, source_target_pairs={{0,6},{1,7},{2,0},{3,1},{4,2},{5,3},{6,4},{7,5},{8,14},{9,15},{10,... | collective-permute-start | bytes 983048 | tf_op jit(solution)/shard_map/ppermute | solution.py:422
  155.4 20.1 %collective-permute-start.2 = (f32[5,128,128]{2,1,0:T(8,128)S(1)}, f32[5,128,128]{2,1,0:T(8,128)S(1)}, u32[]{:S(2)}, u32[]{:S(2)}) collective-permute-start(f32[5,128,128]{2,1,0:T(8,128)S(1)} %get-tuple-element.30), channel_id=1, source_target_pairs={{0,4},{1,5},{2,6},{3,7},{4,0},{5,1},{6,2},{7,3},{8,12},{9,13},{10,... | collective-permute-start | bytes 983048 | tf_op jit(solution)/shard_map/ppermute | solution.py:422
  175.6 4.9 %collective-permute-start.3 = (f32[4,5,128,128]{3,2,1,0:T(8,128)S(1)}, f32[4,5,128,128]{3,2,1,0:T(8,128)S(1)}, u32[]{:S(2)}, u32[]{:S(2)}) collective-permute-start(f32[4,5,128,128]{3,2,1,0:T(8,128)S(1)} %pad_maximum_fusion.own_ref), channel_id=1, source_target_pairs={{0,1},{1,0},{2,3},{3,2},{4,5},{5,4},{6,7},{7,6},{8,9},{9,8},{10,11... | collective-permute-start | bytes 3932168 | tf_op jit(solution)/shard_map/ppermute | solution.py:426
  236.2 2.0 copy-start
  246.5 1.3 copy-start.2
  247.8 1.3 copy-start.3
  285.5 1.6 copy-start.4
Sparse Core Ops, SparseCore 0:
  10.3 44.9 all-gather.9
  57.4 79.4 all-gather.11
Sparse Core Ops, SparseCore 1:
  150.7 37.3 all-gather.7
  189.9 95.5 all-gather.13

commit v5 on v4

--- a/solution.py
+++ b/solution.py
@@ -95,7 +95,7 @@
     return [pairs + [(0, blocks - 1)] * (share - len(pairs)) for pairs in dealt]
 
 
-def panel_kernel(grid_rows, index_ref, base_ref, narrow_ref, lines_ref, split_ref, rows_ref):
+def panel_kernel(grid_rows, index_ref, base_ref, narrow_ref, lines_ref, rows_ref):
     groups, child_tiles = index_ref.shape
     total, blocks, _ = base_ref.shape
     slices = narrow_ref.shape[0] // (groups * child_tiles)
@@ -103,7 +103,10 @@
     halves = blocks // PANELS
     dealt = dealt_pairs(blocks)
     share = len(dealt[0])
-    per = local_rows * slices + share
+    wide = share + local_rows * slices
+    bands = grid_rows // blocks
+    cuts = grid_rows // (bands * local_rows * slices)
+    per = wide + blocks // cuts
     rows_ref[...] = base_ref[...]
     tile_of = lax.broadcasted_iota(jnp.int32, (blocks, BLOCK), 0) // halves
     for g in range(groups):
@@ -132,25 +135,24 @@
             value = rows_ref[m % slices * grid_rows + m // slices][n : n + 1, :]
             for q in range(grid_rows):
                 lines_ref[(q * blocks + p) * per + local_rows * slices + j] = value
-    halves = grid_rows // blocks
-    for p in range(blocks):
-        for i in range(local_rows):
-            for h in range(halves):
-                for u in range(slices):
-                    split_ref[p, (i * halves + h) * slices + u] = rows_ref[(i * slices + u) * grid_rows + h * blocks + p]
+    for q in range(grid_rows):
+        line, cut = q // cuts, q % cuts
+        t, u = line // slices, line % slices
+        for p in range(blocks):
+            value = rows_ref[(t // bands * slices + u) * grid_rows + t % bands * blocks + p]
+            for n in range(blocks // cuts):
+                start = cut * (blocks // cuts) + n
+                lines_ref[(q * blocks + p) * per + wide + n] = value[start : start + 1, :]
 
 
 def make_panel(index, base, narrow, grid_rows):
     total, blocks, _ = base.shape
-    per = total // grid_rows + len(dealt_pairs(blocks)[0])
+    per = total // grid_rows + len(dealt_pairs(blocks)[0]) + blocks * (total // blocks) // grid_rows
     return pl.pallas_call(
         functools.partial(panel_kernel, grid_rows),
-        out_shape=(
-            jax.ShapeDtypeStruct((grid_rows * blocks * per, 1, BLOCK), jnp.float32),
-            jax.ShapeDtypeStruct((blocks, total // blocks, blocks, BLOCK), jnp.float32),
-        ),
+        out_shape=jax.ShapeDtypeStruct((grid_rows * blocks * per, 1, BLOCK), jnp.float32),
         in_specs=[SCALARS, WHOLE, WHOLE],
-        out_specs=(WHOLE, WHOLE),
+        out_specs=WHOLE,
         scratch_shapes=[pltpu.VMEM(base.shape, jnp.float32)],
         cost_estimate=pl.CostEstimate(flops=10**6, bytes_accessed=2 * 2**20, transcendentals=0),
         name="panel",
@@ -285,7 +287,7 @@
     )(place, rows, mine, inverse)
 
 
-def finish_kernel(grid_rows, grid_cols, place_ref, tiles_ref, sides_ref, across_ref, last_ref, solved_ref, boost_ref, out_ref, line_ref):
+def finish_kernel(grid_rows, grid_cols, place_ref, tiles_ref, sides_ref, across_ref, solved_ref, boost_ref, out_ref, line_ref):
     t = pl.program_id(0)
     my_row, my_col = place_ref[0], place_ref[1]
     size = boost_ref.shape[2]
@@ -293,15 +295,10 @@
     local_rows = sides_ref.shape[0] // size
     lines = tiles_ref.shape[0] // BLOCK
     per = lines // (local_rows * halves)
-    order = sides_ref.shape[1]
-    early = pl.num_programs(0) // 2
-    for source, taken in ((across_ref, t < early), (last_ref, t >= early)):
-
-        @pl.when(taken)
-        def _(source=source):
-            for u in range(halves):
-                line_ref[u * BLOCK : (u + 1) * BLOCK, :] = source[:, u].reshape(BLOCK, order)
-
+    cuts, width = across_ref.shape[0] // halves, across_ref.shape[1]
+    for u in range(halves):
+        for n in range(cuts * width):
+            line_ref[u * BLOCK : (u + 1) * BLOCK, n * BLOCK : (n + 1) * BLOCK] = across_ref[u * cuts + n // width, n % width]
     change = times_parts(parts_of(sides_ref[...]), parts_of(line_ref[...]), ROWS_BY_ROWS)
     row = lax.broadcasted_iota(jnp.int32, (BLOCK, BLOCK), 0)
     col = lax.broadcasted_iota(jnp.int32, (BLOCK, BLOCK), 1)
@@ -321,11 +318,9 @@
                 out_ref[pl.ds(start * per + t * halves + h, BLOCK, stride=per), :] = value
 
 
-def finish(place, tiles, sides, across, last, solved, boost, grid_rows, grid_cols):
-    ranks, lines, cols, order = across.shape
-    halves = boost.shape[2] // BLOCK
-    early = lines // halves
-    steps = 2 * early
+def finish(place, tiles, sides, across, solved, boost, grid_rows, grid_cols):
+    order = sides.shape[1]
+    steps = tiles.shape[0] // (sides.shape[0] * (boost.shape[2] // BLOCK))
 
     def still(*shape):
         return pl.BlockSpec(shape, lambda t: (0,) * len(shape))
@@ -338,8 +333,7 @@
             SCALARS,
             still(*tiles.shape),
             still(*sides.shape),
-            pl.BlockSpec((ranks, halves, cols, order), lambda t: (0, jnp.minimum(t, early - 1), 0, 0)),
-            pl.BlockSpec((ranks, halves, cols, order), lambda t: (0, jnp.maximum(t - early, 0), 0, 0)),
+            pl.BlockSpec((across.shape[0] // steps,) + across.shape[1:], lambda t: (t, 0, 0, 0)),
             still(*solved.shape),
             still(*boost.shape),
         ],
@@ -348,7 +342,7 @@
         compiler_params=pltpu.CompilerParams(vmem_limit_bytes=48 * 2**20),
         cost_estimate=pl.CostEstimate(flops=4 * 10**9, bytes_accessed=12 * 2**20, transcendentals=0),
         name="finish",
-    )(place, tiles, sides, across, last, solved, boost)
+    )(place, tiles, sides, across, solved, boost)
 
 
 def body(front_entries, child_updates, diag_boost, tile_mask, child_parent, child_index):
@@ -396,25 +390,21 @@
     )
     boost = jnp.where((jnp.arange(local_rows) == 0)[:, None, None, None, None], boost, 0.0)
     base = jnp.where(kept[:, :, :, :PANELS, 0], entries[:, :, :, :PANELS, 0, :], 0.0) + boost
-    lines, split = make_panel(index, base.reshape(-1, blocks, BLOCK), narrow.reshape(-1, blocks, BLOCK), grid_rows)
-
-    split = lax.all_to_all(split, "col", split_axis=0, concat_axis=0, tiled=True)
-    for_cols = jnp.transpose(split, (1, 0, 2, 3)).reshape(local_cols * slices, grid_cols, order)
+    lines = make_panel(index, base.reshape(-1, blocks, BLOCK), narrow.reshape(-1, blocks, BLOCK), grid_rows)
 
     lines = lines.reshape(grid_rows * grid_cols, -1, 1, BLOCK)
-    lines, for_cols = lax.optimization_barrier((lines, for_cols))
-    part = local_cols * slices // 2
-    across = lax.all_gather(for_cols[:part], "row", axis=0)
     lines = lax.all_to_all(lines, ("row", "col"), split_axis=0, concat_axis=0, tiled=True)
     lines = jnp.transpose(lines.reshape(grid_rows * grid_cols, -1, BLOCK), (1, 0, 2))
-    for_rows, for_top = lines[: local_rows * slices].reshape(local_rows * size, BLOCK), lines[local_rows * slices :]
+    wide = lines.shape[0] - local_cols * slices * blocks // grid_rows
+    across = lax.all_gather(lines[wide:], "row", axis=0)
+    for_rows, for_top = lines[: local_rows * slices].reshape(local_rows * size, BLOCK), lines[local_rows * slices : wide]
 
     spread = jnp.einsum("naube,ntpb->nautpe", arrived, col_hits, precision=HIGHEST)
     assembled = jnp.where(kept, entries, 0.0) + jnp.einsum("niqa,nautpe->iuqpte", row_hits, spread, precision=HIGHEST)
     joined = jnp.transpose(assembled, (2, 3, 0, 1, 4, 5))
     joined = joined.reshape(grid_rows * grid_cols, local_rows * slices, local_cols * size // BLOCK, BLOCK)
 
-    joined, across, last = lax.optimization_barrier((joined, across, for_cols[part:]))
+    for_top, joined = lax.optimization_barrier((for_top, joined))
     tiles = lax.all_to_all(joined, ("row", "col"), split_axis=0, concat_axis=0, tiled=True).reshape(-1, BLOCK)
 
     def over_chips(value):
@@ -429,10 +419,9 @@
     own_top = over_chips(for_top)
     other_top = over_cores(own_top)
     rows = lax.all_gather(for_rows, "col", axis=0)
-    last = lax.all_gather(last, "row", axis=0)
     inverse, mine = factor(place, own_top, other_top, order)
     solved, sides = solve(place, rows, mine, inverse, grid_rows)
-    out = finish(place, tiles, sides, across, last, solved, diag_boost[0][:, None, :], grid_rows, grid_cols)
+    out = finish(place, tiles, sides, across, solved, diag_boost[0][:, None, :], grid_rows, grid_cols)
     return out.reshape(1, local_rows, 1, size, local_cols, 1, size)
 
 

time: 304 us -> 284 us (0.934)
  the two profiles are of different devices: /device:TPU:16 before, /device:TPU:1 now
where the time goes in v5:
time: 284 us; the launch traced here: 279 us
  waiting for transfers between devices  102 us (36%)
  Pallas kernels  75.1 us (26%)
  starting transfers between devices  54 us (19%)
  local copies, waits for them, and re-layouts  18.9 us (7%)
  between operations  13.5 us (5%)
  other arithmetic  8.14 us (3%)
  matrix products  7.2 us (3%)
    pallas_call x1, Pallas kernels, factor(): pl.pallas_call(factor_kernel, out_shape=(jax.ShapeDtypeStruct((order, ord...  55.7 us
    all_to_all x1, waiting for transfers between devices, body(): lax.all_to_all(lines, ('row', 'col'), split_axis=0, concat_axis=0, tiled=...  42.2 us
    all_gather x1, waiting for transfers between devices, body(): across = lax.all_gather(lines[wide:], 'row', axis=0)  41.5 us
    all_to_all x1, starting transfers between devices, body(): lax.all_to_all(lines, ('row', 'col'), split_axis=0, concat_axis=0, tiled=...  22.3 us
    ppermute x3, waiting for transfers between devices, over_chips(): lax.ppermute(value, 'col', [(c, (c + 2 * d) % grid_cols) for c in cols])  14.8 us
    all_to_all x1, starting transfers between devices, body(): lax.all_to_all(joined, ('row', 'col'), split_axis=0, concat_axis=0, tiled...  13.6 us
    unnamed x27, local copies, waits for them, and re-layouts  10.8 us
    ppermute x3, starting transfers between devices, over_chips(): lax.ppermute(value, 'col', [(c, (c + 2 * d) % grid_cols) for c in cols])  10.1 us
  transfers between devices with their start and end apart: 10, of which 6 were waited for; matrix products, arithmetic and copies ran while one was open for 9% of the time, Pallas kernels for 23%

profile of v5, /device:TPU:1, one launch (start us, length us, event | category | flops | bytes accessed | tf_op | source)
XLA Modules:
  0.0 278.7 jit_solution(12199297891938559335)
XLA Ops:
  6.5 0.7 reshape.176
  7.3 1.4 copy.104
  8.7 0.0 copy-start.5
  8.7 0.1 copy.73
  8.8 0.1 broadcast_in_dim.183
  8.9 0.9 select_reduce_fusion.1
  9.7 4.8 %all-to-all-start = ((f32[4,24,8,128]{3,2,1,0:T(8,128)}), f32[4,24,8,128]{3,2,1,0:T(8,128)S(1)}, u32[]{:S(2)}, u32[]{:S(2)}) async-start(f32[4,24,8,128]{3,2,1,0:T(8,128)} %select_reduce_fusion.1), calls=%async_computation | async-start | bytes 786432 | tf_op jit(solution)/shard_map/all_to_all | solution.py:374
  14.6 0.1 fusion.14
  14.8 0.1 iota_compare_fusion.2
  14.8 0.1 select_reduce_fusion.2
  14.9 0.7 broadcast_select_fusion.2.index_ref
  15.6 0.1 broadcast_select_fusion.1
  15.8 0.1 broadcast_in_dim.181
  15.9 1.2 copy.102
  17.2 0.2 copy.71
  17.3 0.8 squeeze.9
  18.1 0.1 broadcast_in_dim.171
  18.2 0.1 broadcast_in_dim.172
  18.3 0.1 eq.107
  18.4 0.1 copy.86
  18.5 0.1 broadcast_in_dim.168
  18.6 0.1 copy.69
  18.7 1.9 select_add_fusion.base_ref
  20.6 0.2 all-to-all-done
  20.8 0.7 copy-done.7
  21.6 2.7 panel.1
  24.3 22.3 %all-to-all-start.1 = ((f32[128,13,1,128]{3,2,1,0:T(1,128)}), f32[128,13,1,128]{3,2,1,0:T(1,128)}, u32[]{:S(2)}, u32[]{:S(2)}) async-start(f32[128,13,1,128]{3,2,1,0:T(1,128)} %bitcast.69), calls=%async_computation.1 | async-start | bytes 1703936 | tf_op jit(solution)/shard_map/all_to_all | solution.py:396
  46.5 0.0 all-gather.8.cloned.1.call-start
  46.6 1.1 copy.76
  47.7 0.0 all-gather.8.cloned.1.call-update
  47.8 0.2 all-gather.6.cloned.1.call-start
  48.0 42.2 %all-to-all-done.1 = f32[128,13,1,128]{3,2,1,0:T(1,128)} async-done(((f32[128,13,1,128]{3,2,1,0:T(1,128)}), f32[128,13,1,128]{3,2,1,0:T(1,128)}, u32[]{:S(2)}, u32[]{:S(2)}) %all-to-all-start.1) | async-done | bytes 852000 | tf_op jit(solution)/shard_map/all_to_all | solution.py:396
  90.2 1.2 copy.103
  91.5 0.8 fusion.15
  92.3 0.0 all-gather.6.cloned.1.call-update
  92.3 0.1 copy.75
  92.5 0.1 iota_add_fusion.1
  92.5 0.1 iota_add_fusion
  92.6 4.0 %select_reduce_fusion = f32[4,12,2,12,256]{4,2,3,1,0:T(2,128)S(1)} fusion(f32[4,2,12,2,12,256]{5,3,4,2,1,0:T(2,128)} %bitcast.71, pred[4,2]{1,0:T(4,128)(4,1)S(1)} %get-tuple-element.18), kind=kLoop, calls=%fused_computation.2 | loop fusion | flops 884736 | bytes 3538952 | tf_op jit(solution)/shard_map/reduce_sum | solution.py:376
  96.6 1.5 convolution_bitcast_fusion
  98.1 5.7 %fusion.2 = f32[16,8,2,2,4,256]{5,0,2,1,4,3:T(8,128)S(1)} fusion(f32[4,12,2,4,8,256,1]{5,4,2,1,3,0,6:T(8,128)S(1)} %convolution_bitcast_fusion, pred[2,16,8,4]{1,0,2,3:T(4,128)(4,1)S(1)} %copy.75, s32[2,16]{1,0:T(2,128)S(1)} %iota_add_fusion.1, s32[4,12]{1,0:T(4,128)S(1)} %copy-done.9, f32[1,2,2,1,1,16,8,4,256]{8,7,6,5,4,3,2,1,0:T(4,128)S(1)} %copy-done.5), kind=kOutput, calls=%fused_computation.4 | convolution fusion | flops 303040000 | bytes 7341376 | tf_op jit(solution)/shard_map/niqa,nautpe->iuqpte/dot_general | solution.py:403
  103.8 1.4 copy.79
  105.2 1.8 reshape.183
  107.0 13.6 %all-to-all-start.2 = ((f32[128,4,8,128]{3,2,1,0:T(8,128)}), f32[128,4,8,128]{3,2,1,0:T(8,128)S(1)}, u32[]{:S(2)}, u32[]{:S(2)}) async-start(f32[128,4,8,128]{3,2,1,0:T(8,128)} %reshape.183), calls=%async_computation.2 | async-start | bytes 4194304 | tf_op jit(solution)/shard_map/all_to_all | solution.py:408
  120.6 0.0 copy-start.1
  120.6 0.0 all-gather.10.cloned.1.call-start
  120.7 0.7 all-gather.10.cloned.1.call-update
  121.4 4.8 %collective-permute-start.2 = (f32[5,128,128]{2,1,0:T(8,128)S(1)}, f32[5,128,128]{2,1,0:T(8,128)S(1)}, u32[]{:S(2)}, u32[]{:S(2)}) collective-permute-start(f32[5,128,128]{2,1,0:T(8,128)S(1)} %slice.31), channel_id=1, source_target_pairs={{0,4},{1,5},{2,6},{3,7},{4,0},{5,1},{6,2},{7,3},{8,12},{9,13},{10,... | collective-permute-start | bytes 983048 | tf_op jit(solution)/shard_map/ppermute | solution.py:412
  126.2 2.8 %collective-permute-start.1 = (f32[5,128,128]{2,1,0:T(8,128)S(1)}, f32[5,128,128]{2,1,0:T(8,128)S(1)}, u32[]{:S(2)}, u32[]{:S(2)}) collective-permute-start(f32[5,128,128]{2,1,0:T(8,128)S(1)} %slice.31), channel_id=1, source_target_pairs={{0,6},{1,7},{2,0},{3,1},{4,2},{5,3},{6,4},{7,5},{8,14},{9,15},{10,... | collective-permute-start | bytes 983048 | tf_op jit(solution)/shard_map/ppermute | solution.py:412
  129.0 2.5 collective-permute-start
  131.5 4.1 %collective-permute-done.2 = f32[5,128,128]{2,1,0:T(8,128)S(1)} collective-permute-done((f32[5,128,128]{2,1,0:T(8,128)S(1)}, f32[5,128,128]{2,1,0:T(8,128)S(1)}, u32[]{:S(2)}, u32[]{:S(2)}) %collective-permute-start.2) | collective-permute-done | bytes 327712 | tf_op jit(solution)/shard_map/ppermute | solution.py:412
  135.6 10.7 %collective-permute-done.1 = f32[5,128,128]{2,1,0:T(8,128)S(1)} collective-permute-done((f32[5,128,128]{2,1,0:T(8,128)S(1)}, f32[5,128,128]{2,1,0:T(8,128)S(1)}, u32[]{:S(2)}, u32[]{:S(2)}) %collective-permute-start.1) | collective-permute-done | bytes 327712 | tf_op jit(solution)/shard_map/ppermute | solution.py:412
  146.2 0.1 pad_maximum_fusion.own_ref
  146.3 3.0 %collective-permute-start.3 = (f32[4,5,128,128]{3,2,1,0:T(8,128)S(1)}, f32[4,5,128,128]{3,2,1,0:T(8,128)S(1)}, u32[]{:S(2)}, u32[]{:S(2)}) collective-permute-start(f32[4,5,128,128]{3,2,1,0:T(8,128)S(1)} %pad_maximum_fusion.own_ref), channel_id=1, source_target_pairs={{0,1},{1,0},{2,3},{3,2},{4,5},{5,4},{6,7},{7,6},{8,9},{9,8},{10,11... | collective-permute-start | bytes 3932168 | tf_op jit(solution)/shard_map/ppermute | solution.py:416
  149.3 0.1 pad_add_fusion.place_ref
  149.4 2.5 collective-permute-done.3.other_ref
  152.0 55.7 %factor.1 = (f32[1024,1024]{1,0:T(8,128)S(1)}, f32[256,1024]{1,0:T(8,128)S(1)}) custom-call(s32[2]{0:T(128)S(1)} %pad_add_fusion.place_ref, s32[2,40]{1,0:T(2,128)S(1)} %copy-done.1, f32[4,5,128,128]{3,2,1,0:T(8,128)S(1)} %pad_maximum_fusion.own_ref, f32[4,5,128,128]{3,2,1,0:T(8,128)S(1)} %collective-permute-done.3.other_ref), custom_call_target="tpu_custom_call" | custom-call | flops 1000000 | bytes 1024 | tf_op jit(solution)/shard_map/factor/pallas_call | solution.py:233
  207.6 2.0 copy-done
  209.6 8.4 %solve.1 = (f32[512,1024]{1,0:T(8,128)S(1)}, f32[512,1024]{1,0:T(8,128)S(1)}) custom-call(s32[2]{0:T(128)S(1)} %pad_add_fusion.place_ref, f32[8,512,128]{2,1,0:T(8,128)} %all-gather.6.cloned.1.call-done.rows_ref, f32[256,1024]{1,0:T(8,128)S(1)} %get-tuple-element.13.mine_ref, f32[1024,1024]{1,0:T(8,128)} %copy-done), custom_call_target="tpu_custom_call" | custom-call | flops 1000000 | bytes 1024 | tf_op jit(solution)/shard_map/solve/pallas_call | solution.py:279
  218.0 1.3 copy-done.2
  219.3 1.4 copy-done.3
  220.7 41.5 %all-gather.10.cloned.1.call-done = f32[64,128,128]{2,1,0:T(8,128)} async-done(((f32[4,128,128]{2,1,0:T(8,128)}), f32[64,128,128]{2,1,0:T(8,128)}) %all-gather.10.cloned.1.call-update) | async-done | bytes 4194320 | tf_op jit(solution)/shard_map/all_gather | solution.py:399
  262.2 1.6 copy-done.4
  263.8 8.4 %finish.1 = f32[4096,128]{1,0:T(8,128)} custom-call(s32[2]{0:T(128)S(1)} %pad_add_fusion.place_ref, f32[4096,128]{1,0:T(8,128)S(1)} %bitcast.65, f32[512,1024]{1,0:T(8,128)S(1)} %copy-done.4, f32[16,4,128,128]{3,2,1,0:T(8,128)} %bitcast.83, f32[512,1024]{1,0:T(8,128)} %copy-done.2, f32[32,1,256]{2,1,0:T(1,128)S(1)} %broadcast_in_dim_squeeze.3.boost_ref), custom_call_target="tpu_custom_call" | custom-call | flops 4000000000 | bytes 12582912 | tf_op jit(solution)/shard_map/finish/pallas_call | solution.py:328
  (37 shorter events, 0.3 us)
Async XLA Ops:
  6.5 8.2 %copy-start.8 = (f32[1,32,256]{2,1,0:T(8,128)S(1)}, f32[1,32,256]{2,1,0:T(8,128)}, u32[]{:S(2)}) copy-start(f32[1,32,256]{2,1,0:T(8,128)} %param.9) | copy-start | bytes 98308
  6.5 8.3 %copy-start.10 = (s32[1,32,32]{2,1,0:T(8,128)S(1)}, s32[1,32,32]{2,1,0:T(8,128)}, u32[]{:S(2)}) copy-start(s32[1,32,32]{2,1,0:T(8,128)} %param.10) | copy-start | bytes 12292
  6.5 8.3 %copy-start.11 = (s32[8,12]{1,0:T(8,128)S(1)}, s32[8,12]{1,0:T(8,128)}, u32[]{:S(2)}) copy-start(s32[8,12]{1,0:T(8,128)} %param.12) | copy-start | bytes 1156
  8.7 7.2 %copy-start.5 = (f32[1,2,2,1,1,16,8,4,256]{8,7,6,5,4,3,2,1,0:T(4,128)S(1)}, f32[1,2,2,1,1,16,8,4,256]{8,7,6,5,4,3,2,1,0:T(4,128)}, u32[]{:S(2)}) copy-start(f32[1,2,2,1,1,16,8,4,256]{8,7,6,5,4,3,2,1,0:T(4,128)} %param.7) | copy-start | bytes 6291460
  9.7 11.1 %all-to-all-start = ((f32[4,24,8,128]{3,2,1,0:T(8,128)}), f32[4,24,8,128]{3,2,1,0:T(8,128)S(1)}, u32[]{:S(2)}, u32[]{:S(2)}) async-start(f32[4,24,8,128]{3,2,1,0:T(8,128)} %select_reduce_fusion.1), calls=%async_computation | async-start | bytes 786432 | tf_op jit(solution)/shard_map/all_to_all | solution.py:374
  18.1 28.4 %copy-start.6 = (f32[2,12,2,1,1,12,256]{6,4,5,3,2,1,0:T(1,128)S(1)}, f32[2,12,2,1,1,12,256]{6,4,5,3,2,1,0:T(1,128)}, u32[]{:S(2)}) copy-start(f32[2,12,2,1,1,12,256]{6,4,5,3,2,1,0:T(1,128)} %param.8) | copy-start | bytes 1769476
  20.8 0.7 copy-start.7
  24.3 65.9 %all-to-all-start.1 = ((f32[128,13,1,128]{3,2,1,0:T(1,128)}), f32[128,13,1,128]{3,2,1,0:T(1,128)}, u32[]{:S(2)}, u32[]{:S(2)}) async-start(f32[128,13,1,128]{3,2,1,0:T(1,128)} %bitcast.69), calls=%async_computation.1 | async-start | bytes 1703936 | tf_op jit(solution)/shard_map/all_to_all | solution.py:396
  46.5 46.1 %all-gather.8.cloned.1.call-start = ((), (), s32[]{:S(2)}) async-start(), calls=%async_computation.4 | async-start | bytes 2949120 | tf_op jit(solution)/shard_map/all_gather | solution.py:375
  47.8 161.9 %all-gather.6.cloned.1.call-start = ((), (), s32[]{:S(2)}) async-start(), calls=%async_computation.3 | async-start | bytes 2359296 | tf_op jit(solution)/shard_map/all_gather | solution.py:421
  92.3 4.3 %copy-start.9 = (s32[4,12]{1,0:T(4,128)S(1)}, s32[4,12]{1,0:T(4,128)}, u32[]{:S(2)}) copy-start(s32[4,12]{1,0:T(4,128)} %broadcast_select_fusion.2.index_ref) | copy-start | bytes 580
  107.0 155.2 %all-to-all-start.2 = ((f32[128,4,8,128]{3,2,1,0:T(8,128)}), f32[128,4,8,128]{3,2,1,0:T(8,128)S(1)}, u32[]{:S(2)}, u32[]{:S(2)}) async-start(f32[128,4,8,128]{3,2,1,0:T(8,128)} %reshape.183), calls=%async_computation.2 | async-start | bytes 4194304 | tf_op jit(solution)/shard_map/all_to_all | solution.py:408
  120.6 31.3 %copy-start.1 = (s32[2,40]{1,0:T(2,128)S(1)}, s32[2,40]{1,0:T(2,128)}, u32[]{:S(2)}) copy-start(s32[2,40]{1,0:T(2,128)} %constant.40.clone.pairs_ref) | copy-start | bytes 964
  120.6 141.6 %all-gather.10.cloned.1.call-start = ((), (), s32[]{:S(2)}) async-start(), calls=%async_computation.5 | async-start | bytes 4456448 | tf_op jit(solution)/shard_map/all_gather | solution.py:399
  121.4 14.2 %collective-permute-start.2 = (f32[5,128,128]{2,1,0:T(8,128)S(1)}, f32[5,128,128]{2,1,0:T(8,128)S(1)}, u32[]{:S(2)}, u32[]{:S(2)}) collective-permute-start(f32[5,128,128]{2,1,0:T(8,128)S(1)} %slice.31), channel_id=1, source_target_pairs={{0,4},{1,5},{2,6},{3,7},{4,0},{5,1},{6,2},{7,3},{8,12},{9,13},{10,... | collective-permute-start | bytes 983048 | tf_op jit(solution)/shard_map/ppermute | solution.py:412
  126.2 20.1 %collective-permute-start.1 = (f32[5,128,128]{2,1,0:T(8,128)S(1)}, f32[5,128,128]{2,1,0:T(8,128)S(1)}, u32[]{:S(2)}, u32[]{:S(2)}) collective-permute-start(f32[5,128,128]{2,1,0:T(8,128)S(1)} %slice.31), channel_id=1, source_target_pairs={{0,6},{1,7},{2,0},{3,1},{4,2},{5,3},{6,4},{7,5},{8,14},{9,15},{10,... | collective-permute-start | bytes 983048 | tf_op jit(solution)/shard_map/ppermute | solution.py:412
  129.0 17.3 %collective-permute-start = (f32[5,128,128]{2,1,0:T(8,128)S(1)}, f32[5,128,128]{2,1,0:T(8,128)S(1)}, u32[]{:S(2)}, u32[]{:S(2)}) collective-permute-start(f32[5,128,128]{2,1,0:T(8,128)S(1)} %slice.31), channel_id=1, source_target_pairs={{0,2},{1,3},{2,4},{3,5},{4,6},{5,7},{6,0},{7,1},{8,10},{9,11},{10,... | collective-permute-start | bytes 983048 | tf_op jit(solution)/shard_map/ppermute | solution.py:412
  146.3 5.6 %collective-permute-start.3 = (f32[4,5,128,128]{3,2,1,0:T(8,128)S(1)}, f32[4,5,128,128]{3,2,1,0:T(8,128)S(1)}, u32[]{:S(2)}, u32[]{:S(2)}) collective-permute-start(f32[4,5,128,128]{3,2,1,0:T(8,128)S(1)} %pad_maximum_fusion.own_ref), channel_id=1, source_target_pairs={{0,1},{1,0},{2,3},{3,2},{4,5},{5,4},{6,7},{7,6},{8,9},{9,8},{10,11... | collective-permute-start | bytes 3932168 | tf_op jit(solution)/shard_map/ppermute | solution.py:416
  207.6 2.0 copy-start
  218.0 1.3 copy-start.2
  219.3 1.4 copy-start.3
  262.2 1.6 copy-start.4
Sparse Core Ops, SparseCore 0:
  49.5 39.9 all-gather.7
  92.4 32.6 all-gather.5
  127.2 134.9 all-gather.9

commit v6 on v4

--- a/solution.py
+++ b/solution.py
@@ -117,7 +117,7 @@
             tile = jnp.maximum(index_ref[g, a], 0)
             for u in range(slices):
                 at = (tile // grid_rows * slices + u) * grid_rows + lax.rem(tile, grid_rows)
-                part = narrow_ref[(g * child_tiles + a) * slices + u]
+                part = narrow_ref[(g * child_tiles + a) * slices + u][:blocks]
                 added = jnp.where(moved[0], part, 0.0)
                 for shift in range(1, PANELS):
                     added = added + jnp.where(moved[shift], pltpu.roll(part, shift * halves, 0), 0.0)
@@ -169,7 +169,8 @@
 def factor_kernel(place_ref, pairs_ref, own_ref, other_ref, inverse_ref, mine_ref, diagonal_ref, before_ref):
     order = inverse_ref.shape[0]
     blocks = order // BLOCK
-    share = own_ref.shape[1]
+    dealt = pairs_ref.shape[1] // blocks
+    skipped = own_ref.shape[1] - dealt
     held_ref = inverse_ref
     row = lax.broadcasted_iota(jnp.int32, (BLOCK, BLOCK), 0)
     col = lax.broadcasted_iota(jnp.int32, (BLOCK, BLOCK), 1)
@@ -184,9 +185,9 @@
     before_ref[...] = jnp.zeros_like(before_ref)
     for core, source in enumerate((own_ref, other_ref)):
         for step in range(len(SOURCES)):
-            first = source_col(place_ref, step, core) * share
-            for j in range(share):
-                held_ref[span(pairs_ref[0, first + j]), span(pairs_ref[1, first + j])] = source[step, j]
+            first = source_col(place_ref, step, core) * dealt
+            for j in range(dealt):
+                held_ref[span(pairs_ref[0, first + j]), span(pairs_ref[1, first + j])] = source[step, skipped + j]
 
     @pl.loop(0, blocks)
     def _(k):
@@ -243,11 +244,16 @@
     )(place, pairs, own, other)
 
 
-def solve_kernel(grid_rows, place_ref, rows_ref, mine_ref, inverse_ref, solved_ref, sides_ref):
+def solve_kernel(grid_rows, place_ref, own_ref, other_ref, mine_ref, inverse_ref, solved_ref, sides_ref, rows_ref):
     total, order = solved_ref.shape
     size = order // PANELS
     per = size // BLOCK
     my_row = place_ref[0]
+    for core, source in enumerate((own_ref, other_ref)):
+        for step in range(len(SOURCES)):
+            col = source_col(place_ref, step, core)
+            for line in range(total // BLOCK):
+                rows_ref[col, line * BLOCK : (line + 1) * BLOCK, :] = source[step, line]
     inverse = [
         [parts_of(inverse_ref[j * size : (j + 1) * size, k * size : (k + 1) * size]) if k >= j else None for k in range(PANELS)]
         for j in range(PANELS)
@@ -272,20 +278,22 @@
         sides_ref[:, j * size : (j + 1) * size] = total_j
 
 
-def solve(place, rows, mine, inverse, grid_rows):
-    out = jax.ShapeDtypeStruct((rows.shape[1], mine.shape[1]), jnp.float32)
+def solve(place, own, other, mine, inverse, grid_rows, local_rows):
+    total, order = local_rows * mine.shape[0], mine.shape[1]
+    out = jax.ShapeDtypeStruct((total, order), jnp.float32)
     return pl.pallas_call(
         functools.partial(solve_kernel, grid_rows),
         out_shape=(out, out),
-        in_specs=[SCALARS, WHOLE, WHOLE, WHOLE],
+        in_specs=[SCALARS, WHOLE, WHOLE, WHOLE, WHOLE],
         out_specs=(WHOLE, WHOLE),
+        scratch_shapes=[pltpu.VMEM((order // BLOCK, total, BLOCK), jnp.float32)],
         compiler_params=pltpu.CompilerParams(vmem_limit_bytes=48 * 2**20),
         cost_estimate=pl.CostEstimate(flops=10**6, bytes_accessed=2**10, transcendentals=0),
         name="solve",
-    )(place, rows, mine, inverse)
-
-
-def finish_kernel(grid_rows, grid_cols, place_ref, tiles_ref, sides_ref, across_ref, last_ref, solved_ref, boost_ref, out_ref, line_ref):
+    )(place, own, other, mine, inverse)
+
+
+def finish_kernel(grid_rows, grid_cols, place_ref, tiles_ref, sides_ref, across_ref, solved_ref, boost_ref, out_ref, line_ref):
     t = pl.program_id(0)
     my_row, my_col = place_ref[0], place_ref[1]
     size = boost_ref.shape[2]
@@ -293,15 +301,8 @@
     local_rows = sides_ref.shape[0] // size
     lines = tiles_ref.shape[0] // BLOCK
     per = lines // (local_rows * halves)
-    order = sides_ref.shape[1]
-    early = pl.num_programs(0) // 2
-    for source, taken in ((across_ref, t < early), (last_ref, t >= early)):
-
-        @pl.when(taken)
-        def _(source=source):
-            for u in range(halves):
-                line_ref[u * BLOCK : (u + 1) * BLOCK, :] = source[:, u].reshape(BLOCK, order)
-
+    for u in range(halves):
+        line_ref[u * BLOCK : (u + 1) * BLOCK, :] = across_ref[:, u].reshape(BLOCK, sides_ref.shape[1])
     change = times_parts(parts_of(sides_ref[...]), parts_of(line_ref[...]), ROWS_BY_ROWS)
     row = lax.broadcasted_iota(jnp.int32, (BLOCK, BLOCK), 0)
     col = lax.broadcasted_iota(jnp.int32, (BLOCK, BLOCK), 1)
@@ -321,11 +322,9 @@
                 out_ref[pl.ds(start * per + t * halves + h, BLOCK, stride=per), :] = value
 
 
-def finish(place, tiles, sides, across, last, solved, boost, grid_rows, grid_cols):
-    ranks, lines, cols, order = across.shape
-    halves = boost.shape[2] // BLOCK
-    early = lines // halves
-    steps = 2 * early
+def finish(place, tiles, sides, across, solved, boost, grid_rows, grid_cols):
+    order = sides.shape[1]
+    steps = tiles.shape[0] // (sides.shape[0] * (boost.shape[2] // BLOCK))
 
     def still(*shape):
         return pl.BlockSpec(shape, lambda t: (0,) * len(shape))
@@ -338,8 +337,7 @@
             SCALARS,
             still(*tiles.shape),
             still(*sides.shape),
-            pl.BlockSpec((ranks, halves, cols, order), lambda t: (0, jnp.minimum(t, early - 1), 0, 0)),
-            pl.BlockSpec((ranks, halves, cols, order), lambda t: (0, jnp.maximum(t - early, 0), 0, 0)),
+            pl.BlockSpec((across.shape[0], across.shape[1] // steps) + across.shape[2:], lambda t: (0, t, 0, 0)),
             still(*solved.shape),
             still(*boost.shape),
         ],
@@ -348,7 +346,7 @@
         compiler_params=pltpu.CompilerParams(vmem_limit_bytes=48 * 2**20),
         cost_estimate=pl.CostEstimate(flops=4 * 10**9, bytes_accessed=12 * 2**20, transcendentals=0),
         name="finish",
-    )(place, tiles, sides, across, last, solved, boost)
+    )(place, tiles, sides, across, solved, boost)
 
 
 def body(front_entries, child_updates, diag_boost, tile_mask, child_parent, child_index):
@@ -367,19 +365,17 @@
     halves = grid_rows // grid_cols
     order = PANELS * size
 
-    pieces = child_updates.reshape(held, child_tiles, slices, child_tiles, size)
+    blocks = order // BLOCK
     parents = child_parent.reshape(groups, held)
     comes = parents == my_group
     index = jnp.sum(jnp.where(comes[:, :, None], child_index.reshape(groups, held, child_tiles), 0), axis=1)
     index = jnp.where(jnp.any(comes, axis=1)[:, None], index, -1)
     mine = lax.dynamic_index_in_dim(parents, my_group, 0, keepdims=False)
     goes = (mine[None, :] == jnp.arange(groups)[:, None])[:, :, None, None, None]
-    blocks = order // BLOCK
-    narrow = pieces[:, :, :, :PANELS].reshape(held, child_tiles * slices, blocks, BLOCK)
-    narrow = jnp.sum(jnp.where(goes, narrow[None], 0.0), axis=1)
-    narrow = lax.all_to_all(narrow, "front", split_axis=0, concat_axis=0, tiled=True)
-    arrived = lax.all_gather(pieces, "front", axis=0)
-    arrived = jnp.sum(jnp.where(comes[:, :, None, None, None, None], arrived, 0.0), axis=1)
+    pieces = child_updates.reshape(held, child_tiles * slices, child_tiles * size // BLOCK, BLOCK)
+    slots = jnp.sum(jnp.where(goes, pieces[None], 0.0), axis=1)
+    lines_of = lax.all_to_all(slots, "front", split_axis=0, concat_axis=0, tiled=True)
+    arrived = lines_of.reshape(groups, child_tiles, slices, child_tiles, size)
 
     entries = front_entries.reshape(local_rows, slices, grid_rows, grid_cols, local_cols, size)
     mask_tiles = jnp.transpose(tile_mask[0].reshape(local_rows, grid_rows, local_cols, grid_cols), (0, 1, 3, 2))
@@ -396,25 +392,24 @@
     )
     boost = jnp.where((jnp.arange(local_rows) == 0)[:, None, None, None, None], boost, 0.0)
     base = jnp.where(kept[:, :, :, :PANELS, 0], entries[:, :, :, :PANELS, 0, :], 0.0) + boost
-    lines, split = make_panel(index, base.reshape(-1, blocks, BLOCK), narrow.reshape(-1, blocks, BLOCK), grid_rows)
+    children = lines_of.reshape((-1,) + lines_of.shape[2:])
+    lines, split = make_panel(index, base.reshape(-1, blocks, BLOCK), children, grid_rows)
 
     split = lax.all_to_all(split, "col", split_axis=0, concat_axis=0, tiled=True)
     for_cols = jnp.transpose(split, (1, 0, 2, 3)).reshape(local_cols * slices, grid_cols, order)
+    lines, for_cols = lax.optimization_barrier((lines, for_cols))
+    across = lax.all_gather(for_cols, "row", axis=0)
 
     lines = lines.reshape(grid_rows * grid_cols, -1, 1, BLOCK)
-    lines, for_cols = lax.optimization_barrier((lines, for_cols))
-    part = local_cols * slices // 2
-    across = lax.all_gather(for_cols[:part], "row", axis=0)
     lines = lax.all_to_all(lines, ("row", "col"), split_axis=0, concat_axis=0, tiled=True)
     lines = jnp.transpose(lines.reshape(grid_rows * grid_cols, -1, BLOCK), (1, 0, 2))
-    for_rows, for_top = lines[: local_rows * slices].reshape(local_rows * size, BLOCK), lines[local_rows * slices :]
 
     spread = jnp.einsum("naube,ntpb->nautpe", arrived, col_hits, precision=HIGHEST)
     assembled = jnp.where(kept, entries, 0.0) + jnp.einsum("niqa,nautpe->iuqpte", row_hits, spread, precision=HIGHEST)
     joined = jnp.transpose(assembled, (2, 3, 0, 1, 4, 5))
     joined = joined.reshape(grid_rows * grid_cols, local_rows * slices, local_cols * size // BLOCK, BLOCK)
 
-    joined, across, last = lax.optimization_barrier((joined, across, for_cols[part:]))
+    lines, joined = lax.optimization_barrier((lines, joined))
     tiles = lax.all_to_all(joined, ("row", "col"), split_axis=0, concat_axis=0, tiled=True).reshape(-1, BLOCK)
 
     def over_chips(value):
@@ -426,13 +421,11 @@
         return lax.ppermute(value, "col", [(c, c ^ 1) for c in range(grid_cols)])
 
     place = jnp.stack([my_row, my_col]).astype(jnp.int32)
-    own_top = over_chips(for_top)
-    other_top = over_cores(own_top)
-    rows = lax.all_gather(for_rows, "col", axis=0)
-    last = lax.all_gather(last, "row", axis=0)
-    inverse, mine = factor(place, own_top, other_top, order)
-    solved, sides = solve(place, rows, mine, inverse, grid_rows)
-    out = finish(place, tiles, sides, across, last, solved, diag_boost[0][:, None, :], grid_rows, grid_cols)
+    own = over_chips(lines)
+    other = over_cores(own)
+    inverse, mine = factor(place, own, other, order)
+    solved, sides = solve(place, own, other, mine, inverse, grid_rows, local_rows)
+    out = finish(place, tiles, sides, across, solved, diag_boost[0][:, None, :], grid_rows, grid_cols)
     return out.reshape(1, local_rows, 1, size, local_cols, 1, size)
 
 

time: 304 us -> 274 us (0.901)
  the two profiles are of different devices: /device:TPU:16 before, /device:TPU:1 now
where the time goes in v6:
time: 274 us; the launch traced here: 269 us
  waiting for transfers between devices  76.9 us (28%)
  Pallas kernels  76 us (28%)
  starting transfers between devices  45.8 us (17%)
  local copies, waits for them, and re-layouts  21.5 us (8%)
  blocking collectives  18 us (7%)
  between operations  13.7 us (5%)
  matrix products  8.62 us (3%)
  other arithmetic  8.43 us (3%)
    pallas_call x1, Pallas kernels, factor(): pl.pallas_call(factor_kernel, out_shape=(jax.ShapeDtypeStruct((order, ord...  55.7 us
    ppermute x3, waiting for transfers between devices, over_chips(): lax.ppermute(value, 'col', [(c, (c + 2 * d) % grid_cols) for c in cols])  28.2 us
    all_gather x1, waiting for transfers between devices, body(): across = lax.all_gather(for_cols, 'row', axis=0)  25 us
    all_to_all x1, starting transfers between devices, body(): lax.all_to_all(lines, ('row', 'col'), split_axis=0, concat_axis=0, tiled=...  18.5 us
    all_to_all x1, blocking collectives, body(): lax.all_to_all(split, 'col', split_axis=0, concat_axis=0, tiled=True)  18 us
    all_to_all x1, waiting for transfers between devices, body(): lax.all_to_all(lines, ('row', 'col'), split_axis=0, concat_axis=0, tiled=...  17.9 us
    ppermute x3, starting transfers between devices, over_chips(): lax.ppermute(value, 'col', [(c, (c + 2 * d) % grid_cols) for c in cols])  10.1 us
    unnamed x33, local copies, waits for them, and re-layouts  9.11 us
  transfers between devices with their start and end apart: 8, of which 7 were waited for; matrix products, arithmetic and copies ran while one was open for 9% of the time, Pallas kernels for 24%

profile of v6, /device:TPU:1, one launch (start us, length us, event | category | flops | bytes accessed | tf_op | source)
XLA Modules:
  0.0 268.9 jit_solution(11270281430948274433)
XLA Ops:
  6.5 0.7 reshape.174
  7.3 0.6 copy-done.14
  7.9 2.5 select_reduce_fusion
  10.3 5.0 %all-to-all-start = ((f32[4,24,24,128]{3,2,1,0:T(8,128)}), f32[4,24,24,128]{3,2,1,0:T(8,128)S(1)}, u32[]{:S(2)}, u32[]{:S(2)}) async-start(f32[4,24,24,128]{3,2,1,0:T(8,128)} %select_reduce_fusion), calls=%async_computation | async-start | bytes 2359296 | tf_op jit(solution)/shard_map/all_to_all | solution.py:377
  15.3 0.7 slice_bitcast_fusion
  16.0 0.1 iota_compare_fusion.2
  16.1 0.1 broadcast_select_fusion.1
  16.3 0.8 broadcast_in_dim.168
  17.1 0.0 copy-done.9
  17.1 1.2 copy.75
  18.3 0.2 copy.52
  18.5 0.8 squeeze.9
  19.3 0.0 copy-done.13
  19.4 0.1 broadcast_in_dim.158
  19.4 0.1 broadcast_in_dim.159
  19.5 0.1 eq.103
  19.6 0.0 copy-start.10
  19.6 0.1 copy.64
  19.8 0.1 broadcast_in_dim.155
  19.8 0.1 copy.50
  19.9 0.8 fusion.14
  20.7 0.8 select_reduce_fusion.1
  21.5 0.6 broadcast_select_fusion.2.index_ref
  22.2 1.9 select_add_fusion.base_ref
  24.1 1.9 all-to-all-done
  26.0 1.0 copy-done.7
  27.0 2.9 %panel.1 = (f32[1152,1,128]{2,1,0:T(1,128)}, f32[8,8,8,128]{3,2,1,0:T(8,128)}) custom-call(s32[4,12]{1,0:T(4,128)} %broadcast_select_fusion.2.index_ref, f32[64,8,128]{2,1,0:T(8,128)} %select_add_fusion.base_ref, f32[96,24,128]{2,1,0:T(8,128)} %bitcast.71), custom_call_target="tpu_custom_call" | custom-call | flops 1000000 | bytes 2097152 | tf_op jit(solution)/shard_map/panel/pallas_call | solution.py:146
  29.9 18.0 %all_to_all.20 = f32[8,8,8,128]{3,2,1,0:T(8,128)} all-to-all(f32[8,8,8,128]{3,2,1,0:T(8,128)} %get-tuple-element.16), channel_id=1, replica_groups=mesh['front'=4,'row'=16,'col'=8] {'col'}, dimensions={0} | all-to-all | bytes 524288 | tf_op jit(solution)/shard_map/all_to_all | solution.py:398
  47.9 1.0 reshape.178
  48.9 0.0 copy-done.10
  48.9 18.5 %all-to-all-start.2 = ((f32[128,9,1,128]{3,2,1,0:T(1,128)}), f32[128,9,1,128]{3,2,1,0:T(1,128)}, u32[]{:S(2)}, u32[]{:S(2)}) async-start(f32[128,9,1,128]{3,2,1,0:T(1,128)} %bitcast.81), calls=%async_computation.2 | async-start | bytes 1179648 | tf_op jit(solution)/shard_map/all_to_all | solution.py:404
  67.4 0.8 copy.54
  68.3 0.6 iota_add_fusion.1
  68.9 0.6 iota_add_fusion
  69.6 1.5 reshape.187
  71.0 2.9 %convolution_bitcast_fusion = f32[4,12,2,4,8,256,1]{5,4,2,1,3,0,6:T(8,128)S(1)} fusion(f32[4,12,2,12,256,1]{4,3,2,1,0,5:T(8,128)} %reshape.187, s32[4,8]{1,0:T(4,128)} %iota_add_fusion, s32[4,12]{1,0:T(4,128)} %broadcast_select_fusion.2.index_ref), kind=kOutput, calls=%fused_computation.7 | convolution fusion | flops 113247744 | bytes 4325696 | tf_op jit(solution)/shard_map/naube,ntpb->nautpe/dot_general | solution.py:407
  74.0 5.7 %fusion.2 = f32[16,8,2,2,4,256]{5,0,2,1,4,3:T(8,128)S(1)} fusion(f32[4,12,2,4,8,256,1]{5,4,2,1,3,0,6:T(8,128)S(1)} %convolution_bitcast_fusion, pred[2,16,8,4]{1,0,2,3:T(4,128)(4,1)S(1)} %copy.54, s32[2,16]{1,0:T(2,128)S(1)} %copy-done.15, s32[4,12]{1,0:T(4,128)S(1)} %copy-done.12, f32[1,2,2,1,1,16,8,4,256]{8,7,6,5,4,3,2,1,0:T(4,128)S(1)} %copy-done.9), kind=kOutput, calls=%fused_computation.5 | convolution fusion | flops 303040000 | bytes 7341376 | tf_op jit(solution)/shard_map/niqa,nautpe->iuqpte/dot_general | solution.py:408
  79.7 1.4 copy.56
  81.1 1.8 reshape.182
  82.9 17.9 %all-to-all-done.2 = f32[128,9,1,128]{3,2,1,0:T(1,128)} async-done(((f32[128,9,1,128]{3,2,1,0:T(1,128)}), f32[128,9,1,128]{3,2,1,0:T(1,128)}, u32[]{:S(2)}, u32[]{:S(2)}) %all-to-all-start.2) | async-done | bytes 589856 | tf_op jit(solution)/shard_map/all_to_all | solution.py:404
  100.8 1.1 copy.76
  101.9 9.0 %all-to-all-start.3 = ((f32[128,4,8,128]{3,2,1,0:T(8,128)}), f32[128,4,8,128]{3,2,1,0:T(8,128)S(1)}, u32[]{:S(2)}, u32[]{:S(2)}) async-start(f32[128,4,8,128]{3,2,1,0:T(8,128)} %reshape.182), calls=%async_computation.3 | async-start | bytes 4194304 | tf_op jit(solution)/shard_map/all_to_all | solution.py:413
  110.9 0.0 all-gather.3.cloned.1.call-start
  111.0 0.9 copy.57
  111.8 0.0 all-gather.3.cloned.1.call-update
  111.9 4.8 %collective-permute-start.2 = (f32[9,128,128]{2,1,0:T(8,128)S(1)}, f32[9,128,128]{2,1,0:T(8,128)S(1)}, u32[]{:S(2)}, u32[]{:S(2)}) collective-permute-start(f32[9,128,128]{2,1,0:T(8,128)S(1)} %bitcast.73), channel_id=1, source_target_pairs={{0,4},{1,5},{2,6},{3,7},{4,0},{5,1},{6,2},{7,3},{8,12},{9,13},{10,... | collective-permute-start | bytes 1769480 | tf_op jit(solution)/shard_map/ppermute | solution.py:417
  116.7 2.8 %collective-permute-start.1 = (f32[9,128,128]{2,1,0:T(8,128)S(1)}, f32[9,128,128]{2,1,0:T(8,128)S(1)}, u32[]{:S(2)}, u32[]{:S(2)}) collective-permute-start(f32[9,128,128]{2,1,0:T(8,128)S(1)} %bitcast.74), channel_id=1, source_target_pairs={{0,6},{1,7},{2,0},{3,1},{4,2},{5,3},{6,4},{7,5},{8,14},{9,15},{10,... | collective-permute-start | bytes 1769480 | tf_op jit(solution)/shard_map/ppermute | solution.py:417
  119.5 2.5 collective-permute-start
  122.0 11.4 %collective-permute-done.2 = f32[9,128,128]{2,1,0:T(8,128)S(1)} collective-permute-done((f32[9,128,128]{2,1,0:T(8,128)S(1)}, f32[9,128,128]{2,1,0:T(8,128)S(1)}, u32[]{:S(2)}, u32[]{:S(2)}) %collective-permute-start.2) | collective-permute-done | bytes 589856 | tf_op jit(solution)/shard_map/ppermute | solution.py:417
  133.4 16.7 %collective-permute-done.1 = f32[9,128,128]{2,1,0:T(8,128)S(1)} collective-permute-done((f32[9,128,128]{2,1,0:T(8,128)S(1)}, f32[9,128,128]{2,1,0:T(8,128)S(1)}, u32[]{:S(2)}, u32[]{:S(2)}) %collective-permute-start.1) | collective-permute-done | bytes 589856 | tf_op jit(solution)/shard_map/ppermute | solution.py:417
  150.1 0.1 collective-permute-done
  150.2 0.2 pad_maximum_fusion.own_ref
  150.4 3.2 %collective-permute-start.3 = (f32[4,9,128,128]{3,2,1,0:T(8,128)S(1)}, f32[4,9,128,128]{3,2,1,0:T(8,128)S(1)}, u32[]{:S(2)}, u32[]{:S(2)}) collective-permute-start(f32[4,9,128,128]{3,2,1,0:T(8,128)S(1)} %pad_maximum_fusion.own_ref), channel_id=1, source_target_pairs={{0,1},{1,0},{2,3},{3,2},{4,5},{5,4},{6,7},{7,6},{8,9},{9,8},{10,11... | collective-permute-start | bytes 7077896 | tf_op jit(solution)/shard_map/ppermute | solution.py:421
  153.7 0.1 pad_add_fusion.place_ref
  153.7 3.8 %collective-permute-done.3.other_ref = f32[4,9,128,128]{3,2,1,0:T(8,128)S(1)} collective-permute-done((f32[4,9,128,128]{3,2,1,0:T(8,128)S(1)}, f32[4,9,128,128]{3,2,1,0:T(8,128)S(1)}, u32[]{:S(2)}, u32[]{:S(2)}) %collective-permute-start.3) | collective-permute-done | bytes 2359328 | tf_op jit(solution)/shard_map/ppermute | solution.py:421
  157.5 55.7 %factor.1 = (f32[1024,1024]{1,0:T(8,128)S(1)}, f32[256,1024]{1,0:T(8,128)S(1)}) custom-call(s32[2]{0:T(128)S(1)} %pad_add_fusion.place_ref, s32[2,40]{1,0:T(2,128)S(1)} %copy-done.3, f32[4,9,128,128]{3,2,1,0:T(8,128)S(1)} %pad_maximum_fusion.own_ref, f32[4,9,128,128]{3,2,1,0:T(8,128)S(1)} %collective-permute-done.3.other_ref), custom_call_target="tpu_custom_call" | custom-call | flops 1000000 | bytes 1024 | tf_op jit(solution)/shard_map/factor/pallas_call | solution.py:232
  213.2 2.0 copy-done.2
  215.2 9.1 %solve.1 = (f32[512,1024]{1,0:T(8,128)S(1)}, f32[512,1024]{1,0:T(8,128)S(1)}) custom-call(s32[2]{0:T(128)S(1)} %pad_add_fusion.place_ref, f32[4,9,128,128]{3,2,1,0:T(8,128)} %copy-done, f32[4,9,128,128]{3,2,1,0:T(8,128)} %copy-done.1, f32[256,1024]{1,0:T(8,128)S(1)} %get-tuple-element.20.mine_ref, f32[1024,1024]{1,0:T(8,128)} %copy-done.2), custom_call_target="tpu_custom_call" | custom-call | flops 1000000 | bytes 1024 | tf_op jit(solution)/shard_map/solve/pallas_call | solution.py:284
  224.3 1.3 copy-done.4
  225.6 1.4 copy-done.5
  227.0 25.0 %all-gather.3.cloned.1.call-done = f32[128,8,1024]{2,1,0:T(8,128)} async-done(((f32[8,8,1024]{2,1,0:T(8,128)}), f32[128,8,1024]{2,1,0:T(8,128)}) %all-gather.3.cloned.1.call-update) | async-done | bytes 4194320 | tf_op jit(solution)/shard_map/all_gather | solution.py:401
  252.0 0.0 all-to-all-done.3
  252.0 1.6 copy-done.6
  253.6 8.4 %finish.1 = f32[4096,128]{1,0:T(8,128)} custom-call(s32[2]{0:T(128)S(1)} %pad_add_fusion.place_ref, f32[4096,128]{1,0:T(8,128)S(1)} %bitcast.70, f32[512,1024]{1,0:T(8,128)S(1)} %copy-done.6, f32[16,8,8,1024]{3,2,1,0:T(8,128)} %bitcast.87, f32[512,1024]{1,0:T(8,128)} %copy-done.4, f32[32,1,256]{2,1,0:T(1,128)S(1)} %broadcast_in_dim_squeeze.3.boost_ref), custom_call_target="tpu_custom_call" | custom-call | flops 4000000000 | bytes 12582912 | tf_op jit(solution)/shard_map/finish/pallas_call | solution.py:332
  (35 shorter events, 0.2 us)
Async XLA Ops:
  7.3 0.6 copy-start.14
  10.3 6.8 %copy-start.9 = (f32[1,2,2,1,1,16,8,4,256]{8,7,6,5,4,3,2,1,0:T(4,128)S(1)}, f32[1,2,2,1,1,16,8,4,256]{8,7,6,5,4,3,2,1,0:T(4,128)}, u32[]{:S(2)}) copy-start(f32[1,2,2,1,1,16,8,4,256]{8,7,6,5,4,3,2,1,0:T(4,128)} %param.7) | copy-start | bytes 6291460
  10.3 15.7 %all-to-all-start = ((f32[4,24,24,128]{3,2,1,0:T(8,128)}), f32[4,24,24,128]{3,2,1,0:T(8,128)S(1)}, u32[]{:S(2)}, u32[]{:S(2)}) async-start(f32[4,24,24,128]{3,2,1,0:T(8,128)} %select_reduce_fusion), calls=%async_computation | async-start | bytes 2359296 | tf_op jit(solution)/shard_map/all_to_all | solution.py:377
  17.1 2.2 copy-start.13
  19.6 29.3 %copy-start.10 = (pred[2,16,4,8]{3,2,1,0:T(4,128)(4,1)}, pred[2,16,4,8]{3,2,1,0:T(4,128)(4,1)S(1)}, u32[]{:S(2)}) copy-start(pred[2,16,4,8]{3,2,1,0:T(4,128)(4,1)S(1)} %eq.103) | copy-start | bytes 3076
  26.0 1.0 copy-start.7
  29.9 39.6 %copy-start.8 = (f32[4,24,24,128]{3,2,1,0:T(8,128)S(1)}, f32[4,24,24,128]{3,2,1,0:T(8,128)}, u32[]{:S(2)}) copy-start(f32[4,24,24,128]{3,2,1,0:T(8,128)} %copy-done.7) | copy-start | bytes 3538948
  48.9 51.9 %all-to-all-start.2 = ((f32[128,9,1,128]{3,2,1,0:T(1,128)}), f32[128,9,1,128]{3,2,1,0:T(1,128)}, u32[]{:S(2)}, u32[]{:S(2)}) async-start(f32[128,9,1,128]{3,2,1,0:T(1,128)} %bitcast.81), calls=%async_computation.2 | async-start | bytes 1179648 | tf_op jit(solution)/shard_map/all_to_all | solution.py:404
  71.0 2.9 %copy-start.12 = (s32[4,12]{1,0:T(4,128)S(1)}, s32[4,12]{1,0:T(4,128)}, u32[]{:S(2)}) copy-start(s32[4,12]{1,0:T(4,128)} %broadcast_select_fusion.2.index_ref) | copy-start | bytes 580
  71.0 2.9 %copy-start.15 = (s32[2,16]{1,0:T(2,128)S(1)}, s32[2,16]{1,0:T(2,128)}, u32[]{:S(2)}) copy-start(s32[2,16]{1,0:T(2,128)} %iota_add_fusion.1) | copy-start | bytes 388
  101.9 150.1 %all-to-all-start.3 = ((f32[128,4,8,128]{3,2,1,0:T(8,128)}), f32[128,4,8,128]{3,2,1,0:T(8,128)S(1)}, u32[]{:S(2)}, u32[]{:S(2)}) async-start(f32[128,4,8,128]{3,2,1,0:T(8,128)} %reshape.182), calls=%async_computation.3 | async-start | bytes 4194304 | tf_op jit(solution)/shard_map/all_to_all | solution.py:413
  110.9 141.1 %all-gather.3.cloned.1.call-start = ((), (), s32[]{:S(2)}) async-start(), calls=%async_computation.4 | async-start | bytes 4456448 | tf_op jit(solution)/shard_map/all_gather | solution.py:401
  111.9 21.5 %collective-permute-start.2 = (f32[9,128,128]{2,1,0:T(8,128)S(1)}, f32[9,128,128]{2,1,0:T(8,128)S(1)}, u32[]{:S(2)}, u32[]{:S(2)}) collective-permute-start(f32[9,128,128]{2,1,0:T(8,128)S(1)} %bitcast.73), channel_id=1, source_target_pairs={{0,4},{1,5},{2,6},{3,7},{4,0},{5,1},{6,2},{7,3},{8,12},{9,13},{10,... | collective-permute-start | bytes 1769480 | tf_op jit(solution)/shard_map/ppermute | solution.py:417
  116.7 33.5 %collective-permute-start.1 = (f32[9,128,128]{2,1,0:T(8,128)S(1)}, f32[9,128,128]{2,1,0:T(8,128)S(1)}, u32[]{:S(2)}, u32[]{:S(2)}) collective-permute-start(f32[9,128,128]{2,1,0:T(8,128)S(1)} %bitcast.74), channel_id=1, source_target_pairs={{0,6},{1,7},{2,0},{3,1},{4,2},{5,3},{6,4},{7,5},{8,14},{9,15},{10,... | collective-permute-start | bytes 1769480 | tf_op jit(solution)/shard_map/ppermute | solution.py:417
  119.5 30.7 %collective-permute-start = (f32[9,128,128]{2,1,0:T(8,128)S(1)}, f32[9,128,128]{2,1,0:T(8,128)S(1)}, u32[]{:S(2)}, u32[]{:S(2)}) collective-permute-start(f32[9,128,128]{2,1,0:T(8,128)S(1)} %bitcast.75), channel_id=1, source_target_pairs={{0,2},{1,3},{2,4},{3,5},{4,6},{5,7},{6,0},{7,1},{8,10},{9,11},{10,... | collective-permute-start | bytes 1769480 | tf_op jit(solution)/shard_map/ppermute | solution.py:417
  150.2 3.4 %copy-start.11 = (f32[1,32,256]{2,1,0:T(8,128)S(1)}, f32[1,32,256]{2,1,0:T(8,128)}, u32[]{:S(2)}) copy-start(f32[1,32,256]{2,1,0:T(8,128)} %param.9) | copy-start | bytes 98308
  150.2 7.4 %copy-start.3 = (s32[2,40]{1,0:T(2,128)S(1)}, s32[2,40]{1,0:T(2,128)}, u32[]{:S(2)}) copy-start(s32[2,40]{1,0:T(2,128)} %constant.40.clone.pairs_ref) | copy-start | bytes 964
  150.4 62.8 %copy-start = (f32[4,9,128,128]{3,2,1,0:T(8,128)}, f32[4,9,128,128]{3,2,1,0:T(8,128)S(1)}, u32[]{:S(2)}) copy-start(f32[4,9,128,128]{3,2,1,0:T(8,128)S(1)} %pad_maximum_fusion.own_ref) | copy-start | bytes 7077892
  150.4 7.1 %collective-permute-start.3 = (f32[4,9,128,128]{3,2,1,0:T(8,128)S(1)}, f32[4,9,128,128]{3,2,1,0:T(8,128)S(1)}, u32[]{:S(2)}, u32[]{:S(2)}) collective-permute-start(f32[4,9,128,128]{3,2,1,0:T(8,128)S(1)} %pad_maximum_fusion.own_ref), channel_id=1, source_target_pairs={{0,1},{1,0},{2,3},{3,2},{4,5},{5,4},{6,7},{7,6},{8,9},{9,8},{10,11... | collective-permute-start | bytes 7077896 | tf_op jit(solution)/shard_map/ppermute | solution.py:421
  157.5 55.7 %copy-start.1 = (f32[4,9,128,128]{3,2,1,0:T(8,128)}, f32[4,9,128,128]{3,2,1,0:T(8,128)S(1)}, u32[]{:S(2)}) copy-start(f32[4,9,128,128]{3,2,1,0:T(8,128)S(1)} %collective-permute-done.3.other_ref) | copy-start | bytes 7077892
  213.2 2.0 copy-start.2
  224.3 1.3 copy-start.4
  225.6 1.4 copy-start.5
  252.0 1.6 copy-start.6
Sparse Core Ops, SparseCore 0:
  113.8 138.1 all-gather.2

commit v7 on v6

--- a/solution.py
+++ b/solution.py
@@ -157,6 +157,21 @@
     )(index, base, narrow)
 
 
+def step_after(place, other, cost):
+    def kernel(place_ref, _, out_ref):
+        for i in range(place_ref.shape[0]):
+            out_ref[i] = place_ref[i]
+
+    return pl.pallas_call(
+        kernel,
+        out_shape=jax.ShapeDtypeStruct(place.shape, place.dtype),
+        in_specs=[SCALARS, pl.BlockSpec(memory_space=pl.ANY)],
+        out_specs=SCALARS,
+        cost_estimate=pl.CostEstimate(flops=cost, bytes_accessed=2**10, transcendentals=0),
+        name="step_after",
+    )(place, other)
+
+
 SOURCES = (0, 1, -1, 2)
 
 
@@ -238,7 +253,7 @@
         in_specs=[SCALARS, SCALARS, WHOLE, WHOLE],
         out_specs=(WHOLE, WHOLE),
         scratch_shapes=[pltpu.VMEM((order, BLOCK), jnp.float32), pltpu.VMEM((order, BLOCK), jnp.float32)],
-        compiler_params=pltpu.CompilerParams(vmem_limit_bytes=40 * 2**20),
+        compiler_params=pltpu.CompilerParams(vmem_limit_bytes=20 * 2**20),
         cost_estimate=pl.CostEstimate(flops=10**6, bytes_accessed=2**10, transcendentals=0),
         name="factor",
     )(place, pairs, own, other)
@@ -287,7 +302,7 @@
         in_specs=[SCALARS, WHOLE, WHOLE, WHOLE, WHOLE],
         out_specs=(WHOLE, WHOLE),
         scratch_shapes=[pltpu.VMEM((order // BLOCK, total, BLOCK), jnp.float32)],
-        compiler_params=pltpu.CompilerParams(vmem_limit_bytes=48 * 2**20),
+        compiler_params=pltpu.CompilerParams(vmem_limit_bytes=20 * 2**20),
         cost_estimate=pl.CostEstimate(flops=10**6, bytes_accessed=2**10, transcendentals=0),
         name="solve",
     )(place, own, other, mine, inverse)
@@ -343,7 +358,7 @@
         ],
         out_specs=still(*tiles.shape),
         scratch_shapes=[pltpu.VMEM((boost.shape[2], order), jnp.float32)],
-        compiler_params=pltpu.CompilerParams(vmem_limit_bytes=48 * 2**20),
+        compiler_params=pltpu.CompilerParams(vmem_limit_bytes=20 * 2**20),
         cost_estimate=pl.CostEstimate(flops=4 * 10**9, bytes_accessed=12 * 2**20, transcendentals=0),
         name="finish",
     )(place, tiles, sides, across, solved, boost)
@@ -397,7 +412,7 @@
 
     split = lax.all_to_all(split, "col", split_axis=0, concat_axis=0, tiled=True)
     for_cols = jnp.transpose(split, (1, 0, 2, 3)).reshape(local_cols * slices, grid_cols, order)
-    lines, for_cols = lax.optimization_barrier((lines, for_cols))
+    lines, for_cols, arrived = lax.optimization_barrier((lines, for_cols, arrived))
     across = lax.all_gather(for_cols, "row", axis=0)
 
     lines = lines.reshape(grid_rows * grid_cols, -1, 1, BLOCK)
@@ -423,6 +438,7 @@
     place = jnp.stack([my_row, my_col]).astype(jnp.int32)
     own = over_chips(lines)
     other = over_cores(own)
+    place = step_after(step_after(place, lines, 10**10), own, 10**11)
     inverse, mine = factor(place, own, other, order)
     solved, sides = solve(place, own, other, mine, inverse, grid_rows, local_rows)
     out = finish(place, tiles, sides, across, solved, diag_boost[0][:, None, :], grid_rows, grid_cols)

time: 274 us -> 259 us (0.945); the launches traced: 269 us -> 258 us
  blocking collectives: 18 us -> 0 us
  starting transfers between devices: 45.8 us -> 59.8 us
  waiting for transfers between devices: 76.9 us -> 71.1 us
    all_to_all x1 -> x0, blocking collectives: 18 us -> none  [body(): lax.all_to_all(split, 'col', split_axis=0, concat_axis=0, tiled=True)]
    ppermute x3, waiting for transfers between devices: 28.2 us -> 13 us  [over_chips(): lax.ppermute(value, 'col', [(c, (c + 2 * d) % grid_cols) for c in cols])]
    all_to_all x0 -> x1, starting transfers between devices: none -> 11.2 us  [body(): lax.all_to_all(split, 'col', split_axis=0, concat_axis=0, tiled=True)]
    all_to_all x1, waiting for transfers between devices: 0.01 us -> 7.25 us  [body(): lax.all_to_all(joined, ('row', 'col'), split_axis=0, concat_axis=0, tiled...]
    all_gather x1, waiting for transfers between devices: 25 us -> 18.6 us  [body(): across = lax.all_gather(for_cols, 'row', axis=0)]
    all_to_all x0 -> x1, waiting for transfers between devices: none -> 4.92 us  [body(): lax.all_to_all(split, 'col', split_axis=0, concat_axis=0, tiled=True)]
    all_to_all x1, waiting for transfers between devices: 17.9 us -> 20.7 us  [body(): lax.all_to_all(lines, ('row', 'col'), split_axis=0, concat_axis=0, tiled=...]
    unnamed x33 -> x39, local copies, waits for them, and re-layouts: 9.11 us -> 10.7 us
  transfers between devices with their start and end apart: 8 -> 9, of which waited for: 7 -> 8; matrix products, arithmetic and copies ran while one was open for 9% -> 9% of each run, Pallas kernels for 24% -> 26%
where the time goes in v7:
time: 259 us; the launch traced here: 258 us
  Pallas kernels  77.4 us (30%)
  waiting for transfers between devices  71.1 us (27%)
  starting transfers between devices  59.8 us (23%)
  local copies, waits for them, and re-layouts  20.8 us (8%)
  between operations  13.7 us (5%)
  other arithmetic  8.2 us (3%)
  matrix products  7.21 us (3%)
    pallas_call x1, Pallas kernels, factor(): pl.pallas_call(factor_kernel, out_shape=(jax.ShapeDtypeStruct((order, ord...  56.8 us
    all_to_all x1, waiting for transfers between devices, body(): lax.all_to_all(lines, ('row', 'col'), split_axis=0, concat_axis=0, tiled=...  20.7 us
    all_gather x1, waiting for transfers between devices, body(): across = lax.all_gather(for_cols, 'row', axis=0)  18.6 us
    all_to_all x1, starting transfers between devices, body(): lax.all_to_all(lines, ('row', 'col'), split_axis=0, concat_axis=0, tiled=...  18.5 us
    ppermute x3, waiting for transfers between devices, over_chips(): lax.ppermute(value, 'col', [(c, (c + 2 * d) % grid_cols) for c in cols])  13 us
    ppermute x3, starting transfers between devices, over_chips(): lax.ppermute(value, 'col', [(c, (c + 2 * d) % grid_cols) for c in cols])  11.5 us
    all_to_all x1, starting transfers between devices, body(): lax.all_to_all(split, 'col', split_axis=0, concat_axis=0, tiled=True)  11.2 us
    unnamed x39, local copies, waits for them, and re-layouts  10.7 us
  transfers between devices with their start and end apart: 9, of which 8 were waited for; matrix products, arithmetic and copies ran while one was open for 9% of the time, Pallas kernels for 26%

profile of v7, /device:TPU:1, one launch (start us, length us, event | category | flops | bytes accessed | tf_op | source)
XLA Modules:
  0.0 258.1 jit_solution(2696958908011472392)
XLA Ops:
  6.5 0.7 reshape.174
  7.3 2.5 select_reduce_fusion
  9.8 5.0 %all-to-all-start = ((f32[4,24,24,128]{3,2,1,0:T(8,128)}), f32[4,24,24,128]{3,2,1,0:T(8,128)S(1)}, u32[]{:S(2)}, u32[]{:S(2)}) async-start(f32[4,24,24,128]{3,2,1,0:T(8,128)} %select_reduce_fusion), calls=%async_computation | async-start | bytes 2359296 | tf_op jit(solution)/shard_map/all_to_all | solution.py:392
  14.8 0.7 slice_bitcast_fusion
  15.5 0.1 iota_compare_fusion.2
  15.5 0.1 broadcast_select_fusion.1
  15.7 0.8 broadcast_in_dim.168
  16.5 1.2 copy.75
  17.8 0.2 copy.52
  17.9 0.1 squeeze.9
  18.1 0.1 broadcast_in_dim.158
  18.2 0.1 broadcast_in_dim.159
  18.3 0.1 eq.103
  18.4 0.1 copy.64
  18.5 0.1 broadcast_in_dim.155
  18.6 0.1 copy.50
  18.7 0.8 fusion.14
  19.5 0.8 select_reduce_fusion.1
  20.2 0.7 broadcast_select_fusion.2.index_ref
  20.9 0.9 select_add_fusion.base_ref
  21.8 3.6 %all-to-all-done = f32[4,24,24,128]{3,2,1,0:T(8,128)S(1)} async-done(((f32[4,24,24,128]{3,2,1,0:T(8,128)}), f32[4,24,24,128]{3,2,1,0:T(8,128)S(1)}, u32[]{:S(2)}, u32[]{:S(2)}) %all-to-all-start) | async-done | bytes 1179680 | tf_op jit(solution)/shard_map/all_to_all | solution.py:392
  25.4 1.0 copy-done.8
  26.5 2.9 %panel.1 = (f32[1152,1,128]{2,1,0:T(1,128)}, f32[8,8,8,128]{3,2,1,0:T(8,128)}) custom-call(s32[4,12]{1,0:T(4,128)} %broadcast_select_fusion.2.index_ref, f32[64,8,128]{2,1,0:T(8,128)} %select_add_fusion.base_ref, f32[96,24,128]{2,1,0:T(8,128)} %bitcast.73), custom_call_target="tpu_custom_call" | custom-call | flops 1000000 | bytes 2097152 | tf_op jit(solution)/shard_map/panel/pallas_call | solution.py:146
  29.3 11.2 %all-to-all-start.1 = ((f32[8,8,8,128]{3,2,1,0:T(8,128)}), f32[8,8,8,128]{3,2,1,0:T(8,128)S(1)}, u32[]{:S(2)}, u32[]{:S(2)}) async-start(f32[8,8,8,128]{3,2,1,0:T(8,128)} %get-tuple-element.17), calls=%async_computation.1 | async-start | bytes 524288 | tf_op jit(solution)/shard_map/all_to_all | solution.py:413
  40.5 1.6 reshape.179
  42.1 4.9 %all-to-all-done.1 = f32[8,8,8,128]{3,2,1,0:T(8,128)S(1)} async-done(((f32[8,8,8,128]{3,2,1,0:T(8,128)}), f32[8,8,8,128]{3,2,1,0:T(8,128)S(1)}, u32[]{:S(2)}, u32[]{:S(2)}) %all-to-all-start.1) | async-done | bytes 262176 | tf_op jit(solution)/shard_map/all_to_all | solution.py:413
  47.1 18.5 %all-to-all-start.2 = ((f32[128,9,1,128]{3,2,1,0:T(1,128)}), f32[128,9,1,128]{3,2,1,0:T(1,128)}, u32[]{:S(2)}, u32[]{:S(2)}) async-start(f32[128,9,1,128]{3,2,1,0:T(1,128)} %bitcast.13), calls=%async_computation.2 | async-start | bytes 1179648 | tf_op jit(solution)/shard_map/all_to_all | solution.py:419
  65.6 0.2 all-gather.3.cloned.1.call-start
  65.9 0.1 copy.54
  66.0 0.7 pad_add_fusion.place_ref
  66.7 0.1 iota_add_fusion.1
  66.7 0.1 iota_add_fusion
  66.8 1.5 convolution_bitcast_fusion
  68.3 0.1 copy-done.10
  68.4 5.8 %fusion.2 = f32[16,8,2,2,4,256]{5,0,2,1,4,3:T(8,128)S(1)} fusion(f32[4,12,2,4,8,256,1]{5,4,2,1,3,0,6:T(8,128)S(1)} %convolution_bitcast_fusion, pred[2,16,8,4]{1,0,2,3:T(4,128)(4,1)S(1)} %copy.54, s32[2,16]{1,0:T(2,128)S(1)} %iota_add_fusion.1, s32[4,12]{1,0:T(4,128)S(1)} %copy-done.16, f32[1,2,2,1,1,16,8,4,256]{8,7,6,5,4,3,2,1,0:T(4,128)S(1)} %copy-done.10), kind=kOutput, calls=%fused_computation.5 | convolution fusion | flops 303040000 | bytes 7341376 | tf_op jit(solution)/shard_map/niqa,nautpe->iuqpte/dot_general | solution.py:423
  74.2 1.4 copy.56
  75.5 1.8 reshape.182
  77.4 0.9 copy.57
  78.2 0.0 all-gather.3.cloned.1.call-update
  78.3 20.7 %all-to-all-done.2 = f32[128,9,1,128]{3,2,1,0:T(1,128)} async-done(((f32[128,9,1,128]{3,2,1,0:T(1,128)}), f32[128,9,1,128]{3,2,1,0:T(1,128)}, u32[]{:S(2)}, u32[]{:S(2)}) %all-to-all-start.2) | async-done | bytes 589856 | tf_op jit(solution)/shard_map/all_to_all | solution.py:419
  99.0 1.1 copy.76
  100.1 6.3 %collective-permute-start.2 = (f32[9,128,128]{2,1,0:T(8,128)S(1)}, f32[9,128,128]{2,1,0:T(8,128)S(1)}, u32[]{:S(2)}, u32[]{:S(2)}) collective-permute-start(f32[9,128,128]{2,1,0:T(8,128)S(1)} %bitcast.75), channel_id=1, source_target_pairs={{0,4},{1,5},{2,6},{3,7},{4,0},{5,1},{6,2},{7,3},{8,12},{9,13},{10,... | collective-permute-start | bytes 1769480 | tf_op jit(solution)/shard_map/ppermute | solution.py:432
  106.4 3.3 %collective-permute-start.1 = (f32[9,128,128]{2,1,0:T(8,128)S(1)}, f32[9,128,128]{2,1,0:T(8,128)S(1)}, u32[]{:S(2)}, u32[]{:S(2)}) collective-permute-start(f32[9,128,128]{2,1,0:T(8,128)S(1)} %bitcast.76), channel_id=1, source_target_pairs={{0,6},{1,7},{2,0},{3,1},{4,2},{5,3},{6,4},{7,5},{8,14},{9,15},{10,... | collective-permute-start | bytes 1769480 | tf_op jit(solution)/shard_map/ppermute | solution.py:432
  109.7 2.0 collective-permute-start
  111.7 9.0 %all-to-all-start.3 = ((f32[128,4,8,128]{3,2,1,0:T(8,128)}), f32[128,4,8,128]{3,2,1,0:T(8,128)}, u32[]{:S(2)}, u32[]{:S(2)}) async-start(f32[128,4,8,128]{3,2,1,0:T(8,128)} %reshape.182), calls=%async_computation.3 | async-start | bytes 4194304 | tf_op jit(solution)/shard_map/all_to_all | solution.py:428
  120.7 1.2 step_after.2.place_ref
  121.9 12.7 %collective-permute-done.1 = f32[9,128,128]{2,1,0:T(8,128)S(1)} collective-permute-done((f32[9,128,128]{2,1,0:T(8,128)S(1)}, f32[9,128,128]{2,1,0:T(8,128)S(1)}, u32[]{:S(2)}, u32[]{:S(2)}) %collective-permute-start.1) | collective-permute-done | bytes 589856 | tf_op jit(solution)/shard_map/ppermute | solution.py:432
  134.6 0.3 collective-permute-done
  135.0 0.5 copy-done.13
  135.5 0.3 copy-done.14
  135.8 1.6 pad_maximum_fusion._.own_ref
  137.4 4.3 %collective-permute-start.3 = (f32[4,9,128,128]{3,2,1,0:T(8,128)S(1)}, f32[4,9,128,128]{3,2,1,0:T(8,128)}, u32[]{:S(2)}, u32[]{:S(2)}) collective-permute-start(f32[4,9,128,128]{3,2,1,0:T(8,128)S(1)} %pad_maximum_fusion._.own_ref), channel_id=1, source_target_pairs={{0,1},{1,0},{2,3},{3,2},{4,5},{5,4},{6,7},{7,6},{8,9},{9,8},{10,11... | collective-permute-start | bytes 7077896 | tf_op jit(solution)/shard_map/ppermute | solution.py:436
  141.7 1.2 step_after.3.place_ref
  142.9 2.8 %collective-permute-done.3.other_ref = f32[4,9,128,128]{3,2,1,0:T(8,128)} collective-permute-done((f32[4,9,128,128]{3,2,1,0:T(8,128)S(1)}, f32[4,9,128,128]{3,2,1,0:T(8,128)}, u32[]{:S(2)}, u32[]{:S(2)}) %collective-permute-start.3) | collective-permute-done | bytes 2359328 | tf_op jit(solution)/shard_map/ppermute | solution.py:436
  145.7 1.7 copy-done.1
  147.4 0.7 copy-done.2
  148.1 56.8 %factor.1 = (f32[1024,1024]{1,0:T(8,128)S(1)}, f32[256,1024]{1,0:T(8,128)S(1)}) custom-call(s32[2]{0:T(128)S(1)} %copy-done.2, s32[2,40]{1,0:T(2,128)S(1)} %copy-done.4, f32[4,9,128,128]{3,2,1,0:T(8,128)S(1)} %copy-done.1, f32[4,9,128,128]{3,2,1,0:T(8,128)} %collective-permute-done.3.other_ref), custom_call_target="tpu_custom_call" | custom-call | flops 1000000 | bytes 1024 | tf_op jit(solution)/shard_map/factor/pallas_call | solution.py:247
  204.9 7.1 %solve.1 = (f32[512,1024]{1,0:T(8,128)S(1)}, f32[512,1024]{1,0:T(8,128)S(1)}) custom-call(s32[2]{0:T(128)S(1)} %copy-done.2, f32[4,9,128,128]{3,2,1,0:T(8,128)S(1)} %copy-done.1, f32[4,9,128,128]{3,2,1,0:T(8,128)} %collective-permute-done.3.other_ref, f32[256,1024]{1,0:T(8,128)S(1)} %get-tuple-element.22.mine_ref, f32[1024,1024]{1,0:T(8,128)S(1)} %get-tuple-element.23.inverse_ref), custom_call_target="tpu_custom_call" | custom-call | flops 1000000 | bytes 1024 | tf_op jit(solution)/shard_map/solve/pallas_call | solution.py:299
  212.0 1.4 copy-done.6
  213.3 18.6 %all-gather.3.cloned.1.call-done = f32[128,8,1024]{2,1,0:T(8,128)} async-done(((f32[8,8,1024]{2,1,0:T(8,128)}), f32[128,8,1024]{2,1,0:T(8,128)}) %all-gather.3.cloned.1.call-update) | async-done | bytes 4194320 | tf_op jit(solution)/shard_map/all_gather | solution.py:416
  232.0 7.2 %all-to-all-done.3 = f32[128,4,8,128]{3,2,1,0:T(8,128)} async-done(((f32[128,4,8,128]{3,2,1,0:T(8,128)}), f32[128,4,8,128]{3,2,1,0:T(8,128)}, u32[]{:S(2)}, u32[]{:S(2)}) %all-to-all-start.3) | async-done | bytes 2097184 | tf_op jit(solution)/shard_map/all_to_all | solution.py:428
  239.2 2.2 copy-done.5
  241.4 1.6 copy-done.7
  243.0 8.3 %finish.1 = f32[4096,128]{1,0:T(8,128)} custom-call(s32[2]{0:T(128)S(1)} %copy-done.3, f32[4096,128]{1,0:T(8,128)} %bitcast.32.tiles_ref, f32[512,1024]{1,0:T(8,128)S(1)} %copy-done.7, f32[16,8,8,1024]{3,2,1,0:T(8,128)S(1)} %bitcast.72, f32[512,1024]{1,0:T(8,128)S(1)} %get-tuple-element.26.solved_ref, f32[32,1,256]{2,1,0:T(1,128)S(1)} %broadcast_in_dim_squeeze.3.boost_ref), custom_call_target="tpu_custom_call" | custom-call | flops 4000000000 | bytes 12582912 | tf_op jit(solution)/shard_map/finish/pallas_call | solution.py:347
  (44 shorter events, 0.3 us)
Async XLA Ops:
  7.3 2.5 copy-start.18
  9.8 6.8 %copy-start.9 = (f32[1,2,2,1,1,16,8,4,256]{8,7,6,5,4,3,2,1,0:T(4,128)S(1)}, f32[1,2,2,1,1,16,8,4,256]{8,7,6,5,4,3,2,1,0:T(4,128)}, u32[]{:S(2)}) copy-start(f32[1,2,2,1,1,16,8,4,256]{8,7,6,5,4,3,2,1,0:T(4,128)} %param.7) | copy-start | bytes 6291460
  9.8 15.7 %all-to-all-start = ((f32[4,24,24,128]{3,2,1,0:T(8,128)}), f32[4,24,24,128]{3,2,1,0:T(8,128)S(1)}, u32[]{:S(2)}, u32[]{:S(2)}) async-start(f32[4,24,24,128]{3,2,1,0:T(8,128)} %select_reduce_fusion), calls=%async_computation | async-start | bytes 2359296 | tf_op jit(solution)/shard_map/all_to_all | solution.py:392
  16.5 1.5 copy-start.17
  16.5 4.4 %copy-start.12 = (f32[64,8,128]{2,1,0:T(8,128)S(1)}, f32[64,8,128]{2,1,0:T(8,128)}, u32[]{:S(2)}) copy-start(f32[64,8,128]{2,1,0:T(8,128)} %broadcast_in_dim.168) | copy-start | bytes 786436
  25.4 1.0 copy-start.8
  29.3 17.7 %all-to-all-start.1 = ((f32[8,8,8,128]{3,2,1,0:T(8,128)}), f32[8,8,8,128]{3,2,1,0:T(8,128)S(1)}, u32[]{:S(2)}, u32[]{:S(2)}) async-start(f32[8,8,8,128]{3,2,1,0:T(8,128)} %get-tuple-element.17), calls=%async_computation.1 | async-start | bytes 524288 | tf_op jit(solution)/shard_map/all_to_all | solution.py:413
  40.5 25.3 %copy-start.15 = (f32[1,32,256]{2,1,0:T(8,128)S(1)}, f32[1,32,256]{2,1,0:T(8,128)}, u32[]{:S(2)}) copy-start(f32[1,32,256]{2,1,0:T(8,128)} %param.9) | copy-start | bytes 98308
  40.5 26.3 %copy-start.16 = (s32[4,12]{1,0:T(4,128)S(1)}, s32[4,12]{1,0:T(4,128)}, u32[]{:S(2)}) copy-start(s32[4,12]{1,0:T(4,128)} %broadcast_select_fusion.2.index_ref) | copy-start | bytes 580
  47.1 51.9 %all-to-all-start.2 = ((f32[128,9,1,128]{3,2,1,0:T(1,128)}), f32[128,9,1,128]{3,2,1,0:T(1,128)}, u32[]{:S(2)}, u32[]{:S(2)}) async-start(f32[128,9,1,128]{3,2,1,0:T(1,128)} %bitcast.13), calls=%async_computation.2 | async-start | bytes 1179648 | tf_op jit(solution)/shard_map/all_to_all | solution.py:419
  65.6 166.4 %all-gather.3.cloned.1.call-start = ((), (), s32[]{:S(2)}) async-start(), calls=%async_computation.4 | async-start | bytes 4456448 | tf_op jit(solution)/shard_map/all_gather | solution.py:416
  66.8 1.6 copy-start.10
  100.1 20.6 %copy-start.11 = (f32[128,9,1,128]{3,0,1,2:T(8,128)}, f32[128,9,1,128]{3,0,1,2:T(8,128)S(1)}, u32[]{:S(2)}) copy-start(f32[128,9,1,128]{3,0,1,2:T(8,128)S(1)} %copy.76) | copy-start | bytes 1769476
  100.1 21.8 %collective-permute-start.2 = (f32[9,128,128]{2,1,0:T(8,128)S(1)}, f32[9,128,128]{2,1,0:T(8,128)S(1)}, u32[]{:S(2)}, u32[]{:S(2)}) collective-permute-start(f32[9,128,128]{2,1,0:T(8,128)S(1)} %bitcast.75), channel_id=1, source_target_pairs={{0,4},{1,5},{2,6},{3,7},{4,0},{5,1},{6,2},{7,3},{8,12},{9,13},{10,... | collective-permute-start | bytes 1769480 | tf_op jit(solution)/shard_map/ppermute | solution.py:432
  106.4 28.2 %collective-permute-start.1 = (f32[9,128,128]{2,1,0:T(8,128)S(1)}, f32[9,128,128]{2,1,0:T(8,128)S(1)}, u32[]{:S(2)}, u32[]{:S(2)}) collective-permute-start(f32[9,128,128]{2,1,0:T(8,128)S(1)} %bitcast.76), channel_id=1, source_target_pairs={{0,6},{1,7},{2,0},{3,1},{4,2},{5,3},{6,4},{7,5},{8,14},{9,15},{10,... | collective-permute-start | bytes 1769480 | tf_op jit(solution)/shard_map/ppermute | solution.py:432
  109.7 25.3 %collective-permute-start = (f32[9,128,128]{2,1,0:T(8,128)S(1)}, f32[9,128,128]{2,1,0:T(8,128)S(1)}, u32[]{:S(2)}, u32[]{:S(2)}) collective-permute-start(f32[9,128,128]{2,1,0:T(8,128)S(1)} %bitcast.77), channel_id=1, source_target_pairs={{0,2},{1,3},{2,4},{3,5},{4,6},{5,7},{6,0},{7,1},{8,10},{9,11},{10,... | collective-permute-start | bytes 1769480 | tf_op jit(solution)/shard_map/ppermute | solution.py:432
  111.7 127.6 %all-to-all-start.3 = ((f32[128,4,8,128]{3,2,1,0:T(8,128)}), f32[128,4,8,128]{3,2,1,0:T(8,128)}, u32[]{:S(2)}, u32[]{:S(2)}) async-start(f32[128,4,8,128]{3,2,1,0:T(8,128)} %reshape.182), calls=%async_computation.3 | async-start | bytes 4194304 | tf_op jit(solution)/shard_map/all_to_all | solution.py:428
  134.6 0.8 copy-start.13
  135.0 0.8 copy-start.14
  137.4 4.3 %copy-start = (f32[4,9,128,128]{3,2,1,0:T(8,128)}, f32[4,9,128,128]{3,2,1,0:T(8,128)S(1)}, u32[]{:S(2)}) copy-start(f32[4,9,128,128]{3,2,1,0:T(8,128)S(1)} %pad_maximum_fusion._.own_ref) | copy-start | bytes 7077892
  137.4 8.3 %copy-start.4 = (s32[2,40]{1,0:T(2,128)S(1)}, s32[2,40]{1,0:T(2,128)}, u32[]{:S(2)}) copy-start(s32[2,40]{1,0:T(2,128)} %constant.40.clone.pairs_ref) | copy-start | bytes 964
  137.4 8.3 %collective-permute-start.3 = (f32[4,9,128,128]{3,2,1,0:T(8,128)S(1)}, f32[4,9,128,128]{3,2,1,0:T(8,128)}, u32[]{:S(2)}, u32[]{:S(2)}) collective-permute-start(f32[4,9,128,128]{3,2,1,0:T(8,128)S(1)} %pad_maximum_fusion._.own_ref), channel_id=1, source_target_pairs={{0,1},{1,0},{2,3},{3,2},{4,5},{5,4},{6,7},{7,6},{8,9},{9,8},{10,11... | collective-permute-start | bytes 7077896 | tf_op jit(solution)/shard_map/ppermute | solution.py:436
  145.7 1.7 copy-start.1
  147.4 0.7 copy-start.2
  204.9 34.4 %copy-start.3 = (s32[2]{0:T(128)S(1)}, s32[2]{0:T(128)}, u32[]{:S(2)}) copy-start(s32[2]{0:T(128)} %step_after.3.place_ref) | copy-start | bytes 28
  212.0 1.4 copy-start.6
  239.2 2.2 copy-start.5
  241.4 1.6 copy-start.7
Sparse Core Ops, SparseCore 0:
  78.4 153.5 all-gather.2

commit v8 on v6

--- a/solution.py
+++ b/solution.py
@@ -238,7 +238,7 @@
         in_specs=[SCALARS, SCALARS, WHOLE, WHOLE],
         out_specs=(WHOLE, WHOLE),
         scratch_shapes=[pltpu.VMEM((order, BLOCK), jnp.float32), pltpu.VMEM((order, BLOCK), jnp.float32)],
-        compiler_params=pltpu.CompilerParams(vmem_limit_bytes=40 * 2**20),
+        compiler_params=pltpu.CompilerParams(vmem_limit_bytes=20 * 2**20),
         cost_estimate=pl.CostEstimate(flops=10**6, bytes_accessed=2**10, transcendentals=0),
         name="factor",
     )(place, pairs, own, other)
@@ -287,66 +287,74 @@
         in_specs=[SCALARS, WHOLE, WHOLE, WHOLE, WHOLE],
         out_specs=(WHOLE, WHOLE),
         scratch_shapes=[pltpu.VMEM((order // BLOCK, total, BLOCK), jnp.float32)],
-        compiler_params=pltpu.CompilerParams(vmem_limit_bytes=48 * 2**20),
+        compiler_params=pltpu.CompilerParams(vmem_limit_bytes=20 * 2**20),
         cost_estimate=pl.CostEstimate(flops=10**6, bytes_accessed=2**10, transcendentals=0),
         name="solve",
     )(place, own, other, mine, inverse)
 
 
-def finish_kernel(grid_rows, grid_cols, place_ref, tiles_ref, sides_ref, across_ref, solved_ref, boost_ref, out_ref, line_ref):
-    t = pl.program_id(0)
+def change_kernel(sides_ref, across_ref, change_ref):
+    order = sides_ref.shape[1]
+    across = jnp.concatenate([across_ref[:, u].reshape(BLOCK, order) for u in range(across_ref.shape[1])], axis=0)
+    change_ref[...] = times_parts(parts_of(sides_ref[...]), parts_of(across), ROWS_BY_ROWS)
+
+
+def changes(sides, across, steps, cost):
+    total, order = sides.shape
+    size = across.shape[0] * across.shape[1] * across.shape[2] // steps
+    return pl.pallas_call(
+        change_kernel,
+        grid=(steps,),
+        out_shape=jax.ShapeDtypeStruct((total, steps * size), jnp.float32),
+        in_specs=[
+            pl.BlockSpec((total, order), lambda t: (0, 0)),
+            pl.BlockSpec((across.shape[0], across.shape[1] // steps) + across.shape[2:], lambda t: (0, t, 0, 0)),
+        ],
+        out_specs=pl.BlockSpec((total, size), lambda t: (0, t)),
+        compiler_params=pltpu.CompilerParams(vmem_limit_bytes=20 * 2**20),
+        cost_estimate=pl.CostEstimate(flops=cost, bytes_accessed=2**10, transcendentals=0),
+        name="changes",
+    )(sides, across)
+
+
+def finish_kernel(grid_rows, grid_cols, place_ref, tiles_ref, change_ref, solved_ref, boost_ref, out_ref):
     my_row, my_col = place_ref[0], place_ref[1]
     size = boost_ref.shape[2]
     halves = size // BLOCK
-    local_rows = sides_ref.shape[0] // size
-    lines = tiles_ref.shape[0] // BLOCK
-    per = lines // (local_rows * halves)
-    for u in range(halves):
-        line_ref[u * BLOCK : (u + 1) * BLOCK, :] = across_ref[:, u].reshape(BLOCK, sides_ref.shape[1])
-    change = times_parts(parts_of(sides_ref[...]), parts_of(line_ref[...]), ROWS_BY_ROWS)
+    local_rows = change_ref.shape[0] // size
+    local_cols = change_ref.shape[1] // size
+    per = local_cols * halves
+    lines = local_rows * halves * per
     row = lax.broadcasted_iota(jnp.int32, (BLOCK, BLOCK), 0)
     col = lax.broadcasted_iota(jnp.int32, (BLOCK, BLOCK), 1)
-    in_panel = jnp.logical_and(t == 0, my_col < PANELS)
     for i in range(local_rows):
-        on_diagonal = i * grid_rows + my_row == t * grid_cols + my_col
-        for u in range(halves):
-            for h in range(halves):
+        for t in range(local_cols):
+            on_diagonal = i * grid_rows + my_row == t * grid_cols + my_col
+            for u in range(halves):
                 start = i * size + u * BLOCK
-                value = tiles_ref[pl.ds((i * halves + u) * per + t * halves + h, BLOCK, stride=lines), :]
-                value = value - change[start : start + BLOCK, h * BLOCK : (h + 1) * BLOCK]
-                if u == h:
-                    line = boost_ref[i * grid_rows + my_row][:, h * BLOCK : (h + 1) * BLOCK]
-                    value = value + jnp.where(jnp.logical_and(on_diagonal, row == col), line, 0.0)
-                lane = pl.multiple_of(jnp.minimum(my_col, PANELS - 1) * size + h * BLOCK, BLOCK)
-                value = jnp.where(in_panel, solved_ref[start : start + BLOCK, pl.ds(lane, BLOCK)], value)
-                out_ref[pl.ds(start * per + t * halves + h, BLOCK, stride=per), :] = value
-
-
-def finish(place, tiles, sides, across, solved, boost, grid_rows, grid_cols):
-    order = sides.shape[1]
-    steps = tiles.shape[0] // (sides.shape[0] * (boost.shape[2] // BLOCK))
-
-    def still(*shape):
-        return pl.BlockSpec(shape, lambda t: (0,) * len(shape))
-
+                for h in range(halves):
+                    value = tiles_ref[pl.ds((i * halves + u) * per + t * halves + h, BLOCK, stride=lines), :]
+                    first = t * size + h * BLOCK
+                    value = value - change_ref[start : start + BLOCK, first : first + BLOCK]
+                    if u == h:
+                        line = boost_ref[i * grid_rows + my_row][:, h * BLOCK : (h + 1) * BLOCK]
+                        value = value + jnp.where(jnp.logical_and(on_diagonal, row == col), line, 0.0)
+                    if t == 0:
+                        lane = pl.multiple_of(jnp.minimum(my_col, PANELS - 1) * size + h * BLOCK, BLOCK)
+                        value = jnp.where(my_col < PANELS, solved_ref[start : start + BLOCK, pl.ds(lane, BLOCK)], value)
+                    out_ref[pl.ds(start * per + t * halves + h, BLOCK, stride=per), :] = value
+
+
+def finish(place, tiles, change, solved, boost, grid_rows, grid_cols):
     return pl.pallas_call(
         functools.partial(finish_kernel, grid_rows, grid_cols),
-        grid=(steps,),
         out_shape=jax.ShapeDtypeStruct(tiles.shape, jnp.float32),
-        in_specs=[
-            SCALARS,
-            still(*tiles.shape),
-            still(*sides.shape),
-            pl.BlockSpec((across.shape[0], across.shape[1] // steps) + across.shape[2:], lambda t: (0, t, 0, 0)),
-            still(*solved.shape),
-            still(*boost.shape),
-        ],
-        out_specs=still(*tiles.shape),
-        scratch_shapes=[pltpu.VMEM((boost.shape[2], order), jnp.float32)],
-        compiler_params=pltpu.CompilerParams(vmem_limit_bytes=48 * 2**20),
-        cost_estimate=pl.CostEstimate(flops=4 * 10**9, bytes_accessed=12 * 2**20, transcendentals=0),
+        in_specs=[SCALARS, WHOLE, WHOLE, WHOLE, WHOLE],
+        out_specs=WHOLE,
+        compiler_params=pltpu.CompilerParams(vmem_limit_bytes=16 * 2**20),
+        cost_estimate=pl.CostEstimate(flops=10**6, bytes_accessed=2**10, transcendentals=0),
         name="finish",
-    )(place, tiles, sides, across, solved, boost)
+    )(place, tiles, change, solved, boost)
 
 
 def body(front_entries, child_updates, diag_boost, tile_mask, child_parent, child_index):
@@ -397,7 +405,7 @@
 
     split = lax.all_to_all(split, "col", split_axis=0, concat_axis=0, tiled=True)
     for_cols = jnp.transpose(split, (1, 0, 2, 3)).reshape(local_cols * slices, grid_cols, order)
-    lines, for_cols = lax.optimization_barrier((lines, for_cols))
+    lines, for_cols, arrived = lax.optimization_barrier((lines, for_cols, arrived))
     across = lax.all_gather(for_cols, "row", axis=0)
 
     lines = lines.reshape(grid_rows * grid_cols, -1, 1, BLOCK)
@@ -425,7 +433,8 @@
     other = over_cores(own)
     inverse, mine = factor(place, own, other, order)
     solved, sides = solve(place, own, other, mine, inverse, grid_rows, local_rows)
-    out = finish(place, tiles, sides, across, solved, diag_boost[0][:, None, :], grid_rows, grid_cols)
+    change = changes(sides, across, local_cols, 37 * 10**9)
+    out = finish(place, tiles, change, solved, diag_boost[0][:, None, :], grid_rows, grid_cols)
     return out.reshape(1, local_rows, 1, size, local_cols, 1, size)
 
 

time: 274 us -> 256 us (0.934)
  blocking collectives: 18 us -> 0 us
  starting transfers between devices: 45.8 us -> 54.7 us
  waiting for transfers between devices: 76.9 us -> 69.4 us
  local copies, waits for them, and re-layouts: 21.5 us -> 24.6 us
    all_gather x1, waiting for transfers between devices: 25 us -> 2.89 us  [body(): across = lax.all_gather(for_cols, 'row', axis=0)]
    all_to_all x1 -> x0, blocking collectives: 18 us -> none  [body(): lax.all_to_all(split, 'col', split_axis=0, concat_axis=0, tiled=True)]
    all_to_all x1, waiting for transfers between devices: 17.9 us -> 29.5 us  [body(): lax.all_to_all(lines, ('row', 'col'), split_axis=0, concat_axis=0, tiled=...]
    all_to_all x0 -> x1, starting transfers between devices: none -> 11.2 us  [body(): lax.all_to_all(split, 'col', split_axis=0, concat_axis=0, tiled=True)]
    unnamed x33 -> x29, local copies, waits for them, and re-layouts: 9.11 us -> 13.8 us
    all_to_all x0 -> x1, waiting for transfers between devices: none -> 3.92 us  [body(): lax.all_to_all(split, 'col', split_axis=0, concat_axis=0, tiled=True)]
    pallas_call x1, Pallas kernels: 9.06 us -> 6.31 us  [solve(): pl.pallas_call(functools.partial(solve_kernel, grid_rows), out_shape=(out...]
    pallas_call x1 -> x2, Pallas kernels: 8.37 us -> 8.43 us  [the longest x1 4.54 us: changes(): pl.pallas_call(change_kernel, grid=(steps,), out_shape=jax.ShapeDtypeStru...]
  transfers between devices with their start and end apart: 8 -> 9, of which waited for: 7 -> 7; matrix products, arithmetic and copies ran while one was open for 9% -> 9% of each run, Pallas kernels for 24% -> 27%
where the time goes in v8:
time: 256 us; the launch traced here: 253 us
  Pallas kernels  74.4 us (29%)
  waiting for transfers between devices  69.4 us (27%)
  starting transfers between devices  54.7 us (21%)
  local copies, waits for them, and re-layouts  24.6 us (10%)
  between operations  13.6 us (5%)
  matrix products  8.6 us (3%)
  other arithmetic  7.22 us (3%)
    pallas_call x1, Pallas kernels, factor(): pl.pallas_call(factor_kernel, out_shape=(jax.ShapeDtypeStruct((order, ord...  56.7 us
    all_to_all x1, waiting for transfers between devices, body(): lax.all_to_all(lines, ('row', 'col'), split_axis=0, concat_axis=0, tiled=...  29.5 us
    ppermute x3, waiting for transfers between devices, over_chips(): lax.ppermute(value, 'col', [(c, (c + 2 * d) % grid_cols) for c in cols])  27.3 us
    all_to_all x1, starting transfers between devices, body(): lax.all_to_all(lines, ('row', 'col'), split_axis=0, concat_axis=0, tiled=...  18.1 us
    unnamed x29, local copies, waits for them, and re-layouts  13.8 us
    all_to_all x1, starting transfers between devices, body(): lax.all_to_all(split, 'col', split_axis=0, concat_axis=0, tiled=True)  11.2 us
    ppermute x3, starting transfers between devices, over_chips(): lax.ppermute(value, 'col', [(c, (c + 2 * d) % grid_cols) for c in cols])  10.1 us
    all_to_all x1, starting transfers between devices, body(): lax.all_to_all(joined, ('row', 'col'), split_axis=0, concat_axis=0, tiled...  7.1 us
  transfers between devices with their start and end apart: 9, of which 7 were waited for; matrix products, arithmetic and copies ran while one was open for 9% of the time, Pallas kernels for 27%

profile of v8, /device:TPU:1, one launch (start us, length us, event | category | flops | bytes accessed | tf_op | source)
XLA Modules:
  0.0 252.5 jit_solution(6109114636618530086)
XLA Ops:
  6.5 0.7 reshape.174
  7.3 0.6 copy-done.13
  7.9 2.5 select_reduce_fusion
  10.3 5.0 %all-to-all-start = ((f32[4,24,24,128]{3,2,1,0:T(8,128)}), f32[4,24,24,128]{3,2,1,0:T(8,128)S(1)}, u32[]{:S(2)}, u32[]{:S(2)}) async-start(f32[4,24,24,128]{3,2,1,0:T(8,128)} %select_reduce_fusion), calls=%async_computation | async-start | bytes 2359296 | tf_op jit(solution)/shard_map/all_to_all | solution.py:385
  15.3 0.7 slice_bitcast_fusion
  16.0 0.1 iota_compare_fusion.2
  16.1 0.1 broadcast_select_fusion.1
  16.3 0.8 broadcast_in_dim.168
  17.1 1.2 copy.75
  18.3 0.2 copy.52
  18.5 0.8 squeeze.9
  19.3 0.1 broadcast_in_dim.158
  19.4 0.1 broadcast_in_dim.159
  19.5 0.1 eq.103
  19.6 0.1 copy.64
  19.7 0.1 broadcast_in_dim.155
  19.8 0.1 copy.50
  19.9 0.8 fusion.14
  20.7 0.8 select_reduce_fusion.1
  21.5 0.7 broadcast_select_fusion.2.index_ref
  22.2 1.9 select_add_fusion.base_ref
  24.1 1.9 all-to-all-done
  26.0 1.0 copy-done.8
  27.0 2.9 %panel.1 = (f32[1152,1,128]{2,1,0:T(1,128)}, f32[8,8,8,128]{3,2,1,0:T(8,128)}) custom-call(s32[4,12]{1,0:T(4,128)} %broadcast_select_fusion.2.index_ref, f32[64,8,128]{2,1,0:T(8,128)} %select_add_fusion.base_ref, f32[96,24,128]{2,1,0:T(8,128)} %bitcast.74), custom_call_target="tpu_custom_call" | custom-call | flops 1000000 | bytes 2097152 | tf_op jit(solution)/shard_map/panel/pallas_call | solution.py:146
  29.9 11.2 %all-to-all-start.1 = ((f32[8,8,8,128]{3,2,1,0:T(8,128)}), f32[8,8,8,128]{3,2,1,0:T(8,128)S(1)}, u32[]{:S(2)}, u32[]{:S(2)}) async-start(f32[8,8,8,128]{3,2,1,0:T(8,128)} %get-tuple-element.17), calls=%async_computation.1 | async-start | bytes 524288 | tf_op jit(solution)/shard_map/all_to_all | solution.py:406
  41.2 2.6 %reshape.179 = f32[4,12,2,12,256]{4,3,2,1,0:T(8,128)} reshape(f32[4,24,24,128]{3,2,1,0:T(8,128)} %copy-done.8) | data formatting | bytes 2359296 | tf_op jit(solution)/shard_map/reshape | solution.py:386
  43.7 3.9 %all-to-all-done.1 = f32[8,8,8,128]{3,2,1,0:T(8,128)S(1)} async-done(((f32[8,8,8,128]{3,2,1,0:T(8,128)}), f32[8,8,8,128]{3,2,1,0:T(8,128)S(1)}, u32[]{:S(2)}, u32[]{:S(2)}) %all-to-all-start.1) | async-done | bytes 262176 | tf_op jit(solution)/shard_map/all_to_all | solution.py:406
  47.7 0.9 copy.57
  48.6 0.0 all-gather.3.cloned.1.call-update
  48.6 18.1 %all-to-all-start.2 = ((f32[128,9,1,128]{3,2,1,0:T(1,128)}), f32[128,9,1,128]{3,2,1,0:T(1,128)S(1)}, u32[]{:S(2)}, u32[]{:S(2)}) async-start(f32[128,9,1,128]{3,2,1,0:T(1,128)} %bitcast.84), calls=%async_computation.2 | async-start | bytes 1179648 | tf_op jit(solution)/shard_map/all_to_all | solution.py:412
  66.7 0.1 copy.54
  66.9 0.1 iota_add_fusion.1
  66.9 0.1 iota_add_fusion
  67.0 0.0 copy-done.11
  67.0 2.9 %convolution_bitcast_fusion = f32[4,12,2,4,8,256,1]{5,4,2,1,3,0,6:T(8,128)S(1)} fusion(f32[4,12,2,12,256]{4,3,2,1,0:T(8,128)} %reshape.179, s32[4,8]{1,0:T(4,128)S(1)} %iota_add_fusion, s32[4,12]{1,0:T(4,128)S(1)} %copy-done.11), kind=kOutput, calls=%fused_computation.7 | convolution fusion | flops 113247744 | bytes 4325696 | tf_op jit(solution)/shard_map/naube,ntpb->nautpe/dot_general | solution.py:415
  69.9 5.7 %fusion.2 = f32[16,8,2,2,4,256]{5,0,2,1,4,3:T(8,128)S(1)} fusion(f32[4,12,2,4,8,256,1]{5,4,2,1,3,0,6:T(8,128)S(1)} %convolution_bitcast_fusion, pred[2,16,8,4]{1,0,2,3:T(4,128)(4,1)S(1)} %copy.54, s32[2,16]{1,0:T(2,128)S(1)} %iota_add_fusion.1, s32[4,12]{1,0:T(4,128)S(1)} %copy-done.11, f32[1,2,2,1,1,16,8,4,256]{8,7,6,5,4,3,2,1,0:T(4,128)S(1)} %copy-done.9), kind=kOutput, calls=%fused_computation.5 | convolution fusion | flops 303040000 | bytes 7341376 | tf_op jit(solution)/shard_map/niqa,nautpe->iuqpte/dot_general | solution.py:416
  75.6 1.4 copy.56
  77.0 1.8 reshape.182
  78.8 29.5 %all-to-all-done.2 = f32[128,9,1,128]{3,2,1,0:T(1,128)S(1)} async-done(((f32[128,9,1,128]{3,2,1,0:T(1,128)}), f32[128,9,1,128]{3,2,1,0:T(1,128)S(1)}, u32[]{:S(2)}, u32[]{:S(2)}) %all-to-all-start.2) | async-done | bytes 589856 | tf_op jit(solution)/shard_map/all_to_all | solution.py:412
  108.4 7.1 %all-to-all-start.3 = ((f32[128,4,8,128]{3,2,1,0:T(8,128)}), f32[128,4,8,128]{3,2,1,0:T(8,128)S(1)}, u32[]{:S(2)}, u32[]{:S(2)}) async-start(f32[128,4,8,128]{3,2,1,0:T(8,128)} %reshape.182), calls=%async_computation.3 | async-start | bytes 4194304 | tf_op jit(solution)/shard_map/all_to_all | solution.py:421
  115.5 4.8 %collective-permute-start.2 = (f32[9,128,128]{2,1,0:T(8,128)S(1)}, f32[9,128,128]{2,1,0:T(8,128)S(1)}, u32[]{:S(2)}, u32[]{:S(2)}) collective-permute-start(f32[9,128,128]{2,1,0:T(8,128)S(1)} %bitcast.76), channel_id=1, source_target_pairs={{0,4},{1,5},{2,6},{3,7},{4,0},{5,1},{6,2},{7,3},{8,12},{9,13},{10,... | collective-permute-start | bytes 1769480 | tf_op jit(solution)/shard_map/ppermute | solution.py:425
  120.3 2.8 %collective-permute-start.1 = (f32[9,128,128]{2,1,0:T(8,128)S(1)}, f32[9,128,128]{2,1,0:T(8,128)S(1)}, u32[]{:S(2)}, u32[]{:S(2)}) collective-permute-start(f32[9,128,128]{2,1,0:T(8,128)S(1)} %bitcast.77), channel_id=1, source_target_pairs={{0,6},{1,7},{2,0},{3,1},{4,2},{5,3},{6,4},{7,5},{8,14},{9,15},{10,... | collective-permute-start | bytes 1769480 | tf_op jit(solution)/shard_map/ppermute | solution.py:425
  123.1 2.5 collective-permute-start
  125.6 10.2 %collective-permute-done.2 = f32[9,128,128]{2,1,0:T(8,128)S(1)} collective-permute-done((f32[9,128,128]{2,1,0:T(8,128)S(1)}, f32[9,128,128]{2,1,0:T(8,128)S(1)}, u32[]{:S(2)}, u32[]{:S(2)}) %collective-permute-start.2) | collective-permute-done | bytes 589856 | tf_op jit(solution)/shard_map/ppermute | solution.py:425
  135.8 17.2 %collective-permute-done.1 = f32[9,128,128]{2,1,0:T(8,128)S(1)} collective-permute-done((f32[9,128,128]{2,1,0:T(8,128)S(1)}, f32[9,128,128]{2,1,0:T(8,128)S(1)}, u32[]{:S(2)}, u32[]{:S(2)}) %collective-permute-start.1) | collective-permute-done | bytes 589856 | tf_op jit(solution)/shard_map/ppermute | solution.py:425
  152.9 0.0 collective-permute-done
  152.9 0.2 pad_maximum_fusion.own_ref
  153.1 3.2 %collective-permute-start.3 = (f32[4,9,128,128]{3,2,1,0:T(8,128)S(1)}, f32[4,9,128,128]{3,2,1,0:T(8,128)S(1)}, u32[]{:S(2)}, u32[]{:S(2)}) collective-permute-start(f32[4,9,128,128]{3,2,1,0:T(8,128)S(1)} %pad_maximum_fusion.own_ref), channel_id=1, source_target_pairs={{0,1},{1,0},{2,3},{3,2},{4,5},{5,4},{6,7},{7,6},{8,9},{9,8},{10,11... | collective-permute-start | bytes 7077896 | tf_op jit(solution)/shard_map/ppermute | solution.py:429
  156.4 0.1 pad_add_fusion.place_ref
  156.5 3.8 %collective-permute-done.3.other_ref = f32[4,9,128,128]{3,2,1,0:T(8,128)S(1)} collective-permute-done((f32[4,9,128,128]{3,2,1,0:T(8,128)S(1)}, f32[4,9,128,128]{3,2,1,0:T(8,128)S(1)}, u32[]{:S(2)}, u32[]{:S(2)}) %collective-permute-start.3) | collective-permute-done | bytes 2359328 | tf_op jit(solution)/shard_map/ppermute | solution.py:429
  160.3 56.7 %factor.1 = (f32[1024,1024]{1,0:T(8,128)S(1)}, f32[256,1024]{1,0:T(8,128)S(1)}) custom-call(s32[2]{0:T(128)S(1)} %pad_add_fusion.place_ref, s32[2,40]{1,0:T(2,128)S(1)} %copy-done.4, f32[4,9,128,128]{3,2,1,0:T(8,128)S(1)} %pad_maximum_fusion.own_ref, f32[4,9,128,128]{3,2,1,0:T(8,128)S(1)} %collective-permute-done.3.other_ref), custom_call_target="tpu_custom_call" | custom-call | flops 1000000 | bytes 1024 | tf_op jit(solution)/shard_map/factor/pallas_call | solution.py:232
  217.0 6.3 %solve.1 = (f32[512,1024]{1,0:T(8,128)S(1)}, f32[512,1024]{1,0:T(8,128)S(1)}) custom-call(s32[2]{0:T(128)S(1)} %pad_add_fusion.place_ref, f32[4,9,128,128]{3,2,1,0:T(8,128)S(1)} %pad_maximum_fusion.own_ref, f32[4,9,128,128]{3,2,1,0:T(8,128)S(1)} %collective-permute-done.3.other_ref, f32[256,1024]{1,0:T(8,128)S(1)} %get-tuple-element.22.mine_ref, ...), custom_call_target="tpu_custom_call" | custom-call | flops 1000000 | bytes 1024 | tf_op jit(solution)/shard_map/solve/pallas_call | solution.py:284
  223.3 0.0 copy-start
  223.3 1.3 copy-done
  224.7 1.4 copy-done.6
  226.0 2.9 %all-gather.3.cloned.1.call-done = f32[128,8,1024]{2,1,0:T(8,128)} async-done(((f32[8,8,1024]{2,1,0:T(8,128)}), f32[128,8,1024]{2,1,0:T(8,128)}) %all-gather.3.cloned.1.call-update) | async-done | bytes 4194320 | tf_op jit(solution)/shard_map/all_gather | solution.py:409
  228.9 2.2 copy-done.5
  231.1 1.6 copy-done.7
  232.7 4.5 %changes.1.change_ref = f32[512,1024]{1,0:T(8,128)S(1)} custom-call(f32[512,1024]{1,0:T(8,128)S(1)} %copy-done.7, f32[16,8,8,1024]{3,2,1,0:T(8,128)S(1)} %bitcast.73), custom_call_target="tpu_custom_call" | custom-call | flops 36999999488 | bytes 1024 | tf_op jit(solution)/shard_map/changes/pallas_call | solution.py:305
  237.3 1.3 copy-done.2
  238.6 0.0 all-to-all-done.3
  238.6 1.6 copy-done.1
  240.2 1.6 copy-done.3
  241.8 3.9 %finish.1 = f32[4096,128]{1,0:T(8,128)} custom-call(s32[2]{0:T(128)S(1)} %pad_add_fusion.place_ref, f32[4096,128]{1,0:T(8,128)S(1)} %bitcast.72, f32[512,1024]{1,0:T(8,128)S(1)} %copy-done.3, f32[512,1024]{1,0:T(8,128)S(1)} %copy-done.1, f32[32,1,256]{2,1,0:T(1,128)S(1)} %broadcast_in_dim_squeeze.3.boost_ref), custom_call_target="tpu_custom_call" | custom-call | flops 1000000 | bytes 1024 | tf_op jit(solution)/shard_map/finish/pallas_call | solution.py:349
  (33 shorter events, 0.3 us)
Async XLA Ops:
  7.3 0.6 copy-start.13
  10.3 6.8 %copy-start.9 = (f32[1,2,2,1,1,16,8,4,256]{8,7,6,5,4,3,2,1,0:T(4,128)S(1)}, f32[1,2,2,1,1,16,8,4,256]{8,7,6,5,4,3,2,1,0:T(4,128)}, u32[]{:S(2)}) copy-start(f32[1,2,2,1,1,16,8,4,256]{8,7,6,5,4,3,2,1,0:T(4,128)} %param.7) | copy-start | bytes 6291460
  10.3 15.7 %all-to-all-start = ((f32[4,24,24,128]{3,2,1,0:T(8,128)}), f32[4,24,24,128]{3,2,1,0:T(8,128)S(1)}, u32[]{:S(2)}, u32[]{:S(2)}) async-start(f32[4,24,24,128]{3,2,1,0:T(8,128)} %select_reduce_fusion), calls=%async_computation | async-start | bytes 2359296 | tf_op jit(solution)/shard_map/all_to_all | solution.py:385
  17.1 2.2 copy-start.12
  26.0 1.0 copy-start.8
  29.9 17.7 %all-to-all-start.1 = ((f32[8,8,8,128]{3,2,1,0:T(8,128)}), f32[8,8,8,128]{3,2,1,0:T(8,128)S(1)}, u32[]{:S(2)}, u32[]{:S(2)}) async-start(f32[8,8,8,128]{3,2,1,0:T(8,128)} %get-tuple-element.17), calls=%async_computation.1 | async-start | bytes 524288 | tf_op jit(solution)/shard_map/all_to_all | solution.py:406
  41.2 25.8 %copy-start.11 = (s32[4,12]{1,0:T(4,128)S(1)}, s32[4,12]{1,0:T(4,128)}, u32[]{:S(2)}) copy-start(s32[4,12]{1,0:T(4,128)} %broadcast_select_fusion.2.index_ref) | copy-start | bytes 580
  41.2 187.7 %all-gather.3.cloned.1.call-start = ((), (), s32[]{:S(2)}) async-start(), calls=%async_computation.4 | async-start | bytes 4456448 | tf_op jit(solution)/shard_map/all_gather | solution.py:409
  48.6 59.7 %all-to-all-start.2 = ((f32[128,9,1,128]{3,2,1,0:T(1,128)}), f32[128,9,1,128]{3,2,1,0:T(1,128)S(1)}, u32[]{:S(2)}, u32[]{:S(2)}) async-start(f32[128,9,1,128]{3,2,1,0:T(1,128)} %bitcast.84), calls=%async_computation.2 | async-start | bytes 1179648 | tf_op jit(solution)/shard_map/all_to_all | solution.py:412
  108.4 130.2 %all-to-all-start.3 = ((f32[128,4,8,128]{3,2,1,0:T(8,128)}), f32[128,4,8,128]{3,2,1,0:T(8,128)S(1)}, u32[]{:S(2)}, u32[]{:S(2)}) async-start(f32[128,4,8,128]{3,2,1,0:T(8,128)} %reshape.182), calls=%async_computation.3 | async-start | bytes 4194304 | tf_op jit(solution)/shard_map/all_to_all | solution.py:421
  115.5 20.3 %collective-permute-start.2 = (f32[9,128,128]{2,1,0:T(8,128)S(1)}, f32[9,128,128]{2,1,0:T(8,128)S(1)}, u32[]{:S(2)}, u32[]{:S(2)}) collective-permute-start(f32[9,128,128]{2,1,0:T(8,128)S(1)} %bitcast.76), channel_id=1, source_target_pairs={{0,4},{1,5},{2,6},{3,7},{4,0},{5,1},{6,2},{7,3},{8,12},{9,13},{10,... | collective-permute-start | bytes 1769480 | tf_op jit(solution)/shard_map/ppermute | solution.py:425
  120.3 32.6 %collective-permute-start.1 = (f32[9,128,128]{2,1,0:T(8,128)S(1)}, f32[9,128,128]{2,1,0:T(8,128)S(1)}, u32[]{:S(2)}, u32[]{:S(2)}) collective-permute-start(f32[9,128,128]{2,1,0:T(8,128)S(1)} %bitcast.77), channel_id=1, source_target_pairs={{0,6},{1,7},{2,0},{3,1},{4,2},{5,3},{6,4},{7,5},{8,14},{9,15},{10,... | collective-permute-start | bytes 1769480 | tf_op jit(solution)/shard_map/ppermute | solution.py:425
  123.1 29.8 %collective-permute-start = (f32[9,128,128]{2,1,0:T(8,128)S(1)}, f32[9,128,128]{2,1,0:T(8,128)S(1)}, u32[]{:S(2)}, u32[]{:S(2)}) collective-permute-start(f32[9,128,128]{2,1,0:T(8,128)S(1)} %bitcast.78), channel_id=1, source_target_pairs={{0,2},{1,3},{2,4},{3,5},{4,6},{5,7},{6,0},{7,1},{8,10},{9,11},{10,... | collective-permute-start | bytes 1769480 | tf_op jit(solution)/shard_map/ppermute | solution.py:425
  152.9 3.4 %copy-start.10 = (f32[1,32,256]{2,1,0:T(8,128)S(1)}, f32[1,32,256]{2,1,0:T(8,128)}, u32[]{:S(2)}) copy-start(f32[1,32,256]{2,1,0:T(8,128)} %param.9) | copy-start | bytes 98308
  152.9 7.3 %copy-start.4 = (s32[2,40]{1,0:T(2,128)S(1)}, s32[2,40]{1,0:T(2,128)}, u32[]{:S(2)}) copy-start(s32[2,40]{1,0:T(2,128)} %constant.40.clone.pairs_ref) | copy-start | bytes 964
  153.1 7.2 %collective-permute-start.3 = (f32[4,9,128,128]{3,2,1,0:T(8,128)S(1)}, f32[4,9,128,128]{3,2,1,0:T(8,128)S(1)}, u32[]{:S(2)}, u32[]{:S(2)}) collective-permute-start(f32[4,9,128,128]{3,2,1,0:T(8,128)S(1)} %pad_maximum_fusion.own_ref), channel_id=1, source_target_pairs={{0,1},{1,0},{2,3},{3,2},{4,5},{5,4},{6,7},{7,6},{8,9},{9,8},{10,11... | collective-permute-start | bytes 7077896 | tf_op jit(solution)/shard_map/ppermute | solution.py:429
  223.3 1.3 copy-start
  224.7 1.4 copy-start.6
  228.9 2.2 copy-start.5
  231.1 1.6 copy-start.7
  237.2 1.3 copy-start.2
  238.6 1.6 copy-start.1
  240.2 1.6 copy-start.3
Sparse Core Ops, SparseCore 0:
  48.7 180.1 all-gather.2

commit v9 on v8

--- a/solution.py
+++ b/solution.py
@@ -244,7 +244,9 @@
     )(place, pairs, own, other)
 
 
-def solve_kernel(grid_rows, place_ref, own_ref, other_ref, mine_ref, inverse_ref, solved_ref, sides_ref, rows_ref):
+def solve_kernel(
+    grid_rows, place_ref, own_ref, other_ref, mine_ref, inverse_ref, solved_out, sides_out, solved_ref, sides_ref, rows_ref, sems
+):
     total, order = solved_ref.shape
     size = order // PANELS
     per = size // BLOCK
@@ -269,6 +271,8 @@
     def _():
         solved_ref[0:size, :] = mine_ref[...]
 
+    first = pltpu.make_async_copy(solved_ref, solved_out, sems.at[0])
+    first.start()
     tile = lax.broadcasted_iota(jnp.int32, (total, size), 0) // size * grid_rows + my_row
     used = [parts_of(jnp.where(tile > k, solved_ref[:, k * size : (k + 1) * size], 0.0)) for k in range(PANELS)]
     for j in range(PANELS):
@@ -276,6 +280,10 @@
         for k in range(j + 1, PANELS):
             total_j = total_j + times_parts(used[k], inverse[j][k], ROWS_BY_ROWS)
         sides_ref[:, j * size : (j + 1) * size] = total_j
+    second = pltpu.make_async_copy(sides_ref, sides_out, sems.at[1])
+    second.start()
+    first.wait()
+    second.wait()
 
 
 def solve(place, own, other, mine, inverse, grid_rows, local_rows):
@@ -285,8 +293,13 @@
         functools.partial(solve_kernel, grid_rows),
         out_shape=(out, out),
         in_specs=[SCALARS, WHOLE, WHOLE, WHOLE, WHOLE],
-        out_specs=(WHOLE, WHOLE),
-        scratch_shapes=[pltpu.VMEM((order // BLOCK, total, BLOCK), jnp.float32)],
+        out_specs=(pl.BlockSpec(memory_space=pltpu.HBM),) * 2,
+        scratch_shapes=[
+            pltpu.VMEM((total, order), jnp.float32),
+            pltpu.VMEM((total, order), jnp.float32),
+            pltpu.VMEM((order // BLOCK, total, BLOCK), jnp.float32),
+            pltpu.SemaphoreType.DMA((2,)),
+        ],
         compiler_params=pltpu.CompilerParams(vmem_limit_bytes=20 * 2**20),
         cost_estimate=pl.CostEstimate(flops=10**6, bytes_accessed=2**10, transcendentals=0),
         name="solve",
@@ -311,7 +324,7 @@
             pl.BlockSpec((across.shape[0], across.shape[1] // steps) + across.shape[2:], lambda t: (0, t, 0, 0)),
         ],
         out_specs=pl.BlockSpec((total, size), lambda t: (0, t)),
-        compiler_params=pltpu.CompilerParams(vmem_limit_bytes=20 * 2**20),
+        compiler_params=pltpu.CompilerParams(vmem_limit_bytes=60 * 2**20),
         cost_estimate=pl.CostEstimate(flops=cost, bytes_accessed=2**10, transcendentals=0),
         name="changes",
     )(sides, across)
@@ -321,40 +334,50 @@
     my_row, my_col = place_ref[0], place_ref[1]
     size = boost_ref.shape[2]
     halves = size // BLOCK
-    local_rows = change_ref.shape[0] // size
-    local_cols = change_ref.shape[1] // size
+    bands, count, order = change_ref.shape
+    local_cols = order // size
     per = local_cols * halves
-    lines = local_rows * halves * per
-    row = lax.broadcasted_iota(jnp.int32, (BLOCK, BLOCK), 0)
-    col = lax.broadcasted_iota(jnp.int32, (BLOCK, BLOCK), 1)
-    for i in range(local_rows):
+    row = lax.broadcasted_iota(jnp.int32, (count, BLOCK), 0) + pl.program_id(0) * count
+    col = lax.broadcasted_iota(jnp.int32, (count, BLOCK), 1)
+    for band in range(bands):
+        i, u = band // halves, band % halves
+        line = boost_ref[i * grid_rows + my_row][:, u * BLOCK : (u + 1) * BLOCK]
         for t in range(local_cols):
             on_diagonal = i * grid_rows + my_row == t * grid_cols + my_col
-            for u in range(halves):
-                start = i * size + u * BLOCK
-                for h in range(halves):
-                    value = tiles_ref[pl.ds((i * halves + u) * per + t * halves + h, BLOCK, stride=lines), :]
-                    first = t * size + h * BLOCK
-                    value = value - change_ref[start : start + BLOCK, first : first + BLOCK]
-                    if u == h:
-                        line = boost_ref[i * grid_rows + my_row][:, h * BLOCK : (h + 1) * BLOCK]
-                        value = value + jnp.where(jnp.logical_and(on_diagonal, row == col), line, 0.0)
-                    if t == 0:
-                        lane = pl.multiple_of(jnp.minimum(my_col, PANELS - 1) * size + h * BLOCK, BLOCK)
-                        value = jnp.where(my_col < PANELS, solved_ref[start : start + BLOCK, pl.ds(lane, BLOCK)], value)
-                    out_ref[pl.ds(start * per + t * halves + h, BLOCK, stride=per), :] = value
-
-
-def finish(place, tiles, change, solved, boost, grid_rows, grid_cols):
-    return pl.pallas_call(
+            for h in range(halves):
+                first = t * size + h * BLOCK
+                value = tiles_ref[pl.ds(band * per + t * halves + h, count, stride=bands * per), :]
+                value = value - change_ref[band, :, first : first + BLOCK]
+                if u == h:
+                    value = value + jnp.where(jnp.logical_and(on_diagonal, row == col), line, 0.0)
+                if t == 0:
+                    lane = pl.multiple_of(jnp.minimum(my_col, PANELS - 1) * size + h * BLOCK, BLOCK)
+                    value = jnp.where(my_col < PANELS, solved_ref[band, :, pl.ds(lane, BLOCK)], value)
+                out_ref[band, pl.ds(t * halves + h, count, stride=per), :] = value
+
+
+def finish(place, tiles, change, solved, boost, grid_rows, grid_cols, steps=4):
+    total, order = change.shape
+    bands, count = total // BLOCK, BLOCK // steps
+    per = order // BLOCK
+    rows = pl.BlockSpec((bands, count, order), lambda s: (0, s, 0))
+    out = pl.pallas_call(
         functools.partial(finish_kernel, grid_rows, grid_cols),
-        out_shape=jax.ShapeDtypeStruct(tiles.shape, jnp.float32),
-        in_specs=[SCALARS, WHOLE, WHOLE, WHOLE, WHOLE],
-        out_specs=WHOLE,
-        compiler_params=pltpu.CompilerParams(vmem_limit_bytes=16 * 2**20),
+        grid=(steps,),
+        out_shape=jax.ShapeDtypeStruct((bands, BLOCK * per, BLOCK), jnp.float32),
+        in_specs=[
+            SCALARS,
+            pl.BlockSpec((count * bands * per, BLOCK), lambda s: (s, 0)),
+            rows,
+            rows,
+            pl.BlockSpec(boost.shape, lambda s: (0, 0, 0)),
+        ],
+        out_specs=pl.BlockSpec((bands, count * per, BLOCK), lambda s: (0, s, 0)),
+        compiler_params=pltpu.CompilerParams(vmem_limit_bytes=60 * 2**20),
         cost_estimate=pl.CostEstimate(flops=10**6, bytes_accessed=2**10, transcendentals=0),
         name="finish",
-    )(place, tiles, change, solved, boost)
+    )(place, tiles, change.reshape(bands, BLOCK, order), solved.reshape(bands, BLOCK, order), boost)
+    return out
 
 
 def body(front_entries, child_updates, diag_boost, tile_mask, child_parent, child_index):

time: 256 us -> 253 us (0.988)
  local copies, waits for them, and re-layouts: 24.6 us -> 18.2 us
  Pallas kernels: 74.4 us -> 78.4 us
    unnamed x29 -> x23, local copies, waits for them, and re-layouts: 13.8 us -> 6.91 us
    pallas_call x1, Pallas kernels: 4.54 us -> 7.38 us  [changes(): pl.pallas_call(change_kernel, grid=(steps,), out_shape=jax.ShapeDtypeStru...]
  transfers between devices with their start and end apart: 9 -> 9, of which waited for: 7 -> 7; matrix products, arithmetic and copies ran while one was open for 9% -> 10% of each run, Pallas kernels for 27% -> 28%
where the time goes in v9:
time: 253 us; the launch traced here: 250 us
  Pallas kernels  78.4 us (31%)
  waiting for transfers between devices  68.9 us (27%)
  starting transfers between devices  54.7 us (22%)
  local copies, waits for them, and re-layouts  18.2 us (7%)
  between operations  13.6 us (5%)
  matrix products  8.6 us (3%)
  other arithmetic  7.22 us (3%)
    pallas_call x1, Pallas kernels, factor(): pl.pallas_call(factor_kernel, out_shape=(jax.ShapeDtypeStruct((order, ord...  56.5 us
    all_to_all x1, waiting for transfers between devices, body(): lax.all_to_all(lines, ('row', 'col'), split_axis=0, concat_axis=0, tiled=...  29.6 us
    ppermute x3, waiting for transfers between devices, over_chips(): lax.ppermute(value, 'col', [(c, (c + 2 * d) % grid_cols) for c in cols])  27.3 us
    all_to_all x1, starting transfers between devices, body(): lax.all_to_all(lines, ('row', 'col'), split_axis=0, concat_axis=0, tiled=...  18.1 us
    all_to_all x1, starting transfers between devices, body(): lax.all_to_all(split, 'col', split_axis=0, concat_axis=0, tiled=True)  11.2 us
    ppermute x3, starting transfers between devices, over_chips(): lax.ppermute(value, 'col', [(c, (c + 2 * d) % grid_cols) for c in cols])  10.1 us
    pallas_call x1, Pallas kernels, changes(): pl.pallas_call(change_kernel, grid=(steps,), out_shape=jax.ShapeDtypeStru...  7.38 us
    all_to_all x1, starting transfers between devices, body(): lax.all_to_all(joined, ('row', 'col'), split_axis=0, concat_axis=0, tiled...  7.09 us
  transfers between devices with their start and end apart: 9, of which 7 were waited for; matrix products, arithmetic and copies ran while one was open for 10% of the time, Pallas kernels for 28%

profile of v9, /device:TPU:1, one launch (start us, length us, event | category | flops | bytes accessed | tf_op | source)
XLA Modules:
  0.0 249.7 jit_solution(4306300944981110605)
XLA Ops:
  6.5 0.7 reshape.180
  7.3 0.6 copy-done.10
  7.9 2.5 select_reduce_fusion
  10.3 5.0 %all-to-all-start = ((f32[4,24,24,128]{3,2,1,0:T(8,128)}), f32[4,24,24,128]{3,2,1,0:T(8,128)S(1)}, u32[]{:S(2)}, u32[]{:S(2)}) async-start(f32[4,24,24,128]{3,2,1,0:T(8,128)} %select_reduce_fusion), calls=%async_computation | async-start | bytes 2359296 | tf_op jit(solution)/shard_map/all_to_all | solution.py:408
  15.3 0.7 slice_bitcast_fusion
  16.0 0.1 iota_compare_fusion.2
  16.1 0.1 broadcast_select_fusion.1
  16.3 0.8 broadcast_in_dim.168
  17.1 0.0 copy-done.5
  17.1 1.2 copy.75
  18.3 0.2 copy.52
  18.5 0.8 squeeze.9
  19.3 0.0 copy-done.9
  19.3 0.1 broadcast_in_dim.158
  19.4 0.1 broadcast_in_dim.159
  19.5 0.1 eq.103
  19.6 0.1 copy.64
  19.7 0.1 broadcast_in_dim.155
  19.8 0.1 copy.50
  19.9 0.8 fusion.14
  20.7 0.8 select_reduce_fusion.1
  21.5 0.7 broadcast_select_fusion.2.index_ref
  22.1 1.9 select_add_fusion.base_ref
  24.1 1.9 all-to-all-done
  26.0 1.0 copy-done.4
  27.0 2.9 %panel.1 = (f32[1152,1,128]{2,1,0:T(1,128)}, f32[8,8,8,128]{3,2,1,0:T(8,128)}) custom-call(s32[4,12]{1,0:T(4,128)} %broadcast_select_fusion.2.index_ref, f32[64,8,128]{2,1,0:T(8,128)} %select_add_fusion.base_ref, f32[96,24,128]{2,1,0:T(8,128)} %bitcast.75), custom_call_target="tpu_custom_call" | custom-call | flops 1000000 | bytes 2097152 | tf_op jit(solution)/shard_map/panel/pallas_call | solution.py:146
  30.0 11.2 %all-to-all-start.1 = ((f32[8,8,8,128]{3,2,1,0:T(8,128)}), f32[8,8,8,128]{3,2,1,0:T(8,128)S(1)}, u32[]{:S(2)}, u32[]{:S(2)}) async-start(f32[8,8,8,128]{3,2,1,0:T(8,128)} %get-tuple-element.17), calls=%async_computation.1 | async-start | bytes 524288 | tf_op jit(solution)/shard_map/all_to_all | solution.py:429
  41.2 0.0 all-gather.3.cloned.1.call-start
  41.2 2.6 %reshape.185 = f32[4,12,2,12,256]{4,3,2,1,0:T(8,128)} reshape(f32[4,24,24,128]{3,2,1,0:T(8,128)} %copy-done.4) | data formatting | bytes 2359296 | tf_op jit(solution)/shard_map/reshape | solution.py:409
  43.8 3.9 %all-to-all-done.1 = f32[8,8,8,128]{3,2,1,0:T(8,128)S(1)} async-done(((f32[8,8,8,128]{3,2,1,0:T(8,128)}), f32[8,8,8,128]{3,2,1,0:T(8,128)S(1)}, u32[]{:S(2)}, u32[]{:S(2)}) %all-to-all-start.1) | async-done | bytes 262176 | tf_op jit(solution)/shard_map/all_to_all | solution.py:429
  47.7 0.9 copy.57
  48.6 0.0 all-gather.3.cloned.1.call-update
  48.6 18.1 %all-to-all-start.2 = ((f32[128,9,1,128]{3,2,1,0:T(1,128)}), f32[128,9,1,128]{3,2,1,0:T(1,128)S(1)}, u32[]{:S(2)}, u32[]{:S(2)}) async-start(f32[128,9,1,128]{3,2,1,0:T(1,128)} %bitcast.87), calls=%async_computation.2 | async-start | bytes 1179648 | tf_op jit(solution)/shard_map/all_to_all | solution.py:435
  66.7 0.1 copy.54
  66.9 0.1 iota_add_fusion.1
  66.9 0.1 iota_add_fusion
  67.0 0.0 copy-done.8
  67.0 2.9 %convolution_bitcast_fusion = f32[4,12,2,4,8,256,1]{5,4,2,1,3,0,6:T(8,128)S(1)} fusion(f32[4,12,2,12,256]{4,3,2,1,0:T(8,128)} %reshape.185, s32[4,8]{1,0:T(4,128)S(1)} %iota_add_fusion, s32[4,12]{1,0:T(4,128)S(1)} %copy-done.8), kind=kOutput, calls=%fused_computation.7 | convolution fusion | flops 113247744 | bytes 4325696 | tf_op jit(solution)/shard_map/naube,ntpb->nautpe/dot_general | solution.py:438
  69.9 5.7 %fusion.2 = f32[16,8,2,2,4,256]{5,0,2,1,4,3:T(8,128)S(1)} fusion(f32[4,12,2,4,8,256,1]{5,4,2,1,3,0,6:T(8,128)S(1)} %convolution_bitcast_fusion, pred[2,16,8,4]{1,0,2,3:T(4,128)(4,1)S(1)} %copy.54, s32[2,16]{1,0:T(2,128)S(1)} %iota_add_fusion.1, s32[4,12]{1,0:T(4,128)S(1)} %copy-done.8, f32[1,2,2,1,1,16,8,4,256]{8,7,6,5,4,3,2,1,0:T(4,128)S(1)} %copy-done.5), kind=kOutput, calls=%fused_computation.5 | convolution fusion | flops 303040000 | bytes 7341376 | tf_op jit(solution)/shard_map/niqa,nautpe->iuqpte/dot_general | solution.py:439
  75.6 1.4 copy.56
  77.0 1.8 reshape.188
  78.8 29.6 %all-to-all-done.2 = f32[128,9,1,128]{3,2,1,0:T(1,128)S(1)} async-done(((f32[128,9,1,128]{3,2,1,0:T(1,128)}), f32[128,9,1,128]{3,2,1,0:T(1,128)S(1)}, u32[]{:S(2)}, u32[]{:S(2)}) %all-to-all-start.2) | async-done | bytes 589856 | tf_op jit(solution)/shard_map/all_to_all | solution.py:435
  108.4 7.1 %all-to-all-start.3 = ((f32[128,4,8,128]{3,2,1,0:T(8,128)}), f32[128,4,8,128]{3,2,1,0:T(8,128)S(1)}, u32[]{:S(2)}, u32[]{:S(2)}) async-start(f32[128,4,8,128]{3,2,1,0:T(8,128)} %reshape.188), calls=%async_computation.3 | async-start | bytes 4194304 | tf_op jit(solution)/shard_map/all_to_all | solution.py:444
  115.5 4.8 %collective-permute-start.2 = (f32[9,128,128]{2,1,0:T(8,128)S(1)}, f32[9,128,128]{2,1,0:T(8,128)S(1)}, u32[]{:S(2)}, u32[]{:S(2)}) collective-permute-start(f32[9,128,128]{2,1,0:T(8,128)S(1)} %bitcast.78), channel_id=1, source_target_pairs={{0,4},{1,5},{2,6},{3,7},{4,0},{5,1},{6,2},{7,3},{8,12},{9,13},{10,... | collective-permute-start | bytes 1769480 | tf_op jit(solution)/shard_map/ppermute | solution.py:448
  120.3 2.8 %collective-permute-start.1 = (f32[9,128,128]{2,1,0:T(8,128)S(1)}, f32[9,128,128]{2,1,0:T(8,128)S(1)}, u32[]{:S(2)}, u32[]{:S(2)}) collective-permute-start(f32[9,128,128]{2,1,0:T(8,128)S(1)} %bitcast.79), channel_id=1, source_target_pairs={{0,6},{1,7},{2,0},{3,1},{4,2},{5,3},{6,4},{7,5},{8,14},{9,15},{10,... | collective-permute-start | bytes 1769480 | tf_op jit(solution)/shard_map/ppermute | solution.py:448
  123.1 2.5 collective-permute-start
  125.6 10.2 %collective-permute-done.2 = f32[9,128,128]{2,1,0:T(8,128)S(1)} collective-permute-done((f32[9,128,128]{2,1,0:T(8,128)S(1)}, f32[9,128,128]{2,1,0:T(8,128)S(1)}, u32[]{:S(2)}, u32[]{:S(2)}) %collective-permute-start.2) | collective-permute-done | bytes 589856 | tf_op jit(solution)/shard_map/ppermute | solution.py:448
  135.8 17.2 %collective-permute-done.1 = f32[9,128,128]{2,1,0:T(8,128)S(1)} collective-permute-done((f32[9,128,128]{2,1,0:T(8,128)S(1)}, f32[9,128,128]{2,1,0:T(8,128)S(1)}, u32[]{:S(2)}, u32[]{:S(2)}) %collective-permute-start.1) | collective-permute-done | bytes 589856 | tf_op jit(solution)/shard_map/ppermute | solution.py:448
  153.0 0.0 collective-permute-done
  153.0 0.2 pad_maximum_fusion.own_ref
  153.1 3.3 %collective-permute-start.3 = (f32[4,9,128,128]{3,2,1,0:T(8,128)S(1)}, f32[4,9,128,128]{3,2,1,0:T(8,128)S(1)}, u32[]{:S(2)}, u32[]{:S(2)}) collective-permute-start(f32[4,9,128,128]{3,2,1,0:T(8,128)S(1)} %pad_maximum_fusion.own_ref), channel_id=1, source_target_pairs={{0,1},{1,0},{2,3},{3,2},{4,5},{5,4},{6,7},{7,6},{8,9},{9,8},{10,11... | collective-permute-start | bytes 7077896 | tf_op jit(solution)/shard_map/ppermute | solution.py:452
  156.4 0.0 copy-done.7
  156.4 0.6 broadcast_in_dim_squeeze.3.boost_ref
  157.0 0.1 pad_add_fusion.place_ref
  157.1 3.2 %collective-permute-done.3.other_ref = f32[4,9,128,128]{3,2,1,0:T(8,128)S(1)} collective-permute-done((f32[4,9,128,128]{3,2,1,0:T(8,128)S(1)}, f32[4,9,128,128]{3,2,1,0:T(8,128)S(1)}, u32[]{:S(2)}, u32[]{:S(2)}) %collective-permute-start.3) | collective-permute-done | bytes 2359328 | tf_op jit(solution)/shard_map/ppermute | solution.py:452
  160.3 56.5 %factor.1 = (f32[1024,1024]{1,0:T(8,128)S(1)}, f32[256,1024]{1,0:T(8,128)S(1)}) custom-call(s32[2]{0:T(128)S(1)} %pad_add_fusion.place_ref, s32[2,40]{1,0:T(2,128)S(1)} %copy-done.2, f32[4,9,128,128]{3,2,1,0:T(8,128)S(1)} %pad_maximum_fusion.own_ref, f32[4,9,128,128]{3,2,1,0:T(8,128)S(1)} %collective-permute-done.3.other_ref), custom_call_target="tpu_custom_call" | custom-call | flops 1000000 | bytes 1024 | tf_op jit(solution)/shard_map/factor/pallas_call | solution.py:232
  216.8 6.3 %solve.1 = (f32[512,1024]{1,0:T(8,128)S(1)}, f32[512,1024]{1,0:T(8,128)S(1)}) custom-call(s32[2]{0:T(128)S(1)} %pad_add_fusion.place_ref, f32[4,9,128,128]{3,2,1,0:T(8,128)S(1)} %pad_maximum_fusion.own_ref, f32[4,9,128,128]{3,2,1,0:T(8,128)S(1)} %collective-permute-done.3.other_ref, f32[256,1024]{1,0:T(8,128)S(1)} %get-tuple-element.22.mine_ref, ...), custom_call_target="tpu_custom_call" | custom-call | flops 1000000 | bytes 1024 | tf_op jit(solution)/shard_map/solve/pallas_call | solution.py:292
  223.2 1.3 copy-done
  224.5 1.4 copy-done.3
  225.9 3.0 %all-gather.3.cloned.1.call-done = f32[128,8,1024]{2,1,0:T(8,128)} async-done(((f32[8,8,1024]{2,1,0:T(8,128)}), f32[128,8,1024]{2,1,0:T(8,128)}) %all-gather.3.cloned.1.call-update) | async-done | bytes 4194320 | tf_op jit(solution)/shard_map/all_gather | solution.py:432
  228.9 7.4 %changes.1 = f32[512,1024]{1,0:T(8,128)} custom-call(f32[512,1024]{1,0:T(8,128)} %copy-done.3, f32[16,8,8,1024]{3,2,1,0:T(8,128)} %bitcast.93), custom_call_target="tpu_custom_call" | custom-call | flops 36999999488 | bytes 1024 | tf_op jit(solution)/shard_map/changes/pallas_call | solution.py:318
  236.3 0.0 all-to-all-done.3
  236.3 1.3 copy-done.6
  237.6 5.3 %finish.1 = f32[4,1024,128]{2,1,0:T(8,128)} custom-call(s32[2]{0:T(128)} %copy-done.1, f32[4096,128]{1,0:T(8,128)} %bitcast.76, f32[4,128,1024]{2,1,0:T(8,128)} %bitcast.82, f32[4,128,1024]{2,1,0:T(8,128)} %bitcast.74, f32[32,1,256]{2,1,0:T(1,128)} %broadcast_in_dim_squeeze.3.boost_ref), custom_call_target="tpu_custom_call" | custom-call | flops 1000000 | bytes 1024 | tf_op jit(solution)/shard_map/finish/pallas_call | solution.py:364
  (27 shorter events, 0.2 us)
Async XLA Ops:
  7.3 0.6 copy-start.10
  10.3 6.7 %copy-start.5 = (f32[1,2,2,1,1,16,8,4,256]{8,7,6,5,4,3,2,1,0:T(4,128)S(1)}, f32[1,2,2,1,1,16,8,4,256]{8,7,6,5,4,3,2,1,0:T(4,128)}, u32[]{:S(2)}) copy-start(f32[1,2,2,1,1,16,8,4,256]{8,7,6,5,4,3,2,1,0:T(4,128)} %param.7) | copy-start | bytes 6291460
  10.3 15.7 %all-to-all-start = ((f32[4,24,24,128]{3,2,1,0:T(8,128)}), f32[4,24,24,128]{3,2,1,0:T(8,128)S(1)}, u32[]{:S(2)}, u32[]{:S(2)}) async-start(f32[4,24,24,128]{3,2,1,0:T(8,128)} %select_reduce_fusion), calls=%async_computation | async-start | bytes 2359296 | tf_op jit(solution)/shard_map/all_to_all | solution.py:408
  17.1 2.2 copy-start.9
  26.0 1.0 copy-start.4
  30.0 17.7 %all-to-all-start.1 = ((f32[8,8,8,128]{3,2,1,0:T(8,128)}), f32[8,8,8,128]{3,2,1,0:T(8,128)S(1)}, u32[]{:S(2)}, u32[]{:S(2)}) async-start(f32[8,8,8,128]{3,2,1,0:T(8,128)} %get-tuple-element.17), calls=%async_computation.1 | async-start | bytes 524288 | tf_op jit(solution)/shard_map/all_to_all | solution.py:429
  41.2 25.8 %copy-start.8 = (s32[4,12]{1,0:T(4,128)S(1)}, s32[4,12]{1,0:T(4,128)}, u32[]{:S(2)}) copy-start(s32[4,12]{1,0:T(4,128)} %broadcast_select_fusion.2.index_ref) | copy-start | bytes 580
  41.2 187.7 %all-gather.3.cloned.1.call-start = ((), (), s32[]{:S(2)}) async-start(), calls=%async_computation.4 | async-start | bytes 4456448 | tf_op jit(solution)/shard_map/all_gather | solution.py:432
  48.6 59.8 %all-to-all-start.2 = ((f32[128,9,1,128]{3,2,1,0:T(1,128)}), f32[128,9,1,128]{3,2,1,0:T(1,128)S(1)}, u32[]{:S(2)}, u32[]{:S(2)}) async-start(f32[128,9,1,128]{3,2,1,0:T(1,128)} %bitcast.87), calls=%async_computation.2 | async-start | bytes 1179648 | tf_op jit(solution)/shard_map/all_to_all | solution.py:435
  108.4 127.8 %all-to-all-start.3 = ((f32[128,4,8,128]{3,2,1,0:T(8,128)}), f32[128,4,8,128]{3,2,1,0:T(8,128)S(1)}, u32[]{:S(2)}, u32[]{:S(2)}) async-start(f32[128,4,8,128]{3,2,1,0:T(8,128)} %reshape.188), calls=%async_computation.3 | async-start | bytes 4194304 | tf_op jit(solution)/shard_map/all_to_all | solution.py:444
  115.5 20.3 %collective-permute-start.2 = (f32[9,128,128]{2,1,0:T(8,128)S(1)}, f32[9,128,128]{2,1,0:T(8,128)S(1)}, u32[]{:S(2)}, u32[]{:S(2)}) collective-permute-start(f32[9,128,128]{2,1,0:T(8,128)S(1)} %bitcast.78), channel_id=1, source_target_pairs={{0,4},{1,5},{2,6},{3,7},{4,0},{5,1},{6,2},{7,3},{8,12},{9,13},{10,... | collective-permute-start | bytes 1769480 | tf_op jit(solution)/shard_map/ppermute | solution.py:448
  120.3 32.6 %collective-permute-start.1 = (f32[9,128,128]{2,1,0:T(8,128)S(1)}, f32[9,128,128]{2,1,0:T(8,128)S(1)}, u32[]{:S(2)}, u32[]{:S(2)}) collective-permute-start(f32[9,128,128]{2,1,0:T(8,128)S(1)} %bitcast.79), channel_id=1, source_target_pairs={{0,6},{1,7},{2,0},{3,1},{4,2},{5,3},{6,4},{7,5},{8,14},{9,15},{10,... | collective-permute-start | bytes 1769480 | tf_op jit(solution)/shard_map/ppermute | solution.py:448
  123.1 29.8 %collective-permute-start = (f32[9,128,128]{2,1,0:T(8,128)S(1)}, f32[9,128,128]{2,1,0:T(8,128)S(1)}, u32[]{:S(2)}, u32[]{:S(2)}) collective-permute-start(f32[9,128,128]{2,1,0:T(8,128)S(1)} %bitcast.80), channel_id=1, source_target_pairs={{0,2},{1,3},{2,4},{3,5},{4,6},{5,7},{6,0},{7,1},{8,10},{9,11},{10,... | collective-permute-start | bytes 1769480 | tf_op jit(solution)/shard_map/ppermute | solution.py:448
  153.0 3.4 %copy-start.7 = (f32[1,32,256]{2,1,0:T(8,128)S(1)}, f32[1,32,256]{2,1,0:T(8,128)}, u32[]{:S(2)}) copy-start(f32[1,32,256]{2,1,0:T(8,128)} %param.9) | copy-start | bytes 98308
  153.0 7.3 %copy-start.2 = (s32[2,40]{1,0:T(2,128)S(1)}, s32[2,40]{1,0:T(2,128)}, u32[]{:S(2)}) copy-start(s32[2,40]{1,0:T(2,128)} %constant.40.clone.pairs_ref) | copy-start | bytes 964
  153.1 7.2 %collective-permute-start.3 = (f32[4,9,128,128]{3,2,1,0:T(8,128)S(1)}, f32[4,9,128,128]{3,2,1,0:T(8,128)S(1)}, u32[]{:S(2)}, u32[]{:S(2)}) collective-permute-start(f32[4,9,128,128]{3,2,1,0:T(8,128)S(1)} %pad_maximum_fusion.own_ref), channel_id=1, source_target_pairs={{0,1},{1,0},{2,3},{3,2},{4,5},{5,4},{6,7},{7,6},{8,9},{9,8},{10,11... | collective-permute-start | bytes 7077896 | tf_op jit(solution)/shard_map/ppermute | solution.py:452
  157.1 59.7 %copy-start.1 = (s32[2]{0:T(128)}, s32[2]{0:T(128)S(1)}, u32[]{:S(2)}) copy-start(s32[2]{0:T(128)S(1)} %pad_add_fusion.place_ref) | copy-start | bytes 28
  223.2 1.3 copy-start
  224.5 1.4 copy-start.3
  236.3 1.3 copy-start.6
Sparse Core Ops, SparseCore 0:
  48.7 180.0 all-gather.2

commit v10 on v9

--- a/solution.py
+++ b/solution.py
@@ -306,10 +306,15 @@
     )(place, own, other, mine, inverse)
 
 
-def change_kernel(sides_ref, across_ref, change_ref):
+def change_kernel(sides_ref, across_ref, change_ref, high_ref, low_ref):
     order = sides_ref.shape[1]
+
+    @pl.when(pl.program_id(0) == 0)
+    def _():
+        high_ref[...], low_ref[...] = parts_of(sides_ref[...])
+
     across = jnp.concatenate([across_ref[:, u].reshape(BLOCK, order) for u in range(across_ref.shape[1])], axis=0)
-    change_ref[...] = times_parts(parts_of(sides_ref[...]), parts_of(across), ROWS_BY_ROWS)
+    change_ref[...] = times_parts((high_ref[...], low_ref[...]), parts_of(across), ROWS_BY_ROWS)
 
 
 def changes(sides, across, steps, cost):
@@ -324,6 +329,7 @@
             pl.BlockSpec((across.shape[0], across.shape[1] // steps) + across.shape[2:], lambda t: (0, t, 0, 0)),
         ],
         out_specs=pl.BlockSpec((total, size), lambda t: (0, t)),
+        scratch_shapes=[pltpu.VMEM((total, order), jnp.bfloat16), pltpu.VMEM((total, order), jnp.bfloat16)],
         compiler_params=pltpu.CompilerParams(vmem_limit_bytes=60 * 2**20),
         cost_estimate=pl.CostEstimate(flops=cost, bytes_accessed=2**10, transcendentals=0),
         name="changes",
@@ -456,7 +462,7 @@
     other = over_cores(own)
     inverse, mine = factor(place, own, other, order)
     solved, sides = solve(place, own, other, mine, inverse, grid_rows, local_rows)
-    change = changes(sides, across, local_cols, 37 * 10**9)
+    change = changes(sides, across, local_cols, 59 * 10**9)
     out = finish(place, tiles, change, solved, diag_boost[0][:, None, :], grid_rows, grid_cols)
     return out.reshape(1, local_rows, 1, size, local_cols, 1, size)
 

time: 253 us -> 251 us (level)
  waiting for transfers between devices: 68.9 us -> 64.9 us
    ppermute x3, waiting for transfers between devices: 27.3 us -> 14.7 us  [over_chips(): lax.ppermute(value, 'col', [(c, (c + 2 * d) % grid_cols) for c in cols])]
    all_to_all x1, waiting for transfers between devices: 0.01 us -> 11.5 us  [body(): lax.all_to_all(joined, ('row', 'col'), split_axis=0, concat_axis=0, tiled...]
    all_gather x1, waiting for transfers between devices: 2.98 us -> 0.01 us  [body(): across = lax.all_gather(for_cols, 'row', axis=0)]
where the time goes in v10:
time: 251 us; the launch traced here: 249 us
  Pallas kernels  78.9 us (31%)
  waiting for transfers between devices  64.9 us (26%)
  starting transfers between devices  56.6 us (23%)
  local copies, waits for them, and re-layouts  18.2 us (7%)
  between operations  13.6 us (5%)
  matrix products  8.6 us (3%)
  other arithmetic  8.5 us (3%)
    pallas_call x1, Pallas kernels, factor(): pl.pallas_call(factor_kernel, out_shape=(jax.ShapeDtypeStruct((order, ord...  56.5 us
    all_to_all x1, waiting for transfers between devices, body(): lax.all_to_all(lines, ('row', 'col'), split_axis=0, concat_axis=0, tiled=...  29.6 us
    all_to_all x1, starting transfers between devices, body(): lax.all_to_all(lines, ('row', 'col'), split_axis=0, concat_axis=0, tiled=...  18.1 us
    ppermute x3, waiting for transfers between devices, over_chips(): lax.ppermute(value, 'col', [(c, (c + 2 * d) % grid_cols) for c in cols])  14.7 us
    all_to_all x1, waiting for transfers between devices, body(): lax.all_to_all(joined, ('row', 'col'), split_axis=0, concat_axis=0, tiled...  11.5 us
    all_to_all x1, starting transfers between devices, body(): lax.all_to_all(split, 'col', split_axis=0, concat_axis=0, tiled=True)  11.2 us
    ppermute x3, starting transfers between devices, over_chips(): lax.ppermute(value, 'col', [(c, (c + 2 * d) % grid_cols) for c in cols])  9.96 us
    all_to_all x1, starting transfers between devices, body(): lax.all_to_all(joined, ('row', 'col'), split_axis=0, concat_axis=0, tiled...  8.51 us
  transfers between devices with their start and end apart: 9, of which 7 were waited for; matrix products, arithmetic and copies ran while one was open for 10% of the time, Pallas kernels for 28%

profile of v10, /device:TPU:1, one launch (start us, length us, event | category | flops | bytes accessed | tf_op | source)
XLA Modules:
  0.0 249.4 jit_solution(17471432381473001445)
XLA Ops:
  6.5 0.7 reshape.180
  7.3 0.6 copy-done.10
  7.9 2.5 select_reduce_fusion
  10.3 5.0 %all-to-all-start = ((f32[4,24,24,128]{3,2,1,0:T(8,128)}), f32[4,24,24,128]{3,2,1,0:T(8,128)S(1)}, u32[]{:S(2)}, u32[]{:S(2)}) async-start(f32[4,24,24,128]{3,2,1,0:T(8,128)} %select_reduce_fusion), calls=%async_computation | async-start | bytes 2359296 | tf_op jit(solution)/shard_map/all_to_all | solution.py:414
  15.3 0.7 slice_bitcast_fusion
  16.0 0.1 iota_compare_fusion.2
  16.1 0.1 broadcast_select_fusion.1
  16.3 0.8 broadcast_in_dim.168
  17.1 0.0 copy-done.5
  17.1 1.2 copy.75
  18.3 0.2 copy.52
  18.5 0.8 squeeze.9
  19.3 0.0 copy-done.9
  19.3 0.1 broadcast_in_dim.158
  19.4 0.1 broadcast_in_dim.159
  19.5 0.1 eq.103
  19.6 0.1 copy.64
  19.7 0.1 broadcast_in_dim.155
  19.8 0.1 copy.50
  19.9 0.8 fusion.14
  20.7 0.8 select_reduce_fusion.1
  21.5 0.7 broadcast_select_fusion.2.index_ref
  22.1 1.9 select_add_fusion.base_ref
  24.1 1.9 all-to-all-done
  26.0 1.0 copy-done.4
  27.0 2.9 %panel.1 = (f32[1152,1,128]{2,1,0:T(1,128)}, f32[8,8,8,128]{3,2,1,0:T(8,128)}) custom-call(s32[4,12]{1,0:T(4,128)} %broadcast_select_fusion.2.index_ref, f32[64,8,128]{2,1,0:T(8,128)} %select_add_fusion.base_ref, f32[96,24,128]{2,1,0:T(8,128)} %bitcast.75), custom_call_target="tpu_custom_call" | custom-call | flops 1000000 | bytes 2097152 | tf_op jit(solution)/shard_map/panel/pallas_call | solution.py:146
  30.0 11.2 %all-to-all-start.1 = ((f32[8,8,8,128]{3,2,1,0:T(8,128)}), f32[8,8,8,128]{3,2,1,0:T(8,128)S(1)}, u32[]{:S(2)}, u32[]{:S(2)}) async-start(f32[8,8,8,128]{3,2,1,0:T(8,128)} %get-tuple-element.17), calls=%async_computation.1 | async-start | bytes 524288 | tf_op jit(solution)/shard_map/all_to_all | solution.py:435
  41.2 0.0 all-gather.3.cloned.1.call-start
  41.2 2.6 %reshape.185 = f32[4,12,2,12,256]{4,3,2,1,0:T(8,128)} reshape(f32[4,24,24,128]{3,2,1,0:T(8,128)} %copy-done.4) | data formatting | bytes 2359296 | tf_op jit(solution)/shard_map/reshape | solution.py:415
  43.8 3.9 %all-to-all-done.1 = f32[8,8,8,128]{3,2,1,0:T(8,128)S(1)} async-done(((f32[8,8,8,128]{3,2,1,0:T(8,128)}), f32[8,8,8,128]{3,2,1,0:T(8,128)S(1)}, u32[]{:S(2)}, u32[]{:S(2)}) %all-to-all-start.1) | async-done | bytes 262176 | tf_op jit(solution)/shard_map/all_to_all | solution.py:435
  47.7 0.9 copy.57
  48.6 0.0 all-gather.3.cloned.1.call-update
  48.6 18.1 %all-to-all-start.2 = ((f32[128,9,1,128]{3,2,1,0:T(1,128)}), f32[128,9,1,128]{3,2,1,0:T(1,128)S(1)}, u32[]{:S(2)}, u32[]{:S(2)}) async-start(f32[128,9,1,128]{3,2,1,0:T(1,128)} %bitcast.85), calls=%async_computation.2 | async-start | bytes 1179648 | tf_op jit(solution)/shard_map/all_to_all | solution.py:441
  66.7 0.1 copy.54
  66.9 0.1 iota_add_fusion.1
  66.9 0.1 iota_add_fusion
  67.0 0.0 copy-done.8
  67.0 2.9 %convolution_bitcast_fusion = f32[4,12,2,4,8,256,1]{5,4,2,1,3,0,6:T(8,128)S(1)} fusion(f32[4,12,2,12,256]{4,3,2,1,0:T(8,128)} %reshape.185, s32[4,8]{1,0:T(4,128)S(1)} %iota_add_fusion, s32[4,12]{1,0:T(4,128)S(1)} %copy-done.8), kind=kOutput, calls=%fused_computation.7 | convolution fusion | flops 113247744 | bytes 4325696 | tf_op jit(solution)/shard_map/naube,ntpb->nautpe/dot_general | solution.py:444
  69.9 5.7 %fusion.2 = f32[16,8,2,2,4,256]{5,0,2,1,4,3:T(8,128)S(1)} fusion(f32[4,12,2,4,8,256,1]{5,4,2,1,3,0,6:T(8,128)S(1)} %convolution_bitcast_fusion, pred[2,16,8,4]{1,0,2,3:T(4,128)(4,1)S(1)} %copy.54, s32[2,16]{1,0:T(2,128)S(1)} %iota_add_fusion.1, s32[4,12]{1,0:T(4,128)S(1)} %copy-done.8, f32[1,2,2,1,1,16,8,4,256]{8,7,6,5,4,3,2,1,0:T(4,128)S(1)} %copy-done.5), kind=kOutput, calls=%fused_computation.5 | convolution fusion | flops 303040000 | bytes 7341376 | tf_op jit(solution)/shard_map/niqa,nautpe->iuqpte/dot_general | solution.py:445
  75.6 1.4 copy.56
  77.0 1.8 reshape.188
  78.8 29.6 %all-to-all-done.2 = f32[128,9,1,128]{3,2,1,0:T(1,128)S(1)} async-done(((f32[128,9,1,128]{3,2,1,0:T(1,128)}), f32[128,9,1,128]{3,2,1,0:T(1,128)S(1)}, u32[]{:S(2)}, u32[]{:S(2)}) %all-to-all-start.2) | async-done | bytes 589856 | tf_op jit(solution)/shard_map/all_to_all | solution.py:441
  108.5 4.7 %collective-permute-start.2 = (f32[9,128,128]{2,1,0:T(8,128)S(1)}, f32[9,128,128]{2,1,0:T(8,128)S(1)}, u32[]{:S(2)}, u32[]{:S(2)}) collective-permute-start(f32[9,128,128]{2,1,0:T(8,128)S(1)} %bitcast.78), channel_id=1, source_target_pairs={{0,4},{1,5},{2,6},{3,7},{4,0},{5,1},{6,2},{7,3},{8,12},{9,13},{10,... | collective-permute-start | bytes 1769480 | tf_op jit(solution)/shard_map/ppermute | solution.py:454
  113.1 2.6 %collective-permute-start.1 = (f32[9,128,128]{2,1,0:T(8,128)S(1)}, f32[9,128,128]{2,1,0:T(8,128)}, u32[]{:S(2)}, u32[]{:S(2)}) collective-permute-start(f32[9,128,128]{2,1,0:T(8,128)S(1)} %bitcast.79), channel_id=1, source_target_pairs={{0,6},{1,7},{2,0},{3,1},{4,2},{5,3},{6,4},{7,5},{8,14},{9,15},{10,... | collective-permute-start | bytes 1769480 | tf_op jit(solution)/shard_map/ppermute | solution.py:454
  115.7 2.7 %collective-permute-start = (f32[9,128,128]{2,1,0:T(8,128)S(1)}, f32[9,128,128]{2,1,0:T(8,128)}, u32[]{:S(2)}, u32[]{:S(2)}) collective-permute-start(f32[9,128,128]{2,1,0:T(8,128)S(1)} %bitcast.80), channel_id=1, source_target_pairs={{0,2},{1,3},{2,4},{3,5},{4,6},{5,7},{6,0},{7,1},{8,10},{9,11},{10,... | collective-permute-start | bytes 1769480 | tf_op jit(solution)/shard_map/ppermute | solution.py:454
  118.4 8.5 %all-to-all-start.3 = ((f32[128,4,8,128]{3,2,1,0:T(8,128)}), f32[128,4,8,128]{3,2,1,0:T(8,128)S(1)}, u32[]{:S(2)}, u32[]{:S(2)}) async-start(f32[128,4,8,128]{3,2,1,0:T(8,128)} %reshape.188), calls=%async_computation.3 | async-start | bytes 4194304 | tf_op jit(solution)/shard_map/all_to_all | solution.py:450
  127.0 0.0 collective-permute-done.2
  127.0 13.6 %collective-permute-done.1 = f32[9,128,128]{2,1,0:T(8,128)} collective-permute-done((f32[9,128,128]{2,1,0:T(8,128)S(1)}, f32[9,128,128]{2,1,0:T(8,128)}, u32[]{:S(2)}, u32[]{:S(2)}) %collective-permute-start.1) | collective-permute-done | bytes 589856 | tf_op jit(solution)/shard_map/ppermute | solution.py:454
  140.6 1.1 collective-permute-done
  141.7 1.4 pad_maximum_fusion.own_ref
  143.1 3.9 %collective-permute-start.3 = (f32[4,9,128,128]{3,2,1,0:T(8,128)S(1)}, f32[4,9,128,128]{3,2,1,0:T(8,128)S(1)}, u32[]{:S(2)}, u32[]{:S(2)}) collective-permute-start(f32[4,9,128,128]{3,2,1,0:T(8,128)S(1)} %pad_maximum_fusion.own_ref), channel_id=1, source_target_pairs={{0,1},{1,0},{2,3},{3,2},{4,5},{5,4},{6,7},{7,6},{8,9},{9,8},{10,11... | collective-permute-start | bytes 7077896 | tf_op jit(solution)/shard_map/ppermute | solution.py:458
  147.0 0.0 copy-done.7
  147.0 0.6 broadcast_in_dim_squeeze.3.boost_ref
  147.7 0.1 pad_add_fusion.place_ref
  147.7 3.2 %collective-permute-done.3.other_ref = f32[4,9,128,128]{3,2,1,0:T(8,128)S(1)} collective-permute-done((f32[4,9,128,128]{3,2,1,0:T(8,128)S(1)}, f32[4,9,128,128]{3,2,1,0:T(8,128)S(1)}, u32[]{:S(2)}, u32[]{:S(2)}) %collective-permute-start.3) | collective-permute-done | bytes 2359328 | tf_op jit(solution)/shard_map/ppermute | solution.py:458
  150.9 0.0 copy-done.2
  150.9 56.5 %factor.1 = (f32[1024,1024]{1,0:T(8,128)S(1)}, f32[256,1024]{1,0:T(8,128)S(1)}) custom-call(s32[2]{0:T(128)S(1)} %pad_add_fusion.place_ref, s32[2,40]{1,0:T(2,128)S(1)} %copy-done.2, f32[4,9,128,128]{3,2,1,0:T(8,128)S(1)} %pad_maximum_fusion.own_ref, f32[4,9,128,128]{3,2,1,0:T(8,128)S(1)} %collective-permute-done.3.other_ref), custom_call_target="tpu_custom_call" | custom-call | flops 1000000 | bytes 1024 | tf_op jit(solution)/shard_map/factor/pallas_call | solution.py:232
  207.4 6.6 %solve.1 = (f32[512,1024]{1,0:T(8,128)S(1)}, f32[512,1024]{1,0:T(8,128)S(1)}) custom-call(s32[2]{0:T(128)S(1)} %pad_add_fusion.place_ref, f32[4,9,128,128]{3,2,1,0:T(8,128)S(1)} %pad_maximum_fusion.own_ref, f32[4,9,128,128]{3,2,1,0:T(8,128)S(1)} %collective-permute-done.3.other_ref, f32[256,1024]{1,0:T(8,128)S(1)} %get-tuple-element.22.mine_ref, ...), custom_call_target="tpu_custom_call" | custom-call | flops 1000000 | bytes 1024 | tf_op jit(solution)/shard_map/solve/pallas_call | solution.py:292
  214.1 1.3 copy-done
  215.4 1.4 copy-done.3
  216.8 7.7 %changes.1 = f32[512,1024]{1,0:T(8,128)} custom-call(f32[512,1024]{1,0:T(8,128)} %copy-done.3, f32[16,8,8,1024]{3,2,1,0:T(8,128)} %bitcast.91), custom_call_target="tpu_custom_call" | custom-call | flops 59000000512 | bytes 1024 | tf_op jit(solution)/shard_map/changes/pallas_call | solution.py:323
  224.5 11.5 %all-to-all-done.3 = f32[128,4,8,128]{3,2,1,0:T(8,128)S(1)} async-done(((f32[128,4,8,128]{3,2,1,0:T(8,128)}), f32[128,4,8,128]{3,2,1,0:T(8,128)S(1)}, u32[]{:S(2)}, u32[]{:S(2)}) %all-to-all-start.3) | async-done | bytes 2097184 | tf_op jit(solution)/shard_map/all_to_all | solution.py:450
  236.0 1.3 copy-done.6
  237.3 5.3 %finish.1 = f32[4,1024,128]{2,1,0:T(8,128)} custom-call(s32[2]{0:T(128)} %copy-done.1, f32[4096,128]{1,0:T(8,128)} %bitcast.76, f32[4,128,1024]{2,1,0:T(8,128)} %bitcast.82, f32[4,128,1024]{2,1,0:T(8,128)} %bitcast.74, f32[32,1,256]{2,1,0:T(1,128)} %broadcast_in_dim_squeeze.3.boost_ref), custom_call_target="tpu_custom_call" | custom-call | flops 1000000 | bytes 1024 | tf_op jit(solution)/shard_map/finish/pallas_call | solution.py:370
  (27 shorter events, 0.2 us)
Async XLA Ops:
  7.3 0.6 copy-start.10
  10.3 6.7 %copy-start.5 = (f32[1,2,2,1,1,16,8,4,256]{8,7,6,5,4,3,2,1,0:T(4,128)S(1)}, f32[1,2,2,1,1,16,8,4,256]{8,7,6,5,4,3,2,1,0:T(4,128)}, u32[]{:S(2)}) copy-start(f32[1,2,2,1,1,16,8,4,256]{8,7,6,5,4,3,2,1,0:T(4,128)} %param.7) | copy-start | bytes 6291460
  10.3 15.7 %all-to-all-start = ((f32[4,24,24,128]{3,2,1,0:T(8,128)}), f32[4,24,24,128]{3,2,1,0:T(8,128)S(1)}, u32[]{:S(2)}, u32[]{:S(2)}) async-start(f32[4,24,24,128]{3,2,1,0:T(8,128)} %select_reduce_fusion), calls=%async_computation | async-start | bytes 2359296 | tf_op jit(solution)/shard_map/all_to_all | solution.py:414
  17.1 2.2 copy-start.9
  26.0 1.0 copy-start.4
  30.0 17.7 %all-to-all-start.1 = ((f32[8,8,8,128]{3,2,1,0:T(8,128)}), f32[8,8,8,128]{3,2,1,0:T(8,128)S(1)}, u32[]{:S(2)}, u32[]{:S(2)}) async-start(f32[8,8,8,128]{3,2,1,0:T(8,128)} %get-tuple-element.17), calls=%async_computation.1 | async-start | bytes 524288 | tf_op jit(solution)/shard_map/all_to_all | solution.py:435
  41.2 25.8 %copy-start.8 = (s32[4,12]{1,0:T(4,128)S(1)}, s32[4,12]{1,0:T(4,128)}, u32[]{:S(2)}) copy-start(s32[4,12]{1,0:T(4,128)} %broadcast_select_fusion.2.index_ref) | copy-start | bytes 580
  41.2 175.6 %all-gather.3.cloned.1.call-start = ((), (), s32[]{:S(2)}) async-start(), calls=%async_computation.4 | async-start | bytes 4456448 | tf_op jit(solution)/shard_map/all_gather | solution.py:438
  48.6 59.8 %all-to-all-start.2 = ((f32[128,9,1,128]{3,2,1,0:T(1,128)}), f32[128,9,1,128]{3,2,1,0:T(1,128)S(1)}, u32[]{:S(2)}, u32[]{:S(2)}) async-start(f32[128,9,1,128]{3,2,1,0:T(1,128)} %bitcast.85), calls=%async_computation.2 | async-start | bytes 1179648 | tf_op jit(solution)/shard_map/all_to_all | solution.py:441
  108.5 18.5 %collective-permute-start.2 = (f32[9,128,128]{2,1,0:T(8,128)S(1)}, f32[9,128,128]{2,1,0:T(8,128)S(1)}, u32[]{:S(2)}, u32[]{:S(2)}) collective-permute-start(f32[9,128,128]{2,1,0:T(8,128)S(1)} %bitcast.78), channel_id=1, source_target_pairs={{0,4},{1,5},{2,6},{3,7},{4,0},{5,1},{6,2},{7,3},{8,12},{9,13},{10,... | collective-permute-start | bytes 1769480 | tf_op jit(solution)/shard_map/ppermute | solution.py:454
  113.1 27.4 %collective-permute-start.1 = (f32[9,128,128]{2,1,0:T(8,128)S(1)}, f32[9,128,128]{2,1,0:T(8,128)}, u32[]{:S(2)}, u32[]{:S(2)}) collective-permute-start(f32[9,128,128]{2,1,0:T(8,128)S(1)} %bitcast.79), channel_id=1, source_target_pairs={{0,6},{1,7},{2,0},{3,1},{4,2},{5,3},{6,4},{7,5},{8,14},{9,15},{10,... | collective-permute-start | bytes 1769480 | tf_op jit(solution)/shard_map/ppermute | solution.py:454
  115.7 26.0 %collective-permute-start = (f32[9,128,128]{2,1,0:T(8,128)S(1)}, f32[9,128,128]{2,1,0:T(8,128)}, u32[]{:S(2)}, u32[]{:S(2)}) collective-permute-start(f32[9,128,128]{2,1,0:T(8,128)S(1)} %bitcast.80), channel_id=1, source_target_pairs={{0,2},{1,3},{2,4},{3,5},{4,6},{5,7},{6,0},{7,1},{8,10},{9,11},{10,... | collective-permute-start | bytes 1769480 | tf_op jit(solution)/shard_map/ppermute | solution.py:454
  118.4 117.5 %all-to-all-start.3 = ((f32[128,4,8,128]{3,2,1,0:T(8,128)}), f32[128,4,8,128]{3,2,1,0:T(8,128)S(1)}, u32[]{:S(2)}, u32[]{:S(2)}) async-start(f32[128,4,8,128]{3,2,1,0:T(8,128)} %reshape.188), calls=%async_computation.3 | async-start | bytes 4194304 | tf_op jit(solution)/shard_map/all_to_all | solution.py:450
  141.7 5.3 %copy-start.7 = (f32[1,32,256]{2,1,0:T(8,128)S(1)}, f32[1,32,256]{2,1,0:T(8,128)}, u32[]{:S(2)}) copy-start(f32[1,32,256]{2,1,0:T(8,128)} %param.9) | copy-start | bytes 98308
  141.7 9.3 %copy-start.2 = (s32[2,40]{1,0:T(2,128)S(1)}, s32[2,40]{1,0:T(2,128)}, u32[]{:S(2)}) copy-start(s32[2,40]{1,0:T(2,128)} %constant.40.clone.pairs_ref) | copy-start | bytes 964
  143.1 7.8 %collective-permute-start.3 = (f32[4,9,128,128]{3,2,1,0:T(8,128)S(1)}, f32[4,9,128,128]{3,2,1,0:T(8,128)S(1)}, u32[]{:S(2)}, u32[]{:S(2)}) collective-permute-start(f32[4,9,128,128]{3,2,1,0:T(8,128)S(1)} %pad_maximum_fusion.own_ref), channel_id=1, source_target_pairs={{0,1},{1,0},{2,3},{3,2},{4,5},{5,4},{6,7},{7,6},{8,9},{9,8},{10,11... | collective-permute-start | bytes 7077896 | tf_op jit(solution)/shard_map/ppermute | solution.py:458
  147.7 59.7 %copy-start.1 = (s32[2]{0:T(128)}, s32[2]{0:T(128)S(1)}, u32[]{:S(2)}) copy-start(s32[2]{0:T(128)S(1)} %pad_add_fusion.place_ref) | copy-start | bytes 28
  214.1 1.3 copy-start
  215.4 1.4 copy-start.3
  236.0 1.3 copy-start.6
Sparse Core Ops, SparseCore 0:
  48.7 145.5 all-gather.2

commit v11 on v10

--- a/solution.py
+++ b/solution.py
@@ -379,7 +379,7 @@
             pl.BlockSpec(boost.shape, lambda s: (0, 0, 0)),
         ],
         out_specs=pl.BlockSpec((bands, count * per, BLOCK), lambda s: (0, s, 0)),
-        compiler_params=pltpu.CompilerParams(vmem_limit_bytes=60 * 2**20),
+        compiler_params=pltpu.CompilerParams(vmem_limit_bytes=57 * 2**20),
         cost_estimate=pl.CostEstimate(flops=10**6, bytes_accessed=2**10, transcendentals=0),
         name="finish",
     )(place, tiles, change.reshape(bands, BLOCK, order), solved.reshape(bands, BLOCK, order), boost)

time: 251 us -> 251 us (level)
  no operation moved by 1% of the time
where the time goes in v11:
time: 251 us; the launch traced here: 249 us
  Pallas kernels  78.9 us (31%)
  waiting for transfers between devices  64.9 us (26%)
  starting transfers between devices  56.7 us (23%)
  local copies, waits for them, and re-layouts  18.2 us (7%)
  between operations  13.6 us (5%)
  matrix products  8.59 us (3%)
  other arithmetic  8.5 us (3%)
    pallas_call x1, Pallas kernels, factor(): pl.pallas_call(factor_kernel, out_shape=(jax.ShapeDtypeStruct((order, ord...  56.5 us
    all_to_all x1, waiting for transfers between devices, body(): lax.all_to_all(lines, ('row', 'col'), split_axis=0, concat_axis=0, tiled=...  29.6 us
    all_to_all x1, starting transfers between devices, body(): lax.all_to_all(lines, ('row', 'col'), split_axis=0, concat_axis=0, tiled=...  18.1 us
    ppermute x3, waiting for transfers between devices, over_chips(): lax.ppermute(value, 'col', [(c, (c + 2 * d) % grid_cols) for c in cols])  14.7 us
    all_to_all x1, waiting for transfers between devices, body(): lax.all_to_all(joined, ('row', 'col'), split_axis=0, concat_axis=0, tiled...  11.5 us
    all_to_all x1, starting transfers between devices, body(): lax.all_to_all(split, 'col', split_axis=0, concat_axis=0, tiled=True)  11.2 us
    ppermute x3, starting transfers between devices, over_chips(): lax.ppermute(value, 'col', [(c, (c + 2 * d) % grid_cols) for c in cols])  9.96 us
    all_to_all x1, starting transfers between devices, body(): lax.all_to_all(joined, ('row', 'col'), split_axis=0, concat_axis=0, tiled...  8.51 us
  transfers between devices with their start and end apart: 9, of which 7 were waited for; matrix products, arithmetic and copies ran while one was open for 10% of the time, Pallas kernels for 28%

profile of v11, /device:TPU:1, one launch (start us, length us, event | category | flops | bytes accessed | tf_op | source)
XLA Modules:
  0.0 249.5 jit_solution(17471432381473001445)
XLA Ops:
  6.5 0.7 reshape.180
  7.3 0.6 copy-done.10
  7.9 2.5 select_reduce_fusion
  10.3 5.0 %all-to-all-start = ((f32[4,24,24,128]{3,2,1,0:T(8,128)}), f32[4,24,24,128]{3,2,1,0:T(8,128)S(1)}, u32[]{:S(2)}, u32[]{:S(2)}) async-start(f32[4,24,24,128]{3,2,1,0:T(8,128)} %select_reduce_fusion), calls=%async_computation | async-start | bytes 2359296 | tf_op jit(solution)/shard_map/all_to_all | solution.py:414
  15.3 0.7 slice_bitcast_fusion
  16.0 0.1 iota_compare_fusion.2
  16.1 0.1 broadcast_select_fusion.1
  16.3 0.8 broadcast_in_dim.168
  17.1 0.0 copy-done.5
  17.1 1.2 copy.75
  18.3 0.2 copy.52
  18.5 0.8 squeeze.9
  19.3 0.0 copy-done.9
  19.3 0.1 broadcast_in_dim.158
  19.4 0.1 broadcast_in_dim.159
  19.5 0.1 eq.103
  19.6 0.1 copy.64
  19.7 0.1 broadcast_in_dim.155
  19.8 0.1 copy.50
  19.9 0.8 fusion.14
  20.7 0.8 select_reduce_fusion.1
  21.5 0.7 broadcast_select_fusion.2.index_ref
  22.1 1.9 select_add_fusion.base_ref
  24.1 1.9 all-to-all-done
  26.0 1.0 copy-done.4
  27.0 2.9 %panel.1 = (f32[1152,1,128]{2,1,0:T(1,128)}, f32[8,8,8,128]{3,2,1,0:T(8,128)}) custom-call(s32[4,12]{1,0:T(4,128)} %broadcast_select_fusion.2.index_ref, f32[64,8,128]{2,1,0:T(8,128)} %select_add_fusion.base_ref, f32[96,24,128]{2,1,0:T(8,128)} %bitcast.75), custom_call_target="tpu_custom_call" | custom-call | flops 1000000 | bytes 2097152 | tf_op jit(solution)/shard_map/panel/pallas_call | solution.py:146
  29.9 11.2 %all-to-all-start.1 = ((f32[8,8,8,128]{3,2,1,0:T(8,128)}), f32[8,8,8,128]{3,2,1,0:T(8,128)S(1)}, u32[]{:S(2)}, u32[]{:S(2)}) async-start(f32[8,8,8,128]{3,2,1,0:T(8,128)} %get-tuple-element.17), calls=%async_computation.1 | async-start | bytes 524288 | tf_op jit(solution)/shard_map/all_to_all | solution.py:435
  41.2 0.0 all-gather.3.cloned.1.call-start
  41.2 2.6 %reshape.185 = f32[4,12,2,12,256]{4,3,2,1,0:T(8,128)} reshape(f32[4,24,24,128]{3,2,1,0:T(8,128)} %copy-done.4) | data formatting | bytes 2359296 | tf_op jit(solution)/shard_map/reshape | solution.py:415
  43.7 3.9 %all-to-all-done.1 = f32[8,8,8,128]{3,2,1,0:T(8,128)S(1)} async-done(((f32[8,8,8,128]{3,2,1,0:T(8,128)}), f32[8,8,8,128]{3,2,1,0:T(8,128)S(1)}, u32[]{:S(2)}, u32[]{:S(2)}) %all-to-all-start.1) | async-done | bytes 262176 | tf_op jit(solution)/shard_map/all_to_all | solution.py:435
  47.7 0.9 copy.57
  48.6 0.0 all-gather.3.cloned.1.call-update
  48.6 18.1 %all-to-all-start.2 = ((f32[128,9,1,128]{3,2,1,0:T(1,128)}), f32[128,9,1,128]{3,2,1,0:T(1,128)S(1)}, u32[]{:S(2)}, u32[]{:S(2)}) async-start(f32[128,9,1,128]{3,2,1,0:T(1,128)} %bitcast.85), calls=%async_computation.2 | async-start | bytes 1179648 | tf_op jit(solution)/shard_map/all_to_all | solution.py:441
  66.7 0.1 copy.54
  66.9 0.1 iota_add_fusion.1
  66.9 0.1 iota_add_fusion
  67.0 0.0 copy-done.8
  67.0 2.9 %convolution_bitcast_fusion = f32[4,12,2,4,8,256,1]{5,4,2,1,3,0,6:T(8,128)S(1)} fusion(f32[4,12,2,12,256]{4,3,2,1,0:T(8,128)} %reshape.185, s32[4,8]{1,0:T(4,128)S(1)} %iota_add_fusion, s32[4,12]{1,0:T(4,128)S(1)} %copy-done.8), kind=kOutput, calls=%fused_computation.7 | convolution fusion | flops 113247744 | bytes 4325696 | tf_op jit(solution)/shard_map/naube,ntpb->nautpe/dot_general | solution.py:444
  69.9 5.7 %fusion.2 = f32[16,8,2,2,4,256]{5,0,2,1,4,3:T(8,128)S(1)} fusion(f32[4,12,2,4,8,256,1]{5,4,2,1,3,0,6:T(8,128)S(1)} %convolution_bitcast_fusion, pred[2,16,8,4]{1,0,2,3:T(4,128)(4,1)S(1)} %copy.54, s32[2,16]{1,0:T(2,128)S(1)} %iota_add_fusion.1, s32[4,12]{1,0:T(4,128)S(1)} %copy-done.8, f32[1,2,2,1,1,16,8,4,256]{8,7,6,5,4,3,2,1,0:T(4,128)S(1)} %copy-done.5), kind=kOutput, calls=%fused_computation.5 | convolution fusion | flops 303040000 | bytes 7341376 | tf_op jit(solution)/shard_map/niqa,nautpe->iuqpte/dot_general | solution.py:445
  75.6 1.4 copy.56
  77.0 1.8 reshape.188
  78.8 29.6 %all-to-all-done.2 = f32[128,9,1,128]{3,2,1,0:T(1,128)S(1)} async-done(((f32[128,9,1,128]{3,2,1,0:T(1,128)}), f32[128,9,1,128]{3,2,1,0:T(1,128)S(1)}, u32[]{:S(2)}, u32[]{:S(2)}) %all-to-all-start.2) | async-done | bytes 589856 | tf_op jit(solution)/shard_map/all_to_all | solution.py:441
  108.5 4.7 %collective-permute-start.2 = (f32[9,128,128]{2,1,0:T(8,128)S(1)}, f32[9,128,128]{2,1,0:T(8,128)S(1)}, u32[]{:S(2)}, u32[]{:S(2)}) collective-permute-start(f32[9,128,128]{2,1,0:T(8,128)S(1)} %bitcast.78), channel_id=1, source_target_pairs={{0,4},{1,5},{2,6},{3,7},{4,0},{5,1},{6,2},{7,3},{8,12},{9,13},{10,... | collective-permute-start | bytes 1769480 | tf_op jit(solution)/shard_map/ppermute | solution.py:454
  113.1 2.5 %collective-permute-start.1 = (f32[9,128,128]{2,1,0:T(8,128)S(1)}, f32[9,128,128]{2,1,0:T(8,128)}, u32[]{:S(2)}, u32[]{:S(2)}) collective-permute-start(f32[9,128,128]{2,1,0:T(8,128)S(1)} %bitcast.79), channel_id=1, source_target_pairs={{0,6},{1,7},{2,0},{3,1},{4,2},{5,3},{6,4},{7,5},{8,14},{9,15},{10,... | collective-permute-start | bytes 1769480 | tf_op jit(solution)/shard_map/ppermute | solution.py:454
  115.7 2.7 %collective-permute-start = (f32[9,128,128]{2,1,0:T(8,128)S(1)}, f32[9,128,128]{2,1,0:T(8,128)}, u32[]{:S(2)}, u32[]{:S(2)}) collective-permute-start(f32[9,128,128]{2,1,0:T(8,128)S(1)} %bitcast.80), channel_id=1, source_target_pairs={{0,2},{1,3},{2,4},{3,5},{4,6},{5,7},{6,0},{7,1},{8,10},{9,11},{10,... | collective-permute-start | bytes 1769480 | tf_op jit(solution)/shard_map/ppermute | solution.py:454
  118.4 8.5 %all-to-all-start.3 = ((f32[128,4,8,128]{3,2,1,0:T(8,128)}), f32[128,4,8,128]{3,2,1,0:T(8,128)S(1)}, u32[]{:S(2)}, u32[]{:S(2)}) async-start(f32[128,4,8,128]{3,2,1,0:T(8,128)} %reshape.188), calls=%async_computation.3 | async-start | bytes 4194304 | tf_op jit(solution)/shard_map/all_to_all | solution.py:450
  127.0 0.0 collective-permute-done.2
  127.0 13.6 %collective-permute-done.1 = f32[9,128,128]{2,1,0:T(8,128)} collective-permute-done((f32[9,128,128]{2,1,0:T(8,128)S(1)}, f32[9,128,128]{2,1,0:T(8,128)}, u32[]{:S(2)}, u32[]{:S(2)}) %collective-permute-start.1) | collective-permute-done | bytes 589856 | tf_op jit(solution)/shard_map/ppermute | solution.py:454
  140.6 1.1 collective-permute-done
  141.7 1.4 pad_maximum_fusion.own_ref
  143.1 3.9 %collective-permute-start.3 = (f32[4,9,128,128]{3,2,1,0:T(8,128)S(1)}, f32[4,9,128,128]{3,2,1,0:T(8,128)S(1)}, u32[]{:S(2)}, u32[]{:S(2)}) collective-permute-start(f32[4,9,128,128]{3,2,1,0:T(8,128)S(1)} %pad_maximum_fusion.own_ref), channel_id=1, source_target_pairs={{0,1},{1,0},{2,3},{3,2},{4,5},{5,4},{6,7},{7,6},{8,9},{9,8},{10,11... | collective-permute-start | bytes 7077896 | tf_op jit(solution)/shard_map/ppermute | solution.py:458
  147.0 0.0 copy-done.7
  147.1 0.6 broadcast_in_dim_squeeze.3.boost_ref
  147.7 0.1 pad_add_fusion.place_ref
  147.8 3.2 %collective-permute-done.3.other_ref = f32[4,9,128,128]{3,2,1,0:T(8,128)S(1)} collective-permute-done((f32[4,9,128,128]{3,2,1,0:T(8,128)S(1)}, f32[4,9,128,128]{3,2,1,0:T(8,128)S(1)}, u32[]{:S(2)}, u32[]{:S(2)}) %collective-permute-start.3) | collective-permute-done | bytes 2359328 | tf_op jit(solution)/shard_map/ppermute | solution.py:458
  151.0 56.5 %factor.1 = (f32[1024,1024]{1,0:T(8,128)S(1)}, f32[256,1024]{1,0:T(8,128)S(1)}) custom-call(s32[2]{0:T(128)S(1)} %pad_add_fusion.place_ref, s32[2,40]{1,0:T(2,128)S(1)} %copy-done.2, f32[4,9,128,128]{3,2,1,0:T(8,128)S(1)} %pad_maximum_fusion.own_ref, f32[4,9,128,128]{3,2,1,0:T(8,128)S(1)} %collective-permute-done.3.other_ref), custom_call_target="tpu_custom_call" | custom-call | flops 1000000 | bytes 1024 | tf_op jit(solution)/shard_map/factor/pallas_call | solution.py:232
  207.4 0.0 copy-done.1
  207.5 6.6 %solve.1 = (f32[512,1024]{1,0:T(8,128)S(1)}, f32[512,1024]{1,0:T(8,128)S(1)}) custom-call(s32[2]{0:T(128)S(1)} %pad_add_fusion.place_ref, f32[4,9,128,128]{3,2,1,0:T(8,128)S(1)} %pad_maximum_fusion.own_ref, f32[4,9,128,128]{3,2,1,0:T(8,128)S(1)} %collective-permute-done.3.other_ref, f32[256,1024]{1,0:T(8,128)S(1)} %get-tuple-element.22.mine_ref, ...), custom_call_target="tpu_custom_call" | custom-call | flops 1000000 | bytes 1024 | tf_op jit(solution)/shard_map/solve/pallas_call | solution.py:292
  214.1 1.3 copy-done
  215.4 1.4 copy-done.3
  216.8 7.7 %changes.1 = f32[512,1024]{1,0:T(8,128)} custom-call(f32[512,1024]{1,0:T(8,128)} %copy-done.3, f32[16,8,8,1024]{3,2,1,0:T(8,128)} %bitcast.91), custom_call_target="tpu_custom_call" | custom-call | flops 59000000512 | bytes 1024 | tf_op jit(solution)/shard_map/changes/pallas_call | solution.py:323
  224.5 11.5 %all-to-all-done.3 = f32[128,4,8,128]{3,2,1,0:T(8,128)S(1)} async-done(((f32[128,4,8,128]{3,2,1,0:T(8,128)}), f32[128,4,8,128]{3,2,1,0:T(8,128)S(1)}, u32[]{:S(2)}, u32[]{:S(2)}) %all-to-all-start.3) | async-done | bytes 2097184 | tf_op jit(solution)/shard_map/all_to_all | solution.py:450
  236.0 1.3 copy-done.6
  237.4 5.3 %finish.1 = f32[4,1024,128]{2,1,0:T(8,128)} custom-call(s32[2]{0:T(128)} %copy-done.1, f32[4096,128]{1,0:T(8,128)} %bitcast.76, f32[4,128,1024]{2,1,0:T(8,128)} %bitcast.82, f32[4,128,1024]{2,1,0:T(8,128)} %bitcast.74, f32[32,1,256]{2,1,0:T(1,128)} %broadcast_in_dim_squeeze.3.boost_ref), custom_call_target="tpu_custom_call" | custom-call | flops 1000000 | bytes 1024 | tf_op jit(solution)/shard_map/finish/pallas_call | solution.py:370
  (27 shorter events, 0.2 us)
Async XLA Ops:
  7.3 0.6 copy-start.10
  10.3 6.7 %copy-start.5 = (f32[1,2,2,1,1,16,8,4,256]{8,7,6,5,4,3,2,1,0:T(4,128)S(1)}, f32[1,2,2,1,1,16,8,4,256]{8,7,6,5,4,3,2,1,0:T(4,128)}, u32[]{:S(2)}) copy-start(f32[1,2,2,1,1,16,8,4,256]{8,7,6,5,4,3,2,1,0:T(4,128)} %param.7) | copy-start | bytes 6291460
  10.3 15.7 %all-to-all-start = ((f32[4,24,24,128]{3,2,1,0:T(8,128)}), f32[4,24,24,128]{3,2,1,0:T(8,128)S(1)}, u32[]{:S(2)}, u32[]{:S(2)}) async-start(f32[4,24,24,128]{3,2,1,0:T(8,128)} %select_reduce_fusion), calls=%async_computation | async-start | bytes 2359296 | tf_op jit(solution)/shard_map/all_to_all | solution.py:414
  17.1 2.2 copy-start.9
  26.0 1.0 copy-start.4
  29.9 17.7 %all-to-all-start.1 = ((f32[8,8,8,128]{3,2,1,0:T(8,128)}), f32[8,8,8,128]{3,2,1,0:T(8,128)S(1)}, u32[]{:S(2)}, u32[]{:S(2)}) async-start(f32[8,8,8,128]{3,2,1,0:T(8,128)} %get-tuple-element.17), calls=%async_computation.1 | async-start | bytes 524288 | tf_op jit(solution)/shard_map/all_to_all | solution.py:435
  41.2 25.8 %copy-start.8 = (s32[4,12]{1,0:T(4,128)S(1)}, s32[4,12]{1,0:T(4,128)}, u32[]{:S(2)}) copy-start(s32[4,12]{1,0:T(4,128)} %broadcast_select_fusion.2.index_ref) | copy-start | bytes 580
  41.2 175.6 %all-gather.3.cloned.1.call-start = ((), (), s32[]{:S(2)}) async-start(), calls=%async_computation.4 | async-start | bytes 4456448 | tf_op jit(solution)/shard_map/all_gather | solution.py:438
  48.6 59.8 %all-to-all-start.2 = ((f32[128,9,1,128]{3,2,1,0:T(1,128)}), f32[128,9,1,128]{3,2,1,0:T(1,128)S(1)}, u32[]{:S(2)}, u32[]{:S(2)}) async-start(f32[128,9,1,128]{3,2,1,0:T(1,128)} %bitcast.85), calls=%async_computation.2 | async-start | bytes 1179648 | tf_op jit(solution)/shard_map/all_to_all | solution.py:441
  108.5 18.5 %collective-permute-start.2 = (f32[9,128,128]{2,1,0:T(8,128)S(1)}, f32[9,128,128]{2,1,0:T(8,128)S(1)}, u32[]{:S(2)}, u32[]{:S(2)}) collective-permute-start(f32[9,128,128]{2,1,0:T(8,128)S(1)} %bitcast.78), channel_id=1, source_target_pairs={{0,4},{1,5},{2,6},{3,7},{4,0},{5,1},{6,2},{7,3},{8,12},{9,13},{10,... | collective-permute-start | bytes 1769480 | tf_op jit(solution)/shard_map/ppermute | solution.py:454
  113.1 27.5 %collective-permute-start.1 = (f32[9,128,128]{2,1,0:T(8,128)S(1)}, f32[9,128,128]{2,1,0:T(8,128)}, u32[]{:S(2)}, u32[]{:S(2)}) collective-permute-start(f32[9,128,128]{2,1,0:T(8,128)S(1)} %bitcast.79), channel_id=1, source_target_pairs={{0,6},{1,7},{2,0},{3,1},{4,2},{5,3},{6,4},{7,5},{8,14},{9,15},{10,... | collective-permute-start | bytes 1769480 | tf_op jit(solution)/shard_map/ppermute | solution.py:454
  115.7 26.0 %collective-permute-start = (f32[9,128,128]{2,1,0:T(8,128)S(1)}, f32[9,128,128]{2,1,0:T(8,128)}, u32[]{:S(2)}, u32[]{:S(2)}) collective-permute-start(f32[9,128,128]{2,1,0:T(8,128)S(1)} %bitcast.80), channel_id=1, source_target_pairs={{0,2},{1,3},{2,4},{3,5},{4,6},{5,7},{6,0},{7,1},{8,10},{9,11},{10,... | collective-permute-start | bytes 1769480 | tf_op jit(solution)/shard_map/ppermute | solution.py:454
  118.4 117.6 %all-to-all-start.3 = ((f32[128,4,8,128]{3,2,1,0:T(8,128)}), f32[128,4,8,128]{3,2,1,0:T(8,128)S(1)}, u32[]{:S(2)}, u32[]{:S(2)}) async-start(f32[128,4,8,128]{3,2,1,0:T(8,128)} %reshape.188), calls=%async_computation.3 | async-start | bytes 4194304 | tf_op jit(solution)/shard_map/all_to_all | solution.py:450
  141.7 5.4 %copy-start.7 = (f32[1,32,256]{2,1,0:T(8,128)S(1)}, f32[1,32,256]{2,1,0:T(8,128)}, u32[]{:S(2)}) copy-start(f32[1,32,256]{2,1,0:T(8,128)} %param.9) | copy-start | bytes 98308
  141.7 9.3 %copy-start.2 = (s32[2,40]{1,0:T(2,128)S(1)}, s32[2,40]{1,0:T(2,128)}, u32[]{:S(2)}) copy-start(s32[2,40]{1,0:T(2,128)} %constant.40.clone.pairs_ref) | copy-start | bytes 964
  143.1 7.8 %collective-permute-start.3 = (f32[4,9,128,128]{3,2,1,0:T(8,128)S(1)}, f32[4,9,128,128]{3,2,1,0:T(8,128)S(1)}, u32[]{:S(2)}, u32[]{:S(2)}) collective-permute-start(f32[4,9,128,128]{3,2,1,0:T(8,128)S(1)} %pad_maximum_fusion.own_ref), channel_id=1, source_target_pairs={{0,1},{1,0},{2,3},{3,2},{4,5},{5,4},{6,7},{7,6},{8,9},{9,8},{10,11... | collective-permute-start | bytes 7077896 | tf_op jit(solution)/shard_map/ppermute | solution.py:458
  147.8 59.7 %copy-start.1 = (s32[2]{0:T(128)}, s32[2]{0:T(128)S(1)}, u32[]{:S(2)}) copy-start(s32[2]{0:T(128)S(1)} %pad_add_fusion.place_ref) | copy-start | bytes 28
  214.1 1.3 copy-start
  215.4 1.4 copy-start.3
  236.0 1.3 copy-start.6
Sparse Core Ops, SparseCore 0:
  48.7 145.4 all-gather.2
